TPU v7x, 32 devices: a whole 2x2x4 slice. The times are simulated.
32 devices in a mesh: section: 2 (over core), expert: 8 (over z, x), shard: 2 (over y).
Axes of the slice: x: 2, y: 2, z: 4, core: 2. Of those that a mesh axis runs over, the one named last changes fastest.
Arguments:
- edge_inputs: bfloat16 [2, 2, 2048, 1536], P('section', None, ('expert', 'shard')), may hold values from -6 to 6
- seq_lengths: int32 [2, 8, 3], P(None, 'expert'), may hold values from 1 to 128, as said below
- routes: int32 [2, 2, 2048, 8], P('section', None, ('expert', 'shard')), may hold values from 0 to 15, all different within a row; in each aligned block of 128 rows (0 to 127, 128 to 255, ..., all dimensions but the last counted through in order) at most 80 rows name the same one
- w_qkv: bfloat16 [2, 1536, 2560], P('section', 'shard'), may hold values from -0.15625 to 0.15625
- w_out: bfloat16 [2, 1536, 1536], P('section', 'shard'), may hold values from -0.625 to 0.625
- w_router: bfloat16 [2, 1536, 16], P('section', 'shard'), may hold values from -0.078125 to 0.078125
- gain_attn: bfloat16 [2, 1536], P('section', 'shard'), may hold values from 0.25 to 1.75
- gain_moe: bfloat16 [2, 1536], P('section', 'shard'), may hold values from 0.25 to 1.75
- w_gate_up: bfloat16 [2, 16, 1536, 1024], P('section', 'expert'), may hold values from -0.15625 to 0.15625
- w_down: bfloat16 [2, 16, 512, 1536], P('section', 'expert'), may hold values from -0.75 to 0.75
Outputs:
- edge_outputs: float32 [2, 2, 2048, 1536], P('section', None, ('expert', 'shard'))
- grad_w_qkv: float32 [2, 1536, 2560], P('section', 'shard')
- grad_w_out: float32 [2, 1536, 1536], P('section', 'shard')
- grad_w_router: float32 [2, 1536, 16], P('section', 'shard')
- grad_gain_attn: float32 [2, 1536], P('section', 'shard')
- grad_gain_moe: float32 [2, 1536], P('section', 'shard')
- grad_w_gate_up: float32 [2, 16, 1536, 1024], P('section', 'expert')
- grad_w_down: float32 [2, 16, 512, 1536], P('section', 'expert')
Inputs may be any that keep to these rules, and one draw needn't show every extreme that they name: `seq_lengths`: each group's 3 sequences come in order: the first has 1 to 127 tokens, the second exactly 128, the third the rest of the group's 256 tokens. `routes`: every row names 8 different experts; in the rows of one device for one micro-batch and layer (aligned blocks of 128 rows) no expert is named more than 80 times.
All inputs are finite; a program needn't handle non-finite values.
Results may differ from a plain program's by a relative error of at most 0.025.
Values may be sent and summed in bfloat16 or wider, within the bound.
A program may use at most 256 MiB of HBM per device.

v0:
```python
import functools

import jax
import jax.numpy as jnp
from jax import lax
from jax.experimental import pallas as pl
from jax.experimental.pallas import tpu as pltpu
from jax.sharding import PartitionSpec as P

QUERY_HEADS = 24
KEY_VALUE_HEADS = 8
HEAD_SIZE = 64
FF = 512
TOP = 8
EXP_DEV = 2
EPS = 1e-05
MASKED_SCORE = -1e30
QUERY_WIDTH = QUERY_HEADS * HEAD_SIZE
KV_WIDTH = KEY_VALUE_HEADS * HEAD_SIZE
F32 = jnp.float32
BF16 = jnp.bfloat16
MESH = pl.DeviceIdType.MESH
LINE = 4
SIDE = 2
LANES = 128
HALVES = 2
TILE = 256
VMEM_BYTES = 60 * 2**20
COST = pl.CostEstimate(flops=10**11, bytes_accessed=2**24, transcendentals=0)


def chunk_order(z, t):
    near = z + 1 - 2 * lax.rem(z, 2)
    third = jnp.where(z < 2, 2, 1)
    last = jnp.where(z < 2, 3, 0)
    return jnp.where(t == 0, z, jnp.where(t == 1, near, jnp.where(t == 2, third, last)))


def sum_order(z, i):
    first = jnp.where((z == 0) | (z == 2), 1, 2)
    second = jnp.where(z == 0, 2, jnp.where(z == 1, 3, jnp.where(z == 2, 0, 1)))
    third = jnp.where(z == 0, 3, jnp.where(z == 1, 0, jnp.where(z == 2, 3, 0)))
    return jnp.where(i == 0, first, jnp.where(i == 1, second, third))


class Plane:
    def __init__(self, rows, refs):
        (self.gathered, self.parts, self.from_side, self.from_low, self.from_high, self.sums,
         self.line_send, self.gather_recv, self.side_send, self.side_recv,
         self.sum_send, self.low_recv, self.high_recv) = refs
        self.sub = rows // HALVES
        self.both = SIDE * self.sub
        self.sec, self.owner, self.shard = (lax.axis_index(n) for n in ("section", "expert", "shard"))
        self.z, self.x = lax.div(self.owner, SIDE), lax.rem(self.owner, SIDE)
        self.inner = ((self.z > 0) & (self.z < LINE - 1)).astype(jnp.int32)

    def device(self, z, x):
        return (self.sec, z * SIDE + x, self.shard)

    def other_core(self):
        return (1 - self.sec, self.owner, self.shard)

    def other_shard(self):
        return (self.sec, self.owner, 1 - self.shard)

    def chunk(self, c, h):
        return pl.ds(pl.multiple_of((c * HALVES + h) * self.both, self.both), self.both)

    def block(self, c, h, x):
        return pl.ds(pl.multiple_of((c * HALVES + h) * self.both + x * self.sub, self.sub), self.sub)

    def barrier(self, *others):
        z, x = self.z, self.x
        sem = pltpu.get_barrier_semaphore()

        def greet(device):
            pl.semaphore_signal(sem, inc=1, device_id=device, device_id_type=MESH)

        for other in others:
            greet(other)
        greet(self.device(z, 1 - x))
        pl.when(z > 0)(lambda: greet(self.device(z - 1, x)))
        pl.when(z < LINE - 1)(lambda: greet(self.device(z + 1, x)))
        pl.semaphore_wait(sem, 2 + len(others) + self.inner)

    def place(self, block_ref):
        for h in range(HALVES):
            self.gathered[self.block(self.z, h, self.x)] = block_ref[pl.ds(h * self.sub, self.sub)]

    def gather_copy(self, way, c, h, x, device):
        ref = self.gathered.at[self.block(c, h, x)]
        q = c * HALVES + h
        return pltpu.make_async_remote_copy(
            src_ref=ref, dst_ref=ref, send_sem=self.line_send.at[way, q],
            recv_sem=self.gather_recv.at[q, x], device_id=device, device_id_type=MESH)

    def forward_up(self, c, h):
        return self.gather_copy(0, c, h, self.x, self.device(self.z + 1, self.x))

    def forward_down(self, c, h):
        return self.gather_copy(1, c, h, self.x, self.device(self.z - 1, self.x))

    def forward_side(self, c, h):
        return self.gather_copy(2, c, h, self.x, self.device(self.z, 1 - self.x))

    def start_gather(self):
        z = self.z
        for h in range(HALVES):
            pl.when(z < LINE - 1)(lambda h=h: self.forward_up(z, h).start())
            pl.when(z > 0)(lambda h=h: self.forward_down(z, h).start())
            self.forward_side(z, h).start()

    def relay(self, t, h):
        z = self.z

        @pl.when((t > 0) & (z - t >= 0))
        def _():
            c = z - t
            self.forward_side(c, h).wait_recv()
            pl.when(z < LINE - 1)(lambda: self.forward_up(c, h).start())
            self.forward_side(c, h).start()

        @pl.when((t > 0) & (z + t <= LINE - 1))
        def _():
            c = z + t
            self.forward_side(c, h).wait_recv()
            pl.when(z > 0)(lambda: self.forward_down(c, h).start())
            self.forward_side(c, h).start()

    def wait_side_block(self, c, h):
        self.gather_copy(2, c, h, 1 - self.x, self.device(self.z, 1 - self.x)).wait_recv()

    def side_copy(self, c, h):
        q = c * HALVES + h
        return pltpu.make_async_remote_copy(
            src_ref=self.parts.at[self.block(c, h, 1 - self.x)], dst_ref=self.from_side.at[q],
            send_sem=self.side_send.at[q], recv_sem=self.side_recv.at[q],
            device_id=self.device(self.z, 1 - self.x), device_id_type=MESH)

    def up_copy(self, c, h):
        q = c * HALVES + h
        return pltpu.make_async_remote_copy(
            src_ref=self.sums.at[q], dst_ref=self.from_low.at[q], send_sem=self.sum_send.at[q],
            recv_sem=self.low_recv.at[q], device_id=self.device(self.z + 1, self.x), device_id_type=MESH)

    def down_copy(self, c, h):
        q = c * HALVES + h
        return pltpu.make_async_remote_copy(
            src_ref=self.sums.at[q], dst_ref=self.from_high.at[q], send_sem=self.sum_send.at[q],
            recv_sem=self.high_recv.at[q], device_id=self.device(self.z - 1, self.x), device_id_type=MESH)

    def own_part(self, c, h):
        return (self.parts[self.block(c, h, self.x)].astype(F32)
                + self.from_side[c * HALVES + h].astype(F32))

    def pass_sum(self, t, h):
        i = t - 3 - self.inner
        pl.when((i >= 0) & (i < LINE - 1))(lambda: self.pass_chunk(sum_order(self.z, i), h))

    def pass_chunk(self, c, h):
        z = self.z
        q = c * HALVES + h
        self.side_copy(c, h).wait_recv()

        @pl.when(c > z)
        def _():
            @pl.when(z > 0)
            def _():
                self.up_copy(c, h).wait_recv()
                self.sums[q] = (self.own_part(c, h) + self.from_low[q].astype(F32)).astype(BF16)

            @pl.when(z == 0)
            def _():
                self.sums[q] = self.own_part(c, h).astype(BF16)

            self.up_copy(c, h).start()

        @pl.when(c < z)
        def _():
            @pl.when(z < LINE - 1)
            def _():
                self.down_copy(c, h).wait_recv()
                self.sums[q] = (self.own_part(c, h) + self.from_high[q].astype(F32)).astype(BF16)

            @pl.when(z == LINE - 1)
            def _():
                self.sums[q] = self.own_part(c, h).astype(BF16)

            self.down_copy(c, h).start()

    def finish_sum(self, h, out_ref):
        z = self.z
        q = z * HALVES + h
        rows = pl.ds(pl.multiple_of(h * self.sub, self.sub), self.sub)
        self.side_copy(z, h).wait_recv()
        out_ref[rows] = self.own_part(z, h)

        @pl.when(z > 0)
        def _():
            self.up_copy(z, h).wait_recv()
            out_ref[rows] += self.from_low[q].astype(F32)

        @pl.when(z < LINE - 1)
        def _():
            self.down_copy(z, h).wait_recv()
            out_ref[rows] += self.from_high[q].astype(F32)

    def finish_piece(self, h, out_ref):
        z = self.z
        q = z * HALVES + h
        self.side_copy(z, h).wait_recv()

        @pl.when(z == 0)
        def _():
            self.down_copy(z, h).wait_recv()
            out_ref[h] = (self.own_part(z, h) + self.from_high[q].astype(F32)).astype(BF16)

        @pl.when(z == LINE - 1)
        def _():
            self.up_copy(z, h).wait_recv()
            out_ref[h] = (self.own_part(z, h) + self.from_low[q].astype(F32)).astype(BF16)

        @pl.when((z > 0) & (z < LINE - 1))
        def _():
            self.up_copy(z, h).wait_recv()
            self.down_copy(z, h).wait_recv()
            total = self.own_part(z, h) + self.from_low[q].astype(F32)
            out_ref[h] = (total + self.from_high[q].astype(F32)).astype(BF16)

    def drain(self):
        z = self.z

        def one(q, carry):
            c, h = lax.div(q, HALVES), lax.rem(q, HALVES)
            pl.when((z < LINE - 1) & (c <= z))(lambda: self.forward_up(c, h).wait_send())
            pl.when((z > 0) & (c >= z))(lambda: self.forward_down(c, h).wait_send())
            self.forward_side(c, h).wait_send()
            self.side_copy(c, h).wait_send()
            pl.when(c > z)(lambda: self.up_copy(c, h).wait_send())
            pl.when(c < z)(lambda: self.down_copy(c, h).wait_send())
            return carry

        lax.fori_loop(0, LINE * HALVES, one, 0)


def plane_scratch(rows, width, wide):
    count = LINE * HALVES
    block = pltpu.VMEM((count, rows // HALVES, width), BF16)
    return [
        pltpu.VMEM((LINE * SIDE * rows, wide), BF16),
        pltpu.VMEM((LINE * SIDE * rows, width), BF16),
        block, block, block, block,
        pltpu.SemaphoreType.DMA((3, count)),
        pltpu.SemaphoreType.DMA((count, SIDE)),
        pltpu.SemaphoreType.DMA((count,)),
        pltpu.SemaphoreType.DMA((count,)),
        pltpu.SemaphoreType.DMA((count,)),
        pltpu.SemaphoreType.DMA((count,)),
        pltpu.SemaphoreType.DMA((count,)),
    ]


def lane_tile(at, size=TILE):
    return pl.ds(pl.multiple_of(at * size, size), size)


def nn(a, b):
    return jnp.dot(a, b, preferred_element_type=F32)


def nt(a, b):
    return lax.dot_general(a, b, (((1,), (1,)), ((), ())), preferred_element_type=F32)


def tn(a, b):
    return lax.dot_general(a, b, (((0,), (0,)), ((), ())), preferred_element_type=F32)


def pick_lane(block, wanted):
    lane = lax.broadcasted_iota(jnp.int32, block.shape, 1)
    hot = lane == wanted[0]
    for other in wanted[1:]:
        hot = hot | (lane == other)
    return jnp.sum(jnp.where(hot, block, 0.0), axis=1, keepdims=True)


def own_gates(block, owner, experts):
    block = block.astype(F32)
    return [
        pick_lane(block, (owner * EXP_DEV + j, experts + owner * EXP_DEV + j)) for j in range(EXP_DEV)
    ]


def load_layer(layer, sec, own, other, dst, sem):
    copies = [pltpu.make_async_copy(own, dst, sem), pltpu.make_async_copy(other, dst, sem)]
    pl.when(sec == layer)(lambda: copies[0].start())
    pl.when(sec != layer)(lambda: copies[1].start())
    return copies[0]


def load_experts(layer, sec, gu, gu_other, down, down_other, gu_v, down_v, sems):
    loads = [load_layer(layer, sec, gu, gu_other, gu_v, sems.at[0])]
    for j in range(EXP_DEV):
        loads.append(load_layer(
            layer, sec, down.at[j], down_other.at[j], down_v.at[pl.ds(j * FF, FF)], sems.at[1 + j]))
    return loads


def moe_forward_kernel(layer, experts, rows, width, block_ref, gu_hbm, gu_other, down_hbm, down_other,
                       moe_ref, rows_hbm, kept_hbm, scaled_hbm,
                       gu_v, down_v, kept, scaled, load_sem, store_sem, *plane_refs):
    plane = Plane(rows, plane_refs)
    gathered, parts = plane.gathered, plane.parts
    loads = load_experts(layer, plane.sec, gu_hbm, gu_other, down_hbm, down_other, gu_v, down_v, load_sem)
    plane.place(block_ref)
    plane.barrier()
    plane.start_gather()
    for load in loads:
        load.wait()

    def stores(c, h):
        q, at = c * HALVES + h, plane.chunk(c, h)
        return [
            pltpu.make_async_copy(gathered.at[at], rows_hbm.at[at], store_sem.at[0, q]),
            pltpu.make_async_copy(kept.at[at], kept_hbm.at[at], store_sem.at[1, q]),
            pltpu.make_async_copy(scaled.at[at], scaled_hbm.at[at], store_sem.at[2, q]),
        ]

    def step(k, carry):
        t, h = lax.div(k, HALVES), lax.rem(k, HALVES)
        plane.relay(t, h)
        plane.pass_sum(t, h)
        pl.when(t > 0)(lambda: work(chunk_order(plane.z, t - 1), h))
        return carry

    def work(c, h):
        at = plane.chunk(c, h)
        plane.wait_side_block(c, h)
        gates = own_gates(gathered[at, pl.ds(width, LANES)], plane.owner, experts)
        for j in range(EXP_DEV):
            for f in range(FF // TILE):
                data = gathered[at, pl.ds(0, width)]
                low, high = j * 2 * FF + f * TILE, j * 2 * FF + FF + f * TILE
                g = nn(data, gu_v[j, :, pl.ds(f * TILE, TILE)])
                u = nn(data, gu_v[j, :, pl.ds(FF + f * TILE, TILE)])
                z = g * jax.nn.sigmoid(g) * u * gates[j]
                scaled[at, pl.ds(j * FF + f * TILE, TILE)] = z.astype(BF16)
                kept[at, pl.ds(low, TILE)] = g.astype(BF16)
                kept[at, pl.ds(high, TILE)] = u.astype(BF16)
        for n in range(width // TILE):
            parts[at, pl.ds(n * TILE, TILE)] = nn(
                scaled[at, :], down_v[:, pl.ds(n * TILE, TILE)]).astype(BF16)
        plane.side_copy(c, h).start()
        for store in stores(c, h):
            store.start()

    lax.fori_loop(0, (LINE + 1) * HALVES, step, 0)

    def tail(k, carry):
        plane.pass_sum(lax.div(k, HALVES), lax.rem(k, HALVES))
        return carry

    lax.fori_loop((LINE + 1) * HALVES, (LINE + 3) * HALVES, tail, 0)

    def finish(h, carry):
        plane.finish_sum(h, moe_ref)
        return carry

    lax.fori_loop(0, HALVES, finish, 0)
    plane.drain()

    def stored(q, carry):
        for store in stores(lax.div(q, HALVES), lax.rem(q, HALVES)):
            store.wait()
        return carry

    lax.fori_loop(0, LINE * HALVES, stored, 0)


def moe_forward(layer, block, weights, experts, collective_id):
    rows, wide = block.shape
    width = wide - LANES
    total = LINE * SIDE * rows
    any_spec = pl.BlockSpec(memory_space=pl.ANY)
    vmem = pl.BlockSpec(memory_space=pltpu.VMEM)
    return pl.pallas_call(
        functools.partial(moe_forward_kernel, layer, experts, rows, width),
        name="moe_forward",
        out_shape=(
            jax.ShapeDtypeStruct((rows, width), F32),
            jax.ShapeDtypeStruct((total, wide), BF16),
            jax.ShapeDtypeStruct((total, EXP_DEV * 2 * FF), BF16),
            jax.ShapeDtypeStruct((total, EXP_DEV * FF), BF16),
        ),
        in_specs=[vmem] + [any_spec] * 4,
        out_specs=(vmem, any_spec, any_spec, any_spec),
        scratch_shapes=[
            pltpu.VMEM((EXP_DEV, width, 2 * FF), BF16),
            pltpu.VMEM((EXP_DEV * FF, width), BF16),
            pltpu.VMEM((total, EXP_DEV * 2 * FF), BF16),
            pltpu.VMEM((total, EXP_DEV * FF), BF16),
            pltpu.SemaphoreType.DMA((1 + EXP_DEV,)),
            pltpu.SemaphoreType.DMA((3, LINE * HALVES)),
        ] + plane_scratch(rows, width, wide),
        cost_estimate=COST,
        compiler_params=pltpu.CompilerParams(
            collective_id=collective_id, has_side_effects=True, vmem_limit_bytes=VMEM_BYTES),
    )(block, *weights)


def moe_backward_kernel(layer, experts, rows, width, beside, block_ref, router_ref, gu_hbm, gu_other, down_hbm,
                        down_other, rows_hbm, kept_hbm, scaled_hbm, *refs):
    (later, refs) = (refs[:4], refs[4:]) if beside else ((), refs)
    (db_ref, keep_gu_hbm, keep_down_hbm, send_gu_hbm, send_down_hbm, grad_router_ref), refs = refs[:6], refs[6:]
    (later_out, refs) = (refs[:3], refs[3:]) if beside else ((), refs)
    (gu_v, down_v, fwd_rows, kept, scaled, dgu, send_gu, grad_gu, send_down, grad_down,
     load_sem, store_sem), refs = refs[:12], refs[12:]
    (later_v, refs) = (refs[:8], refs[8:]) if beside else ((), refs)
    plane_refs = refs
    plane = Plane(rows, plane_refs)
    gathered, parts = plane.gathered, plane.parts
    loads = load_experts(layer, plane.sec, gu_hbm, gu_other, down_hbm, down_other, gu_v, down_v, load_sem)
    loads.append(pltpu.make_async_copy(rows_hbm, fwd_rows, load_sem.at[3]))
    loads.append(pltpu.make_async_copy(kept_hbm, kept, load_sem.at[4]))
    loads.append(pltpu.make_async_copy(scaled_hbm, scaled, load_sem.at[5]))
    for load in loads[3:]:
        load.start()
    plane.place(block_ref)
    plane.barrier(*([plane.other_core(), plane.other_shard()] if beside else []))
    plane.start_gather()
    if beside:
        other_layer = LaterExperts(plane, *later, *later_out, *later_v)
        other_layer.start_loads()
    for load in loads:
        load.wait()
    if beside:
        other_layer.send()
    total = plane.both
    up_at = EXP_DEV * 2 * FF

    def step(k, carry):
        t, h = lax.div(k, HALVES), lax.rem(k, HALVES)
        plane.relay(t, h)
        plane.pass_sum(t, h)
        pl.when(t > 0)(lambda: work(chunk_order(plane.z, t - 1), h))
        return carry

    def work(c, h):
        at = plane.chunk(c, h)
        plane.wait_side_block(c, h)
        gates = own_gates(fwd_rows[at, pl.ds(width, LANES)], plane.owner, experts)
        outer = jnp.sum(gathered[at, pl.ds(width, LANES)].astype(F32), axis=1, keepdims=True)
        dcs = []
        for j in range(EXP_DEV):
            dgate = jnp.zeros((total, 1), F32)
            for f in range(FF // TILE):
                low, high = pl.ds(j * 2 * FF + f * TILE, TILE), pl.ds(j * 2 * FF + FF + f * TILE, TILE)
                dz = nt(gathered[at, pl.ds(0, width)], down_v[pl.ds(j * FF + f * TILE, TILE), :])
                g = kept[at, low].astype(F32)
                u = kept[at, high].astype(F32)
                sig = jax.nn.sigmoid(g)
                silu = g * sig
                dgate = dgate + jnp.sum(dz * silu * u, axis=1, keepdims=True)
                dz = dz * gates[j]
                dgu[at, low] = (dz * u * sig * (1.0 + g * (1.0 - sig))).astype(BF16)
                dgu[at, high] = (dz * silu).astype(BF16)
            dcs.append(gates[j] * (dgate - outer))
        lane = lax.broadcasted_iota(jnp.int32, (total, LANES), 1)
        extra = jnp.zeros((total, LANES), F32)
        for j in range(EXP_DEV):
            top = dcs[j].astype(BF16).astype(F32)
            column = plane.owner * EXP_DEV + j
            extra = extra + jnp.where(lane == column, top, 0.0)
            extra = extra + jnp.where(lane == LANES // 2 + column, dcs[j] - top, 0.0)
        dgu[at, pl.ds(up_at, LANES)] = extra.astype(BF16)
        for n in range(width // TILE):
            cols = pl.ds(n * TILE, TILE)
            acc = nt(dgu[at, pl.ds(0, 2 * FF)], gu_v[0, cols, :])
            for j in range(1, EXP_DEV):
                acc = acc + nt(dgu[at, pl.ds(j * 2 * FF, 2 * FF)], gu_v[j, cols, :])
            for j in range(EXP_DEV):
                acc = acc + dcs[j] * router_ref[pl.ds(j, 1), cols]
            parts[at, cols] = acc.astype(BF16)
        plane.side_copy(c, h).start()

    lax.fori_loop(0, (LINE + 1) * HALVES, step, 0)

    core = plane.sec
    gu_steps, down_steps = width // TILE, FF // TILE

    def stores_gu(n):
        at = lane_tile(n)
        return [pltpu.make_async_copy(send_gu.at[at], send_gu_hbm.at[at], store_sem.at[0, n]),
                pltpu.make_async_copy(grad_gu.at[at], keep_gu_hbm.at[at], store_sem.at[1, n])]

    def stores_down(n):
        at = lane_tile(n)
        return [pltpu.make_async_copy(send_down.at[at], send_down_hbm.at[at], store_sem.at[2, n]),
                pltpu.make_async_copy(grad_down.at[at], keep_down_hbm.at[at], store_sem.at[3, n])]

    def expert_cols(j, size):
        return pl.ds(pl.multiple_of(j * size, size), size)

    def grad_gu_rows(n):
        rows_t = fwd_rows[:, lane_tile(n)]
        send_gu[lane_tile(n), :] = tn(rows_t, dgu[:, expert_cols(1 - core, 2 * FF)]).astype(BF16)
        grad_gu[lane_tile(n), :] = tn(rows_t, dgu[:, expert_cols(core, 2 * FF)]).astype(BF16)
        grad_router_ref[lane_tile(n), :] = tn(rows_t, dgu[:, pl.ds(up_at, LANES)])
        for store in stores_gu(n):
            store.start()

    def grad_down_rows(n):
        def cols(j):
            return pl.ds(pl.multiple_of(j * FF + n * TILE, TILE), TILE)

        data = gathered[:, pl.ds(0, width)]
        send_down[lane_tile(n), :] = tn(scaled[:, cols(1 - core)], data).astype(BF16)
        grad_down[lane_tile(n), :] = tn(scaled[:, cols(core)], data).astype(BF16)
        for store in stores_down(n):
            store.start()

    slots = 2 * HALVES

    def tail(k, carry):
        pl.loop(lax.div(k * gu_steps, slots), lax.div((k + 1) * gu_steps, slots))(grad_gu_rows)
        plane.pass_sum(LINE + 1 + lax.div(k, HALVES), lax.rem(k, HALVES))
        return carry

    lax.fori_loop(0, slots, tail, 0)
    pl.loop(0, down_steps)(grad_down_rows)

    def finish(h, carry):
        plane.finish_sum(h, db_ref)
        return carry

    lax.fori_loop(0, HALVES, finish, 0)
    if beside:
        other_layer.finish()
    plane.drain()
    for n in range(gu_steps):
        for store in stores_gu(n):
            store.wait()
    for n in range(down_steps):
        for store in stores_down(n):
            store.wait()


class LaterExperts:
    def __init__(self, plane, keep_gu, keep_down, send_gu, send_down, sum_gu_hbm, sum_down_hbm, land_gu,
                 gu_a, gu_b, down_a, down_b, load_sem, core_sem, send_sem, recv_sem):
        self.parts = []
        for keep, sent, out, land, a, b, count in (
            (keep_gu, send_gu, sum_gu_hbm, land_gu, gu_a, gu_b, 4),
            (keep_down, send_down, sum_down_hbm, None, down_a, down_b, 2),
        ):
            size = a.shape[0] // count
            for n in range(count):
                at, k = pl.ds(n * size, size), len(self.parts)
                shard_copy = land_copy = None
                if land is not None:
                    shard_copy = pltpu.make_async_remote_copy(
                        src_ref=a.at[at], dst_ref=land.at[at], send_sem=send_sem.at[k], recv_sem=recv_sem.at[k],
                        device_id=plane.other_shard(), device_id_type=MESH)
                    land_copy = pltpu.make_async_copy(land.at[at], b.at[at], load_sem.at[1, k])
                self.parts.append((
                    a.at[at], b.at[at],
                    pltpu.make_async_copy(keep.at[at], a.at[at], load_sem.at[0, k]),
                    pltpu.make_async_remote_copy(
                        src_ref=sent.at[at], dst_ref=b.at[at], send_sem=core_sem.at[0, k],
                        recv_sem=core_sem.at[1, k], device_id=plane.other_core(), device_id_type=MESH),
                    shard_copy, land_copy,
                    pltpu.make_async_copy(a.at[at], out.at[at], load_sem.at[2, k]),
                ))

    def start_loads(self):
        for _, _, load, core_copy, *_ in self.parts:
            load.start()
            core_copy.start()

    def send(self):
        for a, b, load, core_copy, shard_copy, _, store in self.parts:
            load.wait()
            core_copy.wait()
            a[...] = (a[...].astype(F32) + b[...].astype(F32)).astype(BF16)
            if shard_copy is not None:
                shard_copy.start()
            else:
                store.start()

    def finish(self):
        for _, _, _, _, shard_copy, land_copy, _ in self.parts:
            if shard_copy is not None:
                shard_copy.wait()
                land_copy.start()
        for a, b, _, _, shard_copy, land_copy, store in self.parts:
            if shard_copy is not None:
                land_copy.wait()
                a[...] = (a[...].astype(F32) + b[...].astype(F32)).astype(BF16)
                store.start()
        for *_, store in self.parts:
            store.wait()


def moe_backward(layer, block, router, weights, kept, later, experts, collective_id):
    rows, wide = block.shape
    width = wide - LANES
    total = LINE * SIDE * rows
    any_spec = pl.BlockSpec(memory_space=pl.ANY)
    vmem = pl.BlockSpec(memory_space=pltpu.VMEM)
    expert_gu, expert_down = pltpu.VMEM((width, 2 * FF), BF16), pltpu.VMEM((FF, width), BF16)
    gu_shape = jax.ShapeDtypeStruct((width, 2 * FF), BF16)
    down_shape = jax.ShapeDtypeStruct((FF, width), BF16)
    later_out, later_scratch = (), []
    if later:
        later_out = (gu_shape, down_shape, gu_shape)
        later_scratch = [
            expert_gu, expert_gu, expert_down, expert_down,
            pltpu.SemaphoreType.DMA((3, 6)), pltpu.SemaphoreType.DMA((2, 6)),
            pltpu.SemaphoreType.DMA((4,)), pltpu.SemaphoreType.DMA((4,)),
        ]
    return pl.pallas_call(
        functools.partial(moe_backward_kernel, layer, experts, rows, width, bool(later)),
        name="moe_backward",
        out_shape=(
            jax.ShapeDtypeStruct((rows, width), F32),
            gu_shape, down_shape, gu_shape, down_shape,
            jax.ShapeDtypeStruct((width, LANES), F32),
        ) + later_out,
        in_specs=[vmem, vmem] + [any_spec] * (7 + len(later)),
        out_specs=(vmem,) + (any_spec,) * 4 + (vmem,) + (any_spec,) * len(later_out),
        scratch_shapes=[
            pltpu.VMEM((EXP_DEV, width, 2 * FF), BF16),
            pltpu.VMEM((EXP_DEV * FF, width), BF16),
            pltpu.VMEM((total, wide), BF16),
            pltpu.VMEM((total, EXP_DEV * 2 * FF), BF16),
            pltpu.VMEM((total, EXP_DEV * FF), BF16),
            pltpu.VMEM((total, EXP_DEV * 2 * FF + LANES), BF16),
            expert_gu, expert_gu, expert_down, expert_down,
            pltpu.SemaphoreType.DMA((6,)),
            pltpu.SemaphoreType.DMA((4, width // TILE)),
        ] + later_scratch + plane_scratch(rows, width, wide),
        cost_estimate=COST,
        compiler_params=pltpu.CompilerParams(
            collective_id=collective_id, has_side_effects=True, vmem_limit_bytes=VMEM_BYTES),
    )(block, router, *weights, *kept, *later)


def split_terms(values):
    high = values.astype(BF16)
    return high, (values - high.astype(F32)).astype(BF16)


def with_lanes(block, columns):
    extra = jnp.concatenate(columns, axis=1)
    extra = jnp.pad(extra, ((0, 0), (0, LANES - extra.shape[1])))
    return jnp.concatenate([block, extra], axis=1)


def far_order(z, i):
    low = jnp.where(i == 0, 3, jnp.where(i == 1, jnp.where(z == 0, 2, 0), jnp.where(z == 0, 1, 2)))
    high = jnp.where(i == 0, 0, jnp.where(i == 1, jnp.where(z == 3, 1, 3), jnp.where(z == 3, 2, 1)))
    return jnp.where(z < 2, low, high)


def reduce_kernel(sub, cols, g1, g0, t1, t0, gu_hbm, down_hbm, sent_gu_hbm, sent_down_hbm, gu1_hbm, down1_hbm, edge,
                  sum_hbm, own_gu_hbm, own_down_hbm, got_gu_hbm, got_down_hbm, own_down1_hbm, got_gu1_hbm,
                  got_down1_hbm, got_edge,
                  core_got, small_own, small_got, result, own_gu, core_gu, other_gu, own_down, core_down, other_down,
                  own_down1, other_down1,
                  load_sem, expert_load_sem, expert_core_sem, edge_sem, core_sem, small_sem, move_sem, expert_sem, core_expert_sem, store_sem,
                  *plane_refs):
    plane = Plane(HALVES * sub, plane_refs)
    gathered, parts = plane.gathered, plane.parts
    core, shard, z, x = plane.sec, plane.shard, plane.z, plane.x
    wide = cols + LANES
    grads, smalls = (g1, g0), (t1, t0)
    diagonal = (1 - core, plane.owner, 1 - shard)
    places = [(c, side) for c in range(LINE) for side in range(SIDE)]

    def remote(src, dst, send_sem, recv_sem, device):
        return pltpu.make_async_remote_copy(
            src_ref=src, dst_ref=dst, send_sem=send_sem, recv_sem=recv_sem,
            device_id=device, device_id_type=MESH)

    loads = []
    for h in range(2):
        for n, (c, side) in enumerate(places):
            loads.append(pltpu.make_async_copy(
                grads[h].at[n, core], parts.at[plane.block(c, h, side), pl.ds(0, cols)], load_sem.at[h, n]))
        loads.append(pltpu.make_async_copy(
            smalls[h].at[shard, :, core], small_own.at[h], load_sem.at[h, len(places)]))
    pieces, expert_loads = [], []
    for layer, hbm, sent, own, there, other, own_hbm, got_hbm, count in (
        (1, down1_hbm, None, own_down1, None, other_down1, own_down1_hbm, got_down1_hbm, 2),
        (0, gu_hbm, sent_gu_hbm, own_gu, core_gu, other_gu, own_gu_hbm, got_gu_hbm, 4),
        (0, down_hbm, sent_down_hbm, own_down, core_down, other_down, own_down_hbm, got_down_hbm, 2),
    ):
        size = own.shape[0] // count
        for n in range(count):
            at, k = pl.ds(n * size, size), len(pieces)
            pieces.append((layer, own, there, other, own_hbm, got_hbm, at))
            expert_loads.append((
                pltpu.make_async_copy(hbm.at[at], own.at[at], expert_load_sem.at[k]),
                None if sent is None else remote(
                    sent.at[at], there.at[at], expert_core_sem.at[0, k], expert_core_sem.at[1, k],
                    plane.other_core()),
            ))
    for load in [load for load, _ in expert_loads[:2]] + loads + [load for load, _ in expert_loads[2:]]:
        load.start()
    plane.barrier(plane.other_core(), plane.other_shard(), diagonal)
    cores = [
        remote(grads[h].at[:, 1 - core], core_got.at[h], core_sem.at[0, h], core_sem.at[1, h], plane.other_core())
        for h in range(2)
    ]
    small = []
    for h in range(2):
        for n, (there, half, device) in enumerate((
            (shard, 1 - core, plane.other_core()),
            (1 - shard, core, plane.other_shard()),
            (1 - shard, 1 - core, diagonal),
        )):
            small.append(remote(
                smalls[h].at[there, :, half], small_got.at[h, n], small_sem.at[0, h, n], small_sem.at[1, h, n],
                device))
    for copy in cores[:1] + small + cores[1:]:
        copy.start()
    for _, copy in expert_loads:
        if copy is not None:
            copy.start()
    edges = remote(edge, got_edge, edge_sem.at[0], edge_sem.at[1], plane.other_core())
    edges.start()
    gu1_copy = remote(gu1_hbm, got_gu1_hbm, edge_sem.at[2], edge_sem.at[3], plane.other_core())
    pl.when(core == 0)(lambda: gu1_copy.start())
    exchange = []

    def send_piece():
        n = len(exchange)
        layer, own, there, other, own_hbm, got_hbm, at = pieces[n]
        for load in expert_loads[n]:
            if load is not None:
                load.wait()
        if there is not None:
            own[at] = (own[at].astype(F32) + there[at].astype(F32)).astype(BF16)
        exchange.append(
            remote(own.at[at], other.at[at], expert_sem.at[0, n], expert_sem.at[1, n], plane.other_shard()))
        exchange[-1].start()

    def prepare(h):
        cores[h].wait_recv()
        for copy in small[3 * h : 3 * h + 3]:
            copy.wait_recv()

        def one(k, carry):
            c = jnp.where(k < 2 * (LINE - 1), far_order(z, lax.div(k, 2)), z)
            side = jnp.where(lax.rem(k, 2) == 0, 1 - x, x)
            n = c * SIDE + side
            at = plane.block(c, h, side)
            parts[at, pl.ds(0, cols)] = (
                parts[at, pl.ds(0, cols)].astype(F32) + core_got[h, n].astype(F32)).astype(BF16)
            total = small_own[h, n].astype(F32)
            for other in range(3):
                total = total + small_got[h, other, n].astype(F32)
            parts[at, pl.ds(cols, LANES)] = total.astype(BF16)
            pl.when(side != x)(lambda: plane.side_copy(c, h).start())
            return carry

        lax.fori_loop(0, LINE * SIDE, one, 0)

    send_piece()
    send_piece()
    for load in loads:
        load.wait()
    prepare(0)
    send_piece()

    def pass_piece(i, h):
        plane.pass_chunk(far_order(z, i), h)

    def move(h):
        return remote(
            result.at[h], gathered.at[plane.block(z, core, x)], move_sem.at[0], move_sem.at[1], plane.other_core())

    def send_block(h):
        pl.when(z < LINE - 1)(lambda: plane.forward_up(z, h).start())
        pl.when(z > 0)(lambda: plane.forward_down(z, h).start())
        plane.forward_side(z, h).start()

    def finish(h):
        plane.finish_piece(h, result)
        own_layer = core == 1 - h
        pl.when(jnp.logical_not(own_layer))(lambda: move(h).start())

        @pl.when(own_layer)
        def _():
            gathered[plane.block(z, core, x)] = result[h]
            send_block(core)
            arrived = remote(
                result.at[h], gathered.at[plane.block(z, 1 - core, x)], move_sem.at[0], move_sem.at[1],
                plane.other_core())
            arrived.wait_recv()
            send_block(1 - core)

    def out_copy(c, h, side):
        at = pl.multiple_of(((c * SIDE + side) * HALVES + h) * sub, sub)
        return pltpu.make_async_copy(
            gathered.at[plane.block(c, h, side)], sum_hbm.at[pl.ds(at, sub)],
            store_sem.at[(c * SIDE + side) * HALVES + h])

    def gather(t):
        for turn in range(HALVES):
            h = core if turn == 0 else 1 - core
            plane.relay(t, h)
            c = chunk_order(z, t - 1)
            plane.wait_side_block(c, h)
            out_copy(c, h, x).start()
            out_copy(c, h, 1 - x).start()

    count = LINE * SIDE * HALVES

    def to_core(n):
        layer, own, there, other, own_hbm, got_hbm, at = pieces[n]
        return remote(
            own.at[at], got_hbm.at[at], core_expert_sem.at[0, n], core_expert_sem.at[1, n], plane.other_core())

    def keep(n):
        layer, own, there, other, own_hbm, got_hbm, at = pieces[n]
        return pltpu.make_async_copy(own.at[at], own_hbm.at[at], store_sem.at[count + n])

    def expert_piece(n):
        layer, own, there, other, own_hbm, got_hbm, at = pieces[n]
        exchange[n].wait()
        own[at] = (own[at].astype(F32) + other[at].astype(F32)).astype(BF16)
        pl.when(core != layer)(lambda: to_core(n).start())
        keep(n).start()

    pass_piece(0, 0)
    prepare(1)
    send_piece()
    pass_piece(1, 0)
    send_piece()
    pass_piece(2, 0)
    finish(0)
    while len(exchange) < len(pieces):
        send_piece()
    for i in range(LINE - 1):
        pass_piece(i, 1)
        pl.when(core == 1)(lambda i=i: gather(i + 1))
        expert_piece(i)
    finish(1)
    pl.when(core == 1)(lambda: gather(LINE))

    @pl.when(core == 0)
    def _():
        def one(t, carry):
            gather(t)
            return carry

        lax.fori_loop(1, LINE + 1, one, 0)

    for n in range(LINE - 1, len(pieces)):
        expert_piece(n)
    plane.drain()
    for copy in cores + small:
        copy.wait_send()
    move(0).wait_send()

    def stored(k, carry):
        out_copy(lax.div(k, SIDE * HALVES), lax.rem(k, HALVES), lax.rem(lax.div(k, HALVES), SIDE)).wait()
        return carry

    lax.fori_loop(0, count, stored, 0)
    for n in range(len(pieces)):
        keep(n).wait()
        pl.when(core != pieces[n][0])(lambda n=n: to_core(n).wait_send())
        pl.when(core == pieces[n][0])(lambda n=n: to_core(n).wait_recv())
    edges.wait()
    pl.when(core == 0)(lambda: gu1_copy.wait_send())
    pl.when(core == 1)(lambda: gu1_copy.wait_recv())


def reduce_gradients(g1, g0, t1, t0, experts0, gu1, down1, edge, collective_id):
    places, halves, sub, cols = g1.shape
    grad_gu, grad_down = experts0[:2]
    any_spec = pl.BlockSpec(memory_space=pl.ANY)
    wide = cols + LANES
    gu, down = jax.ShapeDtypeStruct(grad_gu.shape, BF16), jax.ShapeDtypeStruct(grad_down.shape, BF16)
    gu_v, down_v = pltpu.VMEM(grad_gu.shape, BF16), pltpu.VMEM(grad_down.shape, BF16)
    return pl.pallas_call(
        functools.partial(reduce_kernel, sub, cols),
        name="reduce_gradients",
        out_shape=(
            jax.ShapeDtypeStruct((places * halves * sub, wide), BF16), gu, down, gu, down, down, gu, down,
            jax.ShapeDtypeStruct(edge.shape, edge.dtype),
        ),
        in_specs=[any_spec] * 11,
        out_specs=(any_spec,) * 9,
        scratch_shapes=[
            pltpu.VMEM((2, places, sub, cols), BF16),
            pltpu.VMEM((2, places, sub, LANES), BF16),
            pltpu.VMEM((2, 3, places, sub, LANES), BF16),
            pltpu.VMEM((2, sub, wide), BF16),
            gu_v, gu_v, gu_v, down_v, down_v, down_v, down_v, down_v,
            pltpu.SemaphoreType.DMA((2, places + 1)),
            pltpu.SemaphoreType.DMA((8,)),
            pltpu.SemaphoreType.DMA((2, 8)),
            pltpu.SemaphoreType.DMA((4,)),
            pltpu.SemaphoreType.DMA((2, 2)),
            pltpu.SemaphoreType.DMA((2, 2, 3)),
            pltpu.SemaphoreType.DMA((2,)),
            pltpu.SemaphoreType.DMA((2, 8)),
            pltpu.SemaphoreType.DMA((2, 8)),
            pltpu.SemaphoreType.DMA((places * halves + 8,)),
        ] + plane_scratch(halves * sub, wide, wide),
        compiler_params=pltpu.CompilerParams(
            collective_id=collective_id, has_side_effects=True, vmem_limit_bytes=VMEM_BYTES),
    )(g1, g0, t1, t0, *experts0, gu1, down1, edge)


def finish_kernel(qkv_cols, attn, gu_own, gu_got, gu_one, gu_moved, down_own, down_got, down_one, down_moved,
                  qkv_hbm, out_hbm, gu_hbm, down_hbm, attn_v, gu_v, down_v, qkv_f, out_f, gu_f, down_f,
                  load_sem, store_sem):
    core = lax.axis_index("section")
    steps = []

    def chunks(rows, count):
        return [pl.ds(n * (rows // count), rows // count) for n in range(count)]

    def choose(zero, one, dst, sem):
        copies = [pltpu.make_async_copy(zero, dst, sem), pltpu.make_async_copy(one, dst, sem)]
        pl.when(core == 0)(lambda: copies[0].start())
        pl.when(core == 1)(lambda: copies[1].start())
        return copies[0]

    def add(load, convert, stores):
        steps.append((load, convert, stores))

    def store(src, dst, n):
        return pltpu.make_async_copy(src, dst, store_sem.at[n])

    stored = 0
    for j, (zero, one) in enumerate(((gu_own, gu_moved), (gu_got, gu_one))):
        for at in chunks(gu_f.shape[1], 6):
            def convert(j=j, at=at):
                gu_f[j, at, :] = gu_v[j, at, :].astype(F32)

            load = choose(zero.at[at], one.at[at], gu_v.at[j, at], load_sem.at[len(steps)])
            add(load, convert, [store(gu_f.at[j, at], gu_hbm.at[j, at], stored)])
            stored += 1
    for j, (zero, one) in enumerate(((down_own, down_moved), (down_got, down_one))):
        for at in chunks(down_f.shape[1], 2):
            def convert(j=j, at=at):
                down_f[j, at, :] = down_v[j, at, :].astype(F32)

            load = choose(zero.at[at], one.at[at], down_v.at[j, at], load_sem.at[len(steps)])
            add(load, convert, [store(down_f.at[j, at], down_hbm.at[j, at], stored)])
            stored += 1
    for at in chunks(attn_v.shape[0], 8):
        def convert(at=at):
            qkv_f[at, :] = attn_v[at, pl.ds(0, qkv_cols)].astype(F32)
            out_f[at, :] = attn_v[at, pl.ds(qkv_cols, out_f.shape[1])].astype(F32)

        load = pltpu.make_async_copy(attn.at[at, pl.ds(0, attn_v.shape[1])], attn_v.at[at], load_sem.at[len(steps)])
        load.start()
        add(load, convert, [
            store(qkv_f.at[at], qkv_hbm.at[at], stored), store(out_f.at[at], out_hbm.at[at], stored + 1)])
        stored += 2
    for load, convert, stores in steps:
        load.wait()
        convert()
        for copy in stores:
            copy.start()
    for load, convert, stores in steps:
        for copy in stores:
            copy.wait()


def finish_outputs(attn, gus, downs, qkv_cols, out_cols):
    rows = attn.shape[0]
    gu, down = (EXP_DEV,) + gus[0].shape, (EXP_DEV,) + downs[0].shape
    any_spec = pl.BlockSpec(memory_space=pl.ANY)
    return pl.pallas_call(
        functools.partial(finish_kernel, qkv_cols),
        name="finish_outputs",
        out_shape=(
            jax.ShapeDtypeStruct((rows, qkv_cols), F32),
            jax.ShapeDtypeStruct((rows, out_cols), F32),
            jax.ShapeDtypeStruct(gu, F32),
            jax.ShapeDtypeStruct(down, F32),
        ),
        in_specs=[any_spec] * 9,
        out_specs=(any_spec,) * 4,
        scratch_shapes=[
            pltpu.VMEM((rows, qkv_cols + out_cols), BF16),
            pltpu.VMEM(gu, BF16),
            pltpu.VMEM(down, BF16),
            pltpu.VMEM((rows, qkv_cols), F32),
            pltpu.VMEM((rows, out_cols), F32),
            pltpu.VMEM(gu, F32),
            pltpu.VMEM(down, F32),
            pltpu.SemaphoreType.DMA((24,)),
            pltpu.SemaphoreType.DMA((32,)),
        ],
        compiler_params=pltpu.CompilerParams(vmem_limit_bytes=VMEM_BYTES),
    )(attn, *gus, *downs)


PAIRS = 2
GROUP = QUERY_HEADS // KEY_VALUE_HEADS
SCALE = HEAD_SIZE ** (-0.5)


class Pair:
    def __init__(self):
        self.sec, self.owner, self.me = (lax.axis_index(n) for n in ("section", "expert", "shard"))
        self.peer = 1 - self.me

    def barrier(self, with_core=False):
        sem = pltpu.get_barrier_semaphore()
        pl.semaphore_signal(
            sem, inc=1, device_id=(self.sec, self.owner, self.peer), device_id_type=MESH)
        if with_core:
            pl.semaphore_signal(
                sem, inc=1, device_id=(1 - self.sec, self.owner, self.me), device_id_type=MESH)
        pl.semaphore_wait(sem, 1 + with_core)

    def send(self, src, dst, send_sem, recv_sem):
        return pltpu.make_async_remote_copy(
            src_ref=src, dst_ref=dst, send_sem=send_sem, recv_sem=recv_sem,
            device_id=(self.sec, self.owner, self.peer), device_id_type=MESH)


def head_columns(shard):
    kv_pair = KEY_VALUE_HEADS // 2 // PAIRS * HEAD_SIZE
    q_pair = kv_pair * GROUP
    wide = q_pair + 2 * kv_pair
    spans = []
    for i in range(PAIRS):
        at = shard * PAIRS + i
        spans.append((at * q_pair, i * wide, q_pair))
        spans.append((QUERY_WIDTH + at * kv_pair, i * wide + q_pair, kv_pair))
        spans.append((QUERY_WIDTH + KV_WIDTH + at * kv_pair, i * wide + q_pair + kv_pair, kv_pair))
    return spans


def head_at(i, n, g):
    kv_pair = KEY_VALUE_HEADS // 2 // PAIRS * HEAD_SIZE
    q_pair = kv_pair * GROUP
    base = i * (q_pair + 2 * kv_pair)
    return (
        pl.ds(base + (n * GROUP + g) * HEAD_SIZE, HEAD_SIZE),
        pl.ds(base + q_pair + n * HEAD_SIZE, HEAD_SIZE),
        pl.ds(base + q_pair + kv_pair + n * HEAD_SIZE, HEAD_SIZE),
    )


KV_IN_PAIR = KEY_VALUE_HEADS // 2 // PAIRS


def load_attention(layer, sec, wq, wq_other, wo, wo_other, wq_v, wo_v, sems):
    loads = []
    for j in range(2):
        for at, local, size in head_columns(j):
            loads.append(load_layer(
                layer, sec, wq.at[:, pl.ds(at, size)], wq_other.at[:, pl.ds(at, size)],
                wq_v.at[j, :, pl.ds(local, size)], sems.at[len(loads)]))
    loads.append(load_layer(layer, sec, wo, wo_other, wo_v, sems.at[len(loads)]))
    return loads


LOADS = 2 * PAIRS * 3 + 1


def attention_forward_kernel(layer, rows, width, h_ref, allowed_ref, gains_ref, router_ref, mask_ref, wq, wq_other,
                             wo, wo_other, block_ref, h1_ref, a_ref, qkv_ref, p_ref, o_ref,
                             wq_v, wo_v, a_parts, a_half, part_send, got_part, out_send, got_out,
                             load_sem, send_sem, recv_sem, *turn):
    pair = Pair()
    me, peer = pair.me, pair.peer
    half = width // 2
    loads = load_attention(layer, pair.sec, wq, wq_other, wo, wo_other, wq_v, wo_v, load_sem)
    pair.barrier(bool(turn))

    def span(who):
        return pl.ds(pl.multiple_of(who * rows, rows), rows)

    h = h_ref[...].astype(F32)
    r1 = lax.rsqrt(jnp.mean(h * h, axis=1, keepdims=True) + EPS)
    a = (h * r1 * gains_ref[pl.ds(0, 1), :]).astype(BF16)
    for j in range(2):
        a_parts[j] = a[:, j * half : (j + 1) * half]
    if turn:
        pl.when(pair.sec == 0)(lambda: pl.semaphore_wait(turn[0], 1))
    send_a = pair.send(a_parts.at[peer], a_half.at[span(me)], send_sem.at[0], recv_sem.at[0])
    send_a.start()
    a_half[span(me)] = a_parts[me]
    for load in loads[:-1]:
        load.wait()
    part_send[span(me)] = nn(a_parts[me], wq_v[peer]).astype(BF16)
    send_own = pair.send(part_send.at[span(me)], got_part.at[span(me)], send_sem.at[1], recv_sem.at[1])
    send_own.start()
    send_a.wait_recv()
    part_send[span(peer)] = nn(a_half[span(peer)], wq_v[peer]).astype(BF16)
    send_other = pair.send(
        part_send.at[span(peer)], got_part.at[span(peer)], send_sem.at[2], recv_sem.at[2])
    send_other.start()
    mine = nn(a_half[...], wq_v[me])
    a_ref[...] = a_half[...]
    send_own.wait_recv()
    send_other.wait_recv()
    qkv_ref[...] = (mine + got_part[...].astype(F32)).astype(BF16)
    allowed = allowed_ref[...] > 0
    for i in range(PAIRS):
        for n in range(KV_IN_PAIR):
            for g in range(GROUP):
                q_at, k_at, v_at = head_at(i, n, g)
                j = (i * KV_IN_PAIR + n) * GROUP + g
                s = nt(qkv_ref[:, q_at], qkv_ref[:, k_at]) * SCALE
                s = jnp.where(allowed, s, MASKED_SCORE)
                ex = jnp.exp(s - jnp.max(s, axis=1, keepdims=True))
                p = (ex / jnp.sum(ex, axis=1, keepdims=True)).astype(BF16)
                p_ref[j] = p
                o_ref[:, pl.ds(j * HEAD_SIZE, HEAD_SIZE)] = nn(p, qkv_ref[:, v_at]).astype(BF16)
    loads[-1].wait()
    out_send[...] = nn(o_ref[span(peer)], wo_v[...]).astype(BF16)
    send_out = pair.send(out_send, got_out, send_sem.at[3], recv_sem.at[3])
    send_out.start()
    own = nn(o_ref[span(me)], wo_v[...])
    send_out.wait_recv()
    if turn:
        @pl.when(pair.sec == 1)
        def _():
            pl.semaphore_signal(
                turn[0], inc=1, device_id=(1 - pair.sec, pair.owner, me), device_id_type=MESH)

    h1 = h + own + got_out[...].astype(F32)
    h1_ref[...] = h1
    r2 = lax.rsqrt(jnp.mean(h1 * h1, axis=1, keepdims=True) + EPS)
    b = (h1 * r2 * gains_ref[pl.ds(1, 1), :]).astype(BF16)
    block_ref[:, pl.ds(0, width)] = b
    mask = mask_ref[...] > 0
    logits = jnp.where(mask, nt(b, router_ref[...]), MASKED_SCORE)
    ex = jnp.where(mask, jnp.exp(logits - jnp.max(logits, axis=1, keepdims=True)), 0.0)
    gates = ex / (0.5 * jnp.sum(ex, axis=1, keepdims=True))
    high = gates.astype(BF16).astype(F32)
    block_ref[:, pl.ds(width, LANES)] = jnp.where(mask_ref[...] > 1, gates - high, high).astype(BF16)
    for send in (send_a, send_own, send_other, send_out):
        send.wait_send()


def attention_forward(layer, h, allowed, gains, router, mask, weights, collective_id):
    rows, width = h.shape
    half, group = width // 2, 2 * rows
    qkv = (QUERY_WIDTH + 2 * KV_WIDTH) // 2
    heads = QUERY_HEADS // 2
    any_spec = pl.BlockSpec(memory_space=pl.ANY)
    vmem = pl.BlockSpec(memory_space=pltpu.VMEM)
    return pl.pallas_call(
        functools.partial(attention_forward_kernel, layer, rows, width),
        name="attention_forward",
        out_shape=(
            jax.ShapeDtypeStruct((rows, width + LANES), BF16),
            jax.ShapeDtypeStruct((rows, width), F32),
            jax.ShapeDtypeStruct((group, half), BF16),
            jax.ShapeDtypeStruct((group, qkv), BF16),
            jax.ShapeDtypeStruct((heads, group, group), BF16),
            jax.ShapeDtypeStruct((group, QUERY_WIDTH // 2), BF16),
        ),
        in_specs=[vmem] * 5 + [any_spec] * 4,
        out_specs=(vmem,) * 6,
        scratch_shapes=[
            pltpu.VMEM((2, half, qkv), BF16),
            pltpu.VMEM((QUERY_WIDTH // 2, width), BF16),
            pltpu.VMEM((2, rows, half), BF16),
            pltpu.VMEM((group, half), BF16),
            pltpu.VMEM((group, qkv), BF16),
            pltpu.VMEM((group, qkv), BF16),
            pltpu.VMEM((rows, width), BF16),
            pltpu.VMEM((rows, width), BF16),
            pltpu.SemaphoreType.DMA((LOADS,)),
            pltpu.SemaphoreType.DMA((4,)),
            pltpu.SemaphoreType.DMA((4,)),
        ] + ([pltpu.SemaphoreType.REGULAR] if layer == 0 else []),
        cost_estimate=COST,
        compiler_params=pltpu.CompilerParams(
            collective_id=collective_id, has_side_effects=True, vmem_limit_bytes=VMEM_BYTES),
    )(h, allowed, gains, router, mask, *weights)


def attention_backward_kernel(layer, rows, width, experts, router_grad_ref, db_ref, dout_ref, h1_ref, h_ref, gains_ref, a_ref, qkv_ref,
                              p_ref, o_ref, wq, wq_other, wo, wo_other, dh_ref, columns_ref, grad_hbm,
                              wq_v, wo_v, d_all, do, dqkv, got_dqkv, da_send, got_da, dh1_v, grad_q, grad_o,
                              gain_grads_ref, columns_v, load_sem, store_sem, send_sem, recv_sem):
    pair = Pair()
    me, peer = pair.me, pair.peer
    half = width // 2
    qkv_cols = dqkv.shape[1]
    pair_cols = qkv_cols // PAIRS
    loads = load_attention(layer, pair.sec, wq, wq_other, wo, wo_other, wq_v, wo_v, load_sem)
    pair.barrier()

    def span(who):
        return pl.ds(pl.multiple_of(who * rows, rows), rows)

    h1 = h1_ref[...]
    r2 = lax.rsqrt(jnp.mean(h1 * h1, axis=1, keepdims=True) + EPS)
    normed = h1 * r2
    db = db_ref[...]
    scaled = db * gains_ref[pl.ds(1, 1), :]
    gain_grads_ref[...] = jnp.zeros_like(gain_grads_ref)
    gain_grads_ref[pl.ds(experts + 1, 1), :] = jnp.sum(db * normed, axis=0, keepdims=True)
    dh1 = dout_ref[...].astype(F32) + r2 * (
        scaled - normed * jnp.mean(scaled * normed, axis=1, keepdims=True))
    dh1_v[...] = dh1
    d_all[span(me)] = dh1.astype(BF16)
    send_d = pair.send(d_all.at[span(me)], d_all.at[span(me)], send_sem.at[0], recv_sem.at[0])
    send_d.start()
    router_terms = router_grad_ref[...]
    lane = lax.broadcasted_iota(jnp.int32, router_terms.shape, 1)
    router_terms = router_terms + pltpu.roll(router_terms, LANES // 2, 1)
    columns_v[...] = jnp.where(lane < experts, router_terms, 0.0)
    for load in loads:
        load.wait()
    do[span(me)] = nt(d_all[span(me)], wo_v[...]).astype(BF16)
    send_d.wait_recv()
    do[span(peer)] = nt(d_all[span(peer)], wo_v[...]).astype(BF16)
    sends = [send_d]
    for i in range(PAIRS):
        cols = pl.ds(i * pair_cols, pair_cols)
        for n in range(KV_IN_PAIR):
            dk = dv = None
            for g in range(GROUP):
                q_at, k_at, v_at = head_at(i, n, g)
                j = (i * KV_IN_PAIR + n) * GROUP + g
                p_low = p_ref[j]
                p = p_low.astype(F32)
                d_head = do[:, pl.ds(j * HEAD_SIZE, HEAD_SIZE)]
                weighted = p * nt(d_head, qkv_ref[:, v_at])
                ds = (weighted - p * jnp.sum(weighted, axis=1, keepdims=True)).astype(BF16)
                dqkv[:, q_at] = (nn(ds, qkv_ref[:, k_at]) * SCALE).astype(BF16)
                dk_part, dv_part = tn(ds, qkv_ref[:, q_at]), tn(p_low, d_head)
                dk = dk_part if dk is None else dk + dk_part
                dv = dv_part if dv is None else dv + dv_part
            dqkv[:, k_at] = (dk * SCALE).astype(BF16)
            dqkv[:, v_at] = dv.astype(BF16)
        send = pair.send(dqkv.at[:, cols], got_dqkv.at[:, cols], send_sem.at[1 + i], recv_sem.at[1 + i])
        send.start()
        sends.append(send)
    da = nt(dqkv[...], wq_v[me])
    grad_q[me] = tn(a_ref[...], dqkv[...]).astype(BF16)
    grad_o[...] = tn(o_ref[...], d_all[...]).astype(BF16)
    store_o = pltpu.make_async_copy(
        grad_o, grad_hbm.at[:, pl.ds(QUERY_WIDTH + 2 * KV_WIDTH, width)], store_sem.at[LOADS - 1])
    store_o.start()
    for send in sends[1:]:
        send.wait_recv()
    da = da + nt(got_dqkv[...], wq_v[peer])
    da_send[...] = jnp.where(me == 0, da[rows:], da[:rows]).astype(BF16)
    send_da = pair.send(da_send, got_da, send_sem.at[1 + PAIRS], recv_sem.at[1 + PAIRS])
    send_da.start()
    own_da = jnp.where(me == 0, da[:rows], da[rows:])
    grad_q[peer] = tn(a_ref[...], got_dqkv[...]).astype(BF16)
    stores = [store_o]
    for j in range(2):
        for at, local, size in head_columns(j):
            store = pltpu.make_async_copy(
                grad_q.at[j, :, pl.ds(local, size)], grad_hbm.at[:, pl.ds(at, size)],
                store_sem.at[len(stores) - 1])
            store.start()
            stores.append(store)
    send_da.wait_recv()
    other_da = got_da[...].astype(F32)
    h = h_ref[...].astype(F32)
    r1 = lax.rsqrt(jnp.mean(h * h, axis=1, keepdims=True) + EPS)
    halves = []
    total = jnp.zeros((rows, 1), F32)
    for j in range(2):
        cols = pl.ds(j * half, half)
        da_j = jnp.where(me == j, own_da, other_da)
        normed = h[:, j * half : (j + 1) * half] * r1
        gain_grads_ref[pl.ds(experts, 1), cols] = jnp.sum(da_j * normed, axis=0, keepdims=True)
        scaled = da_j * gains_ref[pl.ds(0, 1), cols]
        total = total + jnp.sum(scaled * normed, axis=1, keepdims=True)
        halves.append((cols, scaled, normed))
    columns = columns_v[...] + jnp.transpose(gain_grads_ref[...])
    columns_ref[...] = columns.astype(BF16)
    for cols, scaled, normed in halves:
        dh_ref[:, cols] = dh1_v[:, cols] + r1 * (scaled - normed * (total / width))
    for send in sends + [send_da]:
        send.wait_send()
    for store in stores:
        store.wait()


def attention_backward(layer, experts, router_grad, db, dout, h1, h, gains, a_half, qkv, p, o, weights, collective_id):
    rows, width = db.shape
    half, group = width // 2, 2 * rows
    cols = (QUERY_WIDTH + 2 * KV_WIDTH) // 2
    any_spec = pl.BlockSpec(memory_space=pl.ANY)
    vmem = pl.BlockSpec(memory_space=pltpu.VMEM)
    return pl.pallas_call(
        functools.partial(attention_backward_kernel, layer, rows, width, experts),
        name="attention_backward",
        out_shape=(
            jax.ShapeDtypeStruct((rows, width), F32),
            jax.ShapeDtypeStruct((width, LANES), BF16),
            jax.ShapeDtypeStruct((half, QUERY_WIDTH + 2 * KV_WIDTH + width), BF16),
        ),
        in_specs=[vmem] * 10 + [any_spec] * 4,
        out_specs=(vmem, vmem, any_spec),
        scratch_shapes=[
            pltpu.VMEM((2, half, cols), BF16),
            pltpu.VMEM((QUERY_WIDTH // 2, width), BF16),
            pltpu.VMEM((group, width), BF16),
            pltpu.VMEM((group, QUERY_WIDTH // 2), BF16),
            pltpu.VMEM((group, cols), BF16),
            pltpu.VMEM((group, cols), BF16),
            pltpu.VMEM((rows, half), BF16),
            pltpu.VMEM((rows, half), BF16),
            pltpu.VMEM((rows, width), F32),
            pltpu.VMEM((2, half, cols), BF16),
            pltpu.VMEM((QUERY_WIDTH // 2, width), BF16),
            pltpu.VMEM((LANES, width), F32),
            pltpu.VMEM((width, LANES), F32),
            pltpu.SemaphoreType.DMA((LOADS,)),
            pltpu.SemaphoreType.DMA((LOADS,)),
            pltpu.SemaphoreType.DMA((2 + PAIRS,)),
            pltpu.SemaphoreType.DMA((2 + PAIRS,)),
        ],
        cost_estimate=COST,
        compiler_params=pltpu.CompilerParams(
            collective_id=collective_id, has_side_effects=True, vmem_limit_bytes=VMEM_BYTES),
    )(router_grad, db, dout, h1, h, gains, a_half, qkv, p, o, *weights)


def dot(a, b, dims):
    return lax.dot_general(a, b, (dims, ((), ())), preferred_element_type=F32)


def rms_scale(values):
    return lax.rsqrt(jnp.mean(values * values, axis=-1, keepdims=True) + EPS)


def swap_cores(value):
    return lax.ppermute(value, "section", [(0, 1), (1, 0)])


def both_layers(own):
    return lax.all_gather(own, "section", axis=0, tiled=False)


def document_mask(sequence_lengths, rows):
    pos = jnp.arange(rows, dtype=jnp.int32)
    ends = jnp.cumsum(sequence_lengths)
    doc = jnp.sum((pos[:, None] >= ends[None, :]).astype(jnp.int32), axis=1)
    return (doc[:, None] == doc[None, :]) & (pos[None, :] <= pos[:, None])


def plain_attention(qkv, allowed, heads, kv_heads):
    rows = qkv.shape[0]
    group = heads // kv_heads
    q = qkv[:, : heads * HEAD_SIZE].reshape(rows, kv_heads, group, HEAD_SIZE)
    k = qkv[:, heads * HEAD_SIZE : (heads + kv_heads) * HEAD_SIZE].reshape(rows, kv_heads, HEAD_SIZE)
    v = qkv[:, (heads + kv_heads) * HEAD_SIZE :].reshape(rows, kv_heads, HEAD_SIZE)
    s = jnp.einsum("qhgd,khd->hgqk", q, k, preferred_element_type=F32) * HEAD_SIZE ** (-0.5)
    s = jnp.where(allowed[None, None], s, MASKED_SCORE)
    ex = jnp.exp(s - jnp.max(s, axis=-1, keepdims=True))
    p = ex / jnp.sum(ex, axis=-1, keepdims=True)
    o = jnp.einsum("hgqk,khd->qhgd", p.astype(BF16), v, preferred_element_type=F32)
    return o.reshape(rows, heads * HEAD_SIZE).astype(BF16), p, (q, k, v)


def plain_attention_backward(do, p, heads_in):
    q, k, v = heads_in
    rows = q.shape[0]
    dh = do.reshape(q.shape)
    dv = jnp.einsum("hgqk,qhgd->khd", p.astype(BF16), dh, preferred_element_type=F32)
    dp = jnp.einsum("qhgd,khd->hgqk", dh, v, preferred_element_type=F32)
    ds = (p * (dp - jnp.sum(p * dp, axis=-1, keepdims=True))).astype(BF16)
    dq = jnp.einsum("hgqk,khd->qhgd", ds, k, preferred_element_type=F32) * HEAD_SIZE ** (-0.5)
    dk = jnp.einsum("hgqk,qhgd->khd", ds, q, preferred_element_type=F32) * HEAD_SIZE ** (-0.5)
    return jnp.concatenate(
        [dq.reshape(rows, -1), dk.reshape(rows, -1), dv.reshape(rows, -1)], axis=1
    ).astype(BF16)


def column_parts(n, j):
    qw, kw = QUERY_WIDTH // n, KV_WIDTH // n
    return (
        (j * qw, qw),
        (QUERY_WIDTH + j * kw, kw),
        (QUERY_WIDTH + KV_WIDTH + j * kw, kw),
    )


def plain_shards(
    edge_inputs, seq_lengths, routes, w_qkv, w_out, w_router, gain_attn, gain_moe, w_gate_up, w_down
):
    sec = lax.axis_index("section")
    owner = lax.axis_index("expert")
    shard_pos = lax.axis_index("shard")
    n_shard = lax.axis_size("shard")
    n_owner = lax.axis_size("expert")
    rows, width = edge_inputs.shape[2], edge_inputs.shape[3]
    experts = w_router.shape[2]
    group_rows = rows * n_shard
    half = width // n_shard
    heads, kv_heads = QUERY_HEADS // n_shard, KEY_VALUE_HEADS // n_shard

    def pick(array, index):
        return lax.dynamic_index_in_dim(array, index, 0, keepdims=False)

    own_edge, other_edge = pick(edge_inputs[0], sec), swap_cores(pick(edge_inputs[0], 1 - sec))
    x_in = jnp.where(sec == 0, own_edge, other_edge)
    dy = jnp.where(sec == 0, other_edge, own_edge)
    own_routes, other_routes = pick(routes[0], sec), swap_cores(pick(routes[0], 1 - sec))
    layer_routes = (
        jnp.where(sec == 0, own_routes, other_routes),
        jnp.where(sec == 0, other_routes, own_routes),
    )
    allowed = document_mask(pick(seq_lengths, sec)[0], group_rows)
    wq = both_layers(w_qkv[0])
    wo = both_layers(w_out[0])
    small = jnp.concatenate([w_router[0], gain_attn[0][:, None], gain_moe[0][:, None]], axis=1)
    small = lax.all_gather(both_layers(small), "shard", axis=1, tiled=True)
    wgu = both_layers(w_gate_up[0])
    wd = both_layers(w_down[0])
    columns = jnp.arange(experts, dtype=jnp.int32)
    route_masks = [
        jnp.any(r[:, :, None] == columns[None, None, :], axis=1).astype(BF16) for r in layer_routes
    ]
    plane_masks = [lax.all_gather(m, "expert", axis=0, tiled=True) for m in route_masks]

    def forward(layer, h):
        gain_a = small[layer, :, experts].astype(F32)[None, :]
        gain_m = small[layer, :, experts + 1].astype(F32)[None, :]
        router = small[layer, :, :experts]
        r1 = rms_scale(h)
        a = (h * r1 * gain_a).astype(BF16)
        a_half = lax.all_to_all(
            a.reshape(rows, n_shard, half), "shard", split_axis=1, concat_axis=0, tiled=True
        ).reshape(group_rows, half)
        blocks = []
        for j in range(n_shard):
            blocks.append(
                jnp.concatenate(
                    [
                        dot(a_half, wq[layer, :, at : at + size], ((1,), (0,)))
                        for at, size in column_parts(n_shard, j)
                    ],
                    axis=1,
                ).astype(BF16)
            )
        qkv = lax.psum_scatter(jnp.stack(blocks), "shard", scatter_dimension=0, tiled=False)
        o, p, heads_in = plain_attention(qkv, allowed, heads, kv_heads)
        part = dot(o, wo[layer], ((1,), (0,))).astype(BF16)
        h1 = h + lax.psum_scatter(part, "shard", scatter_dimension=0, tiled=True).astype(F32)
        r2 = rms_scale(h1)
        b = (h1 * r2 * gain_m).astype(BF16)
        b_all = lax.all_gather(b, "expert", axis=0, tiled=True)
        mask = plane_masks[layer].astype(F32) > 0
        logits = jnp.where(mask, dot(b_all, router, ((1,), (0,))), MASKED_SCORE)
        ex = jnp.where(mask, jnp.exp(logits - jnp.max(logits, axis=1, keepdims=True)), 0.0)
        gates = ex / jnp.sum(ex, axis=1, keepdims=True)
        own_gates = lax.dynamic_slice_in_dim(gates, owner * EXP_DEV, EXP_DEV, 1)
        kept, scaled = [], []
        for j in range(EXP_DEV):
            gu = dot(b_all, wgu[layer, j], ((1,), (0,)))
            g, u = gu[:, :FF], gu[:, FF:]
            scaled.append((g * jax.nn.sigmoid(g) * u * own_gates[:, j : j + 1]).astype(BF16))
            kept.append(gu.astype(BF16))
        scaled = jnp.concatenate(scaled, axis=1)
        moe_part = dot(scaled, wd[layer].reshape(EXP_DEV * FF, width), ((1,), (0,))).astype(BF16)
        moe = lax.psum_scatter(moe_part, "expert", scatter_dimension=0, tiled=True).astype(F32)
        state = (h, r1, a_half, p, heads_in, o, h1, r2, b_all, own_gates, kept, scaled, moe)
        return h1 + moe, state

    def backward(layer, dout, dout_low, state):
        h, r1, a_half, p, heads_in, o, h1, r2, b_all, own_gates, kept, scaled, moe = state
        gain_a = small[layer, :, experts].astype(F32)[None, :]
        gain_m = small[layer, :, experts + 1].astype(F32)[None, :]
        router = small[layer, :, :experts]
        own_router = lax.dynamic_slice_in_dim(router, owner * EXP_DEV, EXP_DEV, 1)
        total = lax.all_gather(jnp.sum(dout * moe, axis=1), "expert", axis=0, tiled=True)
        dout_all = lax.all_gather(dout_low, "expert", axis=0, tiled=True)
        dgus, dcs = [], []
        for j in range(EXP_DEV):
            gate = own_gates[:, j : j + 1]
            g, u = kept[j][:, :FF].astype(F32), kept[j][:, FF:].astype(F32)
            sig = jax.nn.sigmoid(g)
            silu = g * sig
            dz = dot(dout_all, wd[layer, j], ((1,), (1,)))
            dgate = jnp.sum(dz * silu * u, axis=1, keepdims=True)
            dcs.append(gate * (dgate - total[:, None]))
            dz = dz * gate
            dgus.append(
                jnp.concatenate(
                    [dz * u * sig * (1.0 + g * (1.0 - sig)), dz * silu], axis=1
                ).astype(BF16)
            )
        dc = jnp.concatenate(dcs, axis=1)
        db_part = sum(dot(dgus[j], wgu[layer, j], ((1,), (1,))) for j in range(EXP_DEV))
        for j in range(EXP_DEV):
            db_part = db_part + dc[:, j : j + 1] * own_router[:, j].astype(F32)[None, :]
        db = lax.psum_scatter(
            db_part.astype(BF16), "expert", scatter_dimension=0, tiled=True
        ).astype(F32)
        grad_down = dot(scaled, dout_all, ((0,), (0,))).reshape(EXP_DEV, FF, width)
        grad_gu = jnp.stack([dot(b_all, dgus[j], ((0,), (0,))) for j in range(EXP_DEV)])
        grad_router = lax.dot_general(
            dc, b_all.astype(F32), (((0,), (0,)), ((), ())), precision=lax.Precision.HIGHEST
        )
        normed = h1 * r2
        grad_gain_m = jnp.sum(db * normed, axis=0)
        scaled_db = db * gain_m
        dh1 = dout + r2 * (scaled_db - normed * jnp.mean(scaled_db * normed, axis=1, keepdims=True))
        dattn = lax.all_gather(dh1.astype(BF16), "shard", axis=0, tiled=True)
        do = dot(dattn, wo[layer], ((1,), (1,))).astype(BF16)
        grad_out = dot(o, dattn, ((0,), (0,)))
        dqkv = lax.all_gather(plain_attention_backward(do, p, heads_in), "shard", axis=0, tiled=False)
        da = 0.0
        grad_qkv = []
        for part in range(3):
            grad_qkv.append([])
        for j in range(n_shard):
            at_local = 0
            for part, (at, size) in enumerate(column_parts(n_shard, j)):
                piece = dqkv[j, :, at_local : at_local + size]
                at_local += size
                da = da + dot(piece, wq[layer, :, at : at + size], ((1,), (1,)))
                grad_qkv[part].append(dot(a_half, piece, ((0,), (0,))))
        grad_qkv = jnp.concatenate([x for part in grad_qkv for x in part], axis=1)
        da = lax.all_to_all(
            da.astype(BF16), "shard", split_axis=0, concat_axis=1, tiled=True
        ).astype(F32)
        normed = h * r1
        grad_gain_a = jnp.sum(da * normed, axis=0)
        scaled_da = da * gain_a
        dh = dh1 + r1 * (scaled_da - normed * jnp.mean(scaled_da * normed, axis=1, keepdims=True))
        return dh, (grad_qkv, grad_out, grad_router, grad_gain_a, grad_gain_m, grad_gu, grad_down)

    out0, state0 = forward(0, x_in.astype(F32))
    mid = out0.astype(BF16).astype(F32)
    final, state1 = forward(1, mid)
    dh_one, grads1 = backward(1, dy.astype(F32), dy, state1)
    low = dh_one.astype(BF16)
    dh_zero, grads0 = backward(0, low.astype(F32), low, state0)

    def half_sum(grad):
        low_grad = grad.astype(BF16)
        halves = low_grad.reshape((2, -1) + low_grad.shape[1:])
        got = swap_cores(pick(halves, 1 - sec))
        return (pick(halves, sec).astype(F32) + got.astype(F32)).astype(BF16)

    def to_owner(half0, half1):
        keep = jnp.where(sec == 0, half0, half1)
        got = swap_cores(jnp.where(sec == 0, half1, half0))
        first = jnp.where(sec == 0, keep, got)
        second = jnp.where(sec == 0, got, keep)
        return jnp.concatenate([first, second], axis=0).astype(F32)

    attn_halves, exp_halves = [], []
    for grads in (grads0, grads1):
        attn = half_sum(jnp.concatenate([grads[0], grads[1]], axis=1))
        attn_halves.append(lax.psum(attn, "expert"))
        exp_halves.append(tuple(lax.psum(half_sum(g), "shard") for g in (grads[5], grads[6])))
    attn = to_owner(*attn_halves)
    grad_qkv, grad_out = attn[:, : w_qkv.shape[2]], attn[:, w_qkv.shape[2] :]
    grad_gu = to_owner(exp_halves[0][0], exp_halves[1][0])
    grad_down = to_owner(exp_halves[0][1], exp_halves[1][1])

    tiny = []
    for grads in (grads0, grads1):
        hot = jnp.arange(experts)[:, None] == owner * EXP_DEV + jnp.arange(EXP_DEV)[None, :]
        router = sum(
            jnp.where(hot[:, j : j + 1], grads[2][j][None, :], 0.0) for j in range(EXP_DEV)
        )
        tiny.append(jnp.concatenate([router, grads[3][None, :], grads[4][None, :]], axis=0))
    tiny = lax.psum(jnp.stack(tiny), ("section", "expert", "shard"))
    tiny = lax.dynamic_slice_in_dim(pick(tiny, sec), shard_pos * half, half, 1)

    send = jnp.where(sec == 0, final, dh_zero)
    keep = jnp.where(sec == 0, dh_zero, final)
    got = swap_cores(send)
    edge = jnp.where(sec == 0, jnp.stack([keep, got]), jnp.stack([got, keep]))
    return (
        edge[None],
        grad_qkv[None],
        grad_out[None],
        tiny[:experts].T[None],
        tiny[experts][None],
        tiny[experts + 1][None],
        grad_gu[None],
        grad_down[None],
    )


def kernel_shards(
    edge_inputs, seq_lengths, routes, w_qkv, w_out, w_router, gain_attn, gain_moe, w_gate_up, w_down
):
    sec = lax.axis_index("section")
    owner = lax.axis_index("expert")
    shard_pos = lax.axis_index("shard")
    rows, width = edge_inputs.shape[2], edge_inputs.shape[3]
    experts = w_router.shape[2]
    half = width // 2
    attn_cols = w_qkv.shape[2] + w_out.shape[2]

    def pick(array, index):
        return lax.dynamic_index_in_dim(array, index, 0, keepdims=False)

    def swap_shards(value):
        return lax.ppermute(value, "shard", [(0, 1), (1, 0)])

    def by_core(own, other):
        return jnp.where(sec == 0, own, other), jnp.where(sec == 0, other, own)

    small = jnp.concatenate([w_router[0].T, gain_attn, gain_moe], axis=0)
    across = lax.ppermute(small, ("section", "shard"), [(0, 3), (1, 2), (2, 1), (3, 0)])

    def joined(mine, other):
        return jnp.where(
            shard_pos == 0,
            jnp.concatenate([mine, other], axis=1),
            jnp.concatenate([other, mine], axis=1),
        )

    layer_small = by_core(joined(small, swap_shards(small)), joined(swap_cores(small), across))
    x_in, dy = by_core(pick(edge_inputs[0], sec), swap_cores(pick(edge_inputs[0], 1 - sec)))
    layer_routes = by_core(pick(routes[0], sec), swap_cores(pick(routes[0], 1 - sec)))
    allowed = document_mask(pick(seq_lengths, sec)[0], 2 * rows).astype(F32)
    attn_weights = (w_qkv[0], swap_cores(w_qkv[0]), w_out[0], swap_cores(w_out[0]))
    expert_weights = (
        w_gate_up[0], swap_cores(w_gate_up[0]), w_down[0], swap_cores(w_down[0])
    )
    gains, routers, masks = [], [], []
    for layer in range(2):
        gains.append(
            jnp.pad(layer_small[layer][experts:].astype(F32), ((0, 8 - 2), (0, 0)))
        )
        router = layer_small[layer][:experts]
        router = jnp.concatenate([router, router], axis=0)
        routers.append(jnp.pad(router, ((0, LANES - 2 * experts), (0, 0))))
        lane = jnp.arange(LANES, dtype=jnp.int32)[None, :]
        hot = jnp.any(layer_routes[layer][:, :, None] == lane[None] % experts, axis=1)
        masks.append(
            jnp.where(hot & (lane < 2 * experts), 1.0 + (lane >= experts), 0.0).astype(F32)
        )

    def forward(layer, h):
        block, h1, *attn_state = attention_forward(
            layer, h, allowed, gains[layer], routers[layer], masks[layer], attn_weights, 1 + layer
        )
        moe, *expert_state = moe_forward(layer, block, expert_weights, experts, 3 + layer)
        return h1 + moe, (h, h1, moe, attn_state, expert_state)

    def backward(layer, dout, state, later):
        h, h1, moe, attn_state, expert_state = state
        outer = jnp.sum(dout.astype(F32) * moe, axis=1, keepdims=True)
        block = with_lanes(dout, split_terms(outer))
        own_router = lax.dynamic_slice_in_dim(
            layer_small[layer].astype(F32), owner * EXP_DEV, EXP_DEV, 0
        )
        own_router = jnp.pad(own_router, ((0, 8 - EXP_DEV), (0, 0)))
        results = moe_backward(
            layer, block, own_router, expert_weights, expert_state, later, experts, 5 + layer
        )
        db, keep_gu, keep_down, send_gu, send_down, grad_router = results[:6]
        dh, columns, grad_attn = attention_backward(
            layer, experts, grad_router, db, dout, h1, h, gains[layer], *attn_state, attn_weights,
            7 + layer,
        )
        places = LINE * SIDE
        sub = half // (2 * places)
        grad_attn = grad_attn.reshape(places, 2, sub, attn_cols)
        columns = columns.reshape(2, places, 2, sub, LANES)
        return dh, grad_attn, columns, (keep_gu, keep_down, send_gu, send_down), results[6:8]

    out0, state0 = forward(0, x_in)
    final, state1 = forward(1, out0.astype(BF16))
    dh_one, attn1, columns1, experts1, _ = backward(1, dy, state1, ())
    dh_zero, attn0, columns0, experts0, sums1 = backward(
        0, dh_one.astype(BF16), state0, experts1
    )
    send = jnp.where(sec == 0, final, dh_zero)
    attn, gu_own, down_own, gu_got, down_got, down_one, gu_moved, down_moved, got = reduce_gradients(
        attn1, attn0, columns1, columns0, experts0, *sums1, send, 9
    )
    grad_qkv, grad_out, grad_gu, grad_down = finish_outputs(
        attn,
        (gu_own, gu_got, sums1[0], gu_moved),
        (down_own, down_got, down_one, down_moved),
        w_qkv.shape[2],
        w_out.shape[2],
    )
    tiny = attn[:, attn_cols : attn_cols + experts + 2].astype(F32)
    keep = jnp.where(sec == 0, dh_zero, final)
    edge = jnp.where(sec == 0, jnp.stack([keep, got]), jnp.stack([got, keep]))
    return (
        edge[None],
        grad_qkv[None],
        grad_out[None],
        tiny[:, :experts][None],
        tiny[:, experts][None],
        tiny[:, experts + 1][None],
        grad_gu[None],
        grad_down[None],
    )


def shards(*arrays):
    if lax.axis_size("expert") == LINE * SIDE and lax.axis_size("shard") == 2:
        return kernel_shards(*arrays)
    return plain_shards(*arrays)


def solution(mesh):
    in_specs = (
        P("section", None, ("expert", "shard"), None),
        P(None, "expert", None),
        P("section", None, ("expert", "shard"), None),
        P("section", "shard", None),
        P("section", "shard", None),
        P("section", "shard", None),
        P("section", "shard"),
        P("section", "shard"),
        P("section", "expert", None, None),
        P("section", "expert", None, None),
    )
    out_specs = (
        P("section", None, ("expert", "shard"), None),
        P("section", "shard", None),
        P("section", "shard", None),
        P("section", "shard", None),
        P("section", "shard"),
        P("section", "shard"),
        P("section", "expert", None, None),
        P("section", "expert", None, None),
    )
    return jax.shard_map(shards, mesh=mesh, in_specs=in_specs, out_specs=out_specs, check_vma=False)
```

profile of v0, /device:TPU:0, one launch (start us, length us, event | category | flops | bytes accessed | tf_op | source)
XLA Modules:
  0.0 650.7 jit_solution(18128195129550854885)
XLA Ops:
  0.7 0.9 pad_maximum_fusion
  1.5 2.5 collective-permute-start.3
  4.0 0.7 collective-permute-start.2
  4.7 0.7 dynamic-slice_bitcast_fusion.1
  6.2 0.8 fusion.11.allowed_ref
  7.0 1.0 dynamic-slice_bitcast_fusion
  8.3 0.7 bitcast_select_fusion.3
  9.6 0.7 and_select_fusion
  11.1 0.9 broadcast_select_fusion.1
  12.0 0.9 broadcast_select_fusion.2
  14.8 0.8 fusion.8.router_ref
  16.2 0.8 fusion.9.router_ref
  17.0 0.9 bitcast_select_fusion.h_ref
  17.9 50.5 %attention_forward.2 = (bf16[128,1664]{1,0:T(8,128)(2,1)}, f32[128,1536]{1,0:T(8,128)}, bf16[256,768]{1,0:T(8,128)(2,1)}, bf16[256,1280]{1,0:T(8,128)(2,1)}, bf1...) custom-call(bf16[128,1536]{1,0:T(8,128)(2,1)} %bitcast_select_fusion.h_ref, f32[256,256]{1,0:T(8,128)} %fusion.11.allowed_ref, ...), custom_call_target="tpu_custom_call" | custom-call | flops 99999997952 | bytes 16777216 | tf_op jit(solution)/shard_map/attention_forward/pallas_call | solution.py:1157
  68.4 71.3 %moe_forward.2 = (f32[128,1536]{1,0:T(8,128)}, bf16[1024,1664]{1,0:T(8,128)(2,1)}, bf16[1024,2048]{1,0:T(8,128)(2,1)}, bf16[1024,1024]{1,0:T(8,128)(2,1)}) custom-call(bf16[128,1664]{1,0:T(8,128)(2,1)} %get-tuple-element.62.block_ref, bf16[2,1536,1024]{2,1,0:T(8,128)(2,1)} %bitcast.59, bf16[2,1536,1024]{2,1,0:T(8,128)(2,1)} %collective-permute-done.7.gu_other, ...), custom_call_target="tpu_custom_call" | custom-call | flops 99999997952 | bytes 16777216 | tf_op jit(solution)/shard_map/moe_forward/pallas_call | solution.py:386
  139.8 2.0 add_convert_fusion.h_ref
  141.8 28.1 %attention_forward.3 = (bf16[128,1664]{1,0:T(8,128)(2,1)}, f32[128,1536]{1,0:T(8,128)}, bf16[256,768]{1,0:T(8,128)(2,1)}, bf16[256,1280]{1,0:T(8,128)(2,1)}, bf1...) custom-call(bf16[128,1536]{1,0:T(8,128)(2,1)} %add_convert_fusion.h_ref, f32[256,256]{1,0:T(8,128)} %fusion.11.allowed_ref, ...), custom_call_target="tpu_custom_call" | custom-call | flops 99999997952 | bytes 16777216 | tf_op jit(solution)/shard_map/attention_forward/pallas_call | solution.py:1157
  170.0 67.0 %moe_forward.3 = (f32[128,1536]{1,0:T(8,128)}, bf16[1024,1664]{1,0:T(8,128)(2,1)}, bf16[1024,2048]{1,0:T(8,128)(2,1)}, bf16[1024,1024]{1,0:T(8,128)(2,1)}) custom-call(bf16[128,1664]{1,0:T(8,128)(2,1)} %get-tuple-element.64.block_ref, bf16[2,1536,1024]{2,1,0:T(8,128)(2,1)} %bitcast.60, bf16[2,1536,1024]{2,1,0:T(8,128)(2,1)} %collective-permute-done.7.gu_other, ...), custom_call_target="tpu_custom_call" | custom-call | flops 99999997952 | bytes 16777216 | tf_op jit(solution)/shard_map/moe_forward/pallas_call | solution.py:386
  237.0 1.4 multiply_reduce_fusion.1
  238.6 0.8 fusion.6.block_ref
  239.4 65.5 %moe_backward.2 = (f32[128,1536]{1,0:T(8,128)}, bf16[1536,1024]{1,0:T(8,128)(2,1)}, bf16[512,1536]{1,0:T(8,128)(2,1)}, bf16[1536,1024]{1,0:T(8,128)(2,1)}, bf16[...) custom-call(bf16[128,1664]{1,0:T(8,128)(2,1)} %fusion.6.block_ref, f32[8,1536]{1,0:T(8,128)} %pad.38.router_ref, ...), custom_call_target="tpu_custom_call" | custom-call | flops 99999997952 | bytes 16777216 | tf_op jit(solution)/shard_map/moe_backward/pallas_call | solution.py:621
  304.9 31.6 %attention_backward.2 = (f32[128,1536]{1,0:T(8,128)}, bf16[1536,128]{1,0:T(8,128)(2,1)}, bf16[768,4096]{1,0:T(8,128)(2,1)}) custom-call(f32[1536,128]{1,0:T(8,128)} %get-tuple-element.69.router_grad_ref, f32[128,1536]{1,0:T(8,128)} %get-tuple-element.70.db_ref, bf16[128,1536]{1,0:T(8,128)(2,1)} %copy-done.9, f32[128,1536]{1,0:T(8,128)} %get-tuple-element.71.h1_ref, ...), custom_call_target="tpu_custom_call" | custom-call | flops 99999997952 | bytes 16777216 | tf_op jit(solution)/shard_map/attention_backward/pallas_call | solution.py:1300
  336.5 1.3 multiply_reduce_fusion
  338.0 0.8 fusion.7.block_ref
  338.8 96.7 %moe_backward.3 = (f32[128,1536]{1,0:T(8,128)}, bf16[1536,1024]{1,0:T(8,128)(2,1)}, bf16[512,1536]{1,0:T(8,128)(2,1)}, bf16[1536,1024]{1,0:T(8,128)(2,1)}, bf16[...) custom-call(bf16[128,1664]{1,0:T(8,128)(2,1)} %fusion.7.block_ref, ...), custom_call_target="tpu_custom_call" | custom-call | flops 99999997952 | bytes 16777216 | tf_op jit(solution)/shard_map/moe_backward/pallas_call | solution.py:621
  435.6 37.7 %attention_backward.3 = (f32[128,1536]{1,0:T(8,128)}, bf16[1536,128]{1,0:T(8,128)(2,1)}, bf16[768,4096]{1,0:T(8,128)(2,1)}) custom-call(f32[1536,128]{1,0:T(8,128)} %get-tuple-element.84.router_grad_ref, f32[128,1536]{1,0:T(8,128)} %get-tuple-element.85.db_ref, bf16[128,1536]{1,0:T(8,128)(2,1)} %copy-done.6, f32[128,1536]{1,0:T(8,128)} %get-tuple-element.61.h1_ref, ...), custom_call_target="tpu_custom_call" | custom-call | flops 99999997952 | bytes 16777216 | tf_op jit(solution)/shard_map/attention_backward/pallas_call | solution.py:1300
  473.3 2.2 select_bitcast_fusion
  475.6 154.7 %reduce_gradients.1 = (bf16[768,4224]{1,0:T(8,128)(2,1)}, bf16[1536,1024]{1,0:T(8,128)(2,1)}, bf16[512,1536]{1,0:T(8,128)(2,1)}, bf16[1536,1024]{1,0:T(8,128)(2,...) custom-call(bf16[8,2,48,4096]{3,2,1,0:T(8,128)(2,1)} %bitcast.48, ...), custom_call_target="tpu_custom_call" | custom-call | tf_op jit(solution)/shard_map/reduce_gradients/pallas_call | solution.py:888
  630.3 1.0 slice_convert_fusion
  631.9 0.8 copy.39
  633.8 1.3 maximum_select_fusion
  635.0 15.4 %finish_outputs.1 = (f32[768,2560]{1,0:T(8,128)}, f32[768,1536]{1,0:T(8,128)}, f32[2,1536,1024]{2,1,0:T(8,128)}, f32[2,512,1536]{2,1,0:T(8,128)}) custom-call(bf16[768,4224]{1,0:T(8,128)(2,1)} %get-tuple-element.102.attn, bf16[1536,1024]{1,0:T(8,128)(2,1)} %get-tuple-element.103.gu_own, bf16[1536,1024]{1,0:T(8,128)(2,1)} %get-tuple-element.104.gu_got, ...), custom_call_target="tpu_custom_call" | custom-call | tf_op jit(solution)/shard_map/finish_outputs/pallas_call | solution.py:981
  (70 shorter events, 7.2 us)
Async XLA Ops:
  0.6 5.3 copy-start
  0.6 16.4 %copy-start.4 = (bf16[1,2,128,1536]{3,2,1,0:T(8,128)(2,1)S(1)}, bf16[1,2,128,1536]{3,2,1,0:T(8,128)(2,1)}, u32[]{:S(2)}) copy-start(bf16[1,2,128,1536]{3,2,1,0:T(8,128)(2,1)} %param.10) | copy-start | bytes 2359300
  1.5 8.8 %collective-permute-start.3 = (bf16[18,768]{1,0:T(8,128)(2,1)S(1)}, bf16[18,768]{1,0:T(8,128)(2,1)S(1)}, u32[]{:S(2)}, u32[]{:S(2)}) collective-permute-start(bf16[18,768]{1,0:T(8,128)(2,1)S(1)} %pad_maximum_fusion), channel_id=1, source_target_pairs={{0,17},{1,16},{16,1},{17,0},{2,19},{3,18},{18,3},{19,2},{4,21},{5,... | collective-permute-start | bytes 82952 | tf_op jit(solution)/shard_map/ppermute | solution.py:1618
  4.0 6.6 %collective-permute-start.2 = (bf16[18,768]{1,0:T(8,128)(2,1)S(1)}, bf16[18,768]{1,0:T(8,128)(2,1)S(1)}, u32[]{:S(2)}, u32[]{:S(2)}) collective-permute-start(bf16[18,768]{1,0:T(8,128)(2,1)S(1)} %pad_maximum_fusion), channel_id=1, source_target_pairs={{0,16},{16,0},{1,17},{17,1},{2,18},{18,2},{3,19},{19,3},{4,20},{20... | collective-permute-start | bytes 82952 | tf_op jit(solution)/shard_map/ppermute | solution.py:1344
  4.7 6.1 collective-permute-start.1
  5.4 2.7 collective-permute-start.4
  5.6 12.3 %collective-permute-start.5 = (bf16[768,2560]{1,0:T(8,128)(2,1)}, bf16[768,2560]{1,0:T(8,128)(2,1)}, u32[]{:S(2)}, u32[]{:S(2)}) collective-permute-start(bf16[768,2560]{1,0:T(8,128)(2,1)} %bitcast.65), channel_id=1, source_target_pairs={{0,16},{16,0},{1,17},{17,1},{2,18},{18,2},{3,19},{19,3},{4,20},{20... | collective-permute-start | bytes 11796488 | tf_op jit(solution)/shard_map/ppermute | solution.py:1344
  8.1 9.8 %collective-permute-start.6 = (bf16[768,1536]{1,0:T(8,128)(2,1)}, bf16[768,1536]{1,0:T(8,128)(2,1)}, u32[]{:S(2)}, u32[]{:S(2)}) collective-permute-start(bf16[768,1536]{1,0:T(8,128)(2,1)} %bitcast.75), channel_id=1, source_target_pairs={{0,16},{16,0},{1,17},{17,1},{2,18},{18,2},{3,19},{19,3},{4,20},{20... | collective-permute-start | bytes 7077896 | tf_op jit(solution)/shard_map/ppermute | solution.py:1344
  10.3 6.7 %collective-permute-start = (bf16[128,1536]{1,0:T(8,128)(2,1)S(1)}, bf16[128,1536]{1,0:T(8,128)(2,1)S(1)}, u32[]{:S(2)}, u32[]{:S(2)}) collective-permute-start(bf16[128,1536]{1,0:T(8,128)(2,1)S(1)} %dynamic-slice_bitcast_fusion), channel_id=1, source_target_pairs={{0,16},{16,0},{1,17},{17,1},{2,18},{18,2},{3,19},{19,3},{4,20},{20... | collective-permute-start | bytes 1179656 | tf_op jit(solution)/shard_map/ppermute | solution.py:1344
  10.6 57.8 %collective-permute-start.8 = (bf16[2,512,1536]{2,1,0:T(8,128)(2,1)}, bf16[2,512,1536]{2,1,0:T(8,128)(2,1)}, u32[]{:S(2)}, u32[]{:S(2)}) collective-permute-start(bf16[2,512,1536]{2,1,0:T(8,128)(2,1)} %bitcast.70), channel_id=1, source_target_pairs={{0,16},{16,0},{1,17},{17,1},{2,18},{18,2},{3,19},{19,3},{4,20},{20... | collective-permute-start | bytes 9437192 | tf_op jit(solution)/shard_map/ppermute | solution.py:1344
  10.8 57.6 %collective-permute-start.7 = (bf16[2,1536,1024]{2,1,0:T(8,128)(2,1)}, bf16[2,1536,1024]{2,1,0:T(8,128)(2,1)}, u32[]{:S(2)}, u32[]{:S(2)}) collective-permute-start(bf16[2,1536,1024]{2,1,0:T(8,128)(2,1)} %bitcast.58), channel_id=1, source_target_pairs={{0,16},{16,0},{1,17},{17,1},{2,18},{18,2},{3,19},{19,3},{4,20},{20... | collective-permute-start | bytes 18874376 | tf_op jit(solution)/shard_map/ppermute | solution.py:1344
  17.0 0.9 copy-start.7
  68.4 71.4 %copy-start.10 = (f32[128,1536]{1,0:T(8,128)S(1)}, f32[128,1536]{1,0:T(8,128)}, u32[]{:S(2)}) copy-start(f32[128,1536]{1,0:T(8,128)} %get-tuple-element.61.h1_ref) | copy-start | bytes 2359300
  170.0 67.0 %copy-start.5 = (bf16[1,2,128,1536]{3,2,1,0:T(8,128)(2,1)S(1)}, bf16[1,2,128,1536]{3,2,1,0:T(8,128)(2,1)}, u32[]{:S(2)}) copy-start(bf16[1,2,128,1536]{3,2,1,0:T(8,128)(2,1)} %param.10) | copy-start | bytes 2359300
  170.0 67.0 %copy-start.8 = (bf16[128,1536]{1,0:T(8,128)(2,1)S(1)}, bf16[128,1536]{1,0:T(8,128)(2,1)}, u32[]{:S(2)}) copy-start(bf16[128,1536]{1,0:T(8,128)(2,1)} %copy-done.7) | copy-start | bytes 1179652
  238.4 66.5 %copy-start.9 = (bf16[128,1536]{1,0:T(8,128)(2,1)}, bf16[128,1536]{1,0:T(8,128)(2,1)S(1)}, u32[]{:S(2)}) copy-start(bf16[128,1536]{1,0:T(8,128)(2,1)S(1)} %get-tuple-element.153.dout_ref) | copy-start | bytes 1179652
  304.9 31.6 %copy-start.2 = (f32[128,1536]{1,0:T(8,128)S(1)}, f32[128,1536]{1,0:T(8,128)}, u32[]{:S(2)}) copy-start(f32[128,1536]{1,0:T(8,128)} %get-tuple-element.63) | copy-start | bytes 2359300
  337.8 97.7 %copy-start.6 = (bf16[128,1536]{1,0:T(8,128)(2,1)}, bf16[128,1536]{1,0:T(8,128)(2,1)S(1)}, u32[]{:S(2)}) copy-start(bf16[128,1536]{1,0:T(8,128)(2,1)S(1)} %get-tuple-element.151.dout_ref) | copy-start | bytes 1179652
  435.5 37.8 %copy-start.3 = (f32[128,1536]{1,0:T(8,128)S(1)}, f32[128,1536]{1,0:T(8,128)}, u32[]{:S(2)}) copy-start(f32[128,1536]{1,0:T(8,128)} %get-tuple-element.65) | copy-start | bytes 2359300
  435.6 37.8 %copy-start.11 = (f32[128,1536]{1,0:T(8,128)S(1)}, f32[128,1536]{1,0:T(8,128)}, u32[]{:S(2)}) copy-start(f32[128,1536]{1,0:T(8,128)} %get-tuple-element.71.h1_ref) | copy-start | bytes 2359300
  630.3 3.5 copy-start.12
  635.0 15.4 %copy-start.1 = (s32[2,1,3]{2,1,0:T(1,128)S(1)}, s32[2,1,3]{2,1,0:T(1,128)}, u32[]{:S(2)}) copy-start(s32[2,1,3]{2,1,0:T(1,128)} %param.11) | copy-start | bytes 76
where the time goes:
time: 657 us; the launch traced here: 651 us
  Pallas kernels  619 us (94%)
  other arithmetic  20 us (3%)
    pallas_call x2, Pallas kernels, moe_backward(): pl.pallas_call(functools.partial(moe_backward_kernel, layer, experts, row...  162 us
    pallas_call x1, Pallas kernels, reduce_gradients(): pl.pallas_call(functools.partial(reduce_kernel, sub, cols), name='reduce_...  155 us
    pallas_call x2, Pallas kernels, moe_forward(): pl.pallas_call(functools.partial(moe_forward_kernel, layer, experts, rows...  138 us
    pallas_call x2, Pallas kernels, attention_forward(): pl.pallas_call(functools.partial(attention_forward_kernel, layer, rows, w...  78.6 us
    pallas_call x2, Pallas kernels, attention_backward(): pl.pallas_call(functools.partial(attention_backward_kernel, layer, rows,...  69.3 us
    pallas_call x1, Pallas kernels, finish_outputs(): pl.pallas_call(functools.partial(finish_kernel, qkv_cols), name='finish_o...  15.4 us
  transfers between devices with their start and end apart: 9, of which 0 were waited for; matrix products, arithmetic and copies ran while one was open for 2% of the time, Pallas kernels for 8%

commit v1 on v0

--- a/solution.py
+++ b/solution.py
@@ -24,6 +24,7 @@
 SIDE = 2
 LANES = 128
 HALVES = 2
+LATER_CROSS = 5
 TILE = 256
 VMEM_BYTES = 60 * 2**20
 COST = pl.CostEstimate(flops=10**11, bytes_accessed=2**24, transcendentals=0)
@@ -149,44 +150,52 @@
             src_ref=self.sums.at[q], dst_ref=self.from_high.at[q], send_sem=self.sum_send.at[q],
             recv_sem=self.high_recv.at[q], device_id=self.device(self.z - 1, self.x), device_id_type=MESH)
 
-    def own_part(self, c, h):
-        return (self.parts[self.block(c, h, self.x)].astype(F32)
-                + self.from_side[c * HALVES + h].astype(F32))
+    def own_part(self, c, h, side=True):
+        part = self.parts[self.block(c, h, self.x)].astype(F32)
+        return part + self.from_side[c * HALVES + h].astype(F32) if side else part
 
     def pass_sum(self, t, h):
         i = t - 3 - self.inner
         pl.when((i >= 0) & (i < LINE - 1))(lambda: self.pass_chunk(sum_order(self.z, i), h))
 
-    def pass_chunk(self, c, h):
+    def pass_chunk(self, c, h, side=True, send=True):
         z = self.z
         q = c * HALVES + h
-        self.side_copy(c, h).wait_recv()
+        if side:
+            self.side_copy(c, h).wait_recv()
 
         @pl.when(c > z)
         def _():
             @pl.when(z > 0)
             def _():
                 self.up_copy(c, h).wait_recv()
-                self.sums[q] = (self.own_part(c, h) + self.from_low[q].astype(F32)).astype(BF16)
+                self.sums[q] = (self.own_part(c, h, side) + self.from_low[q].astype(F32)).astype(BF16)
 
             @pl.when(z == 0)
             def _():
-                self.sums[q] = self.own_part(c, h).astype(BF16)
-
-            self.up_copy(c, h).start()
+                self.sums[q] = self.own_part(c, h, side).astype(BF16)
 
         @pl.when(c < z)
         def _():
             @pl.when(z < LINE - 1)
             def _():
                 self.down_copy(c, h).wait_recv()
-                self.sums[q] = (self.own_part(c, h) + self.from_high[q].astype(F32)).astype(BF16)
+                self.sums[q] = (self.own_part(c, h, side) + self.from_high[q].astype(F32)).astype(BF16)
 
             @pl.when(z == LINE - 1)
             def _():
-                self.sums[q] = self.own_part(c, h).astype(BF16)
-
-            self.down_copy(c, h).start()
+                self.sums[q] = self.own_part(c, h, side).astype(BF16)
+
+        if send:
+            self.send_sum(c, h)
+
+    def send_sum(self, c, h):
+        pl.when(c > self.z)(lambda: self.up_copy(c, h).start())
+        pl.when(c < self.z)(lambda: self.down_copy(c, h).start())
+
+    def wait_sent_sum(self, c, h):
+        pl.when(c > self.z)(lambda: self.up_copy(c, h).wait_send())
+        pl.when(c < self.z)(lambda: self.down_copy(c, h).wait_send())
 
     def finish_sum(self, h, out_ref):
         z = self.z
@@ -205,27 +214,40 @@
             self.down_copy(z, h).wait_recv()
             out_ref[rows] += self.from_high[q].astype(F32)
 
-    def finish_piece(self, h, out_ref):
+    def finish_piece(self, h, out_ref, side=True):
         z = self.z
         q = z * HALVES + h
-        self.side_copy(z, h).wait_recv()
+        if side:
+            self.side_copy(z, h).wait_recv()
 
         @pl.when(z == 0)
         def _():
             self.down_copy(z, h).wait_recv()
-            out_ref[h] = (self.own_part(z, h) + self.from_high[q].astype(F32)).astype(BF16)
+            out_ref[h] = (self.own_part(z, h, side) + self.from_high[q].astype(F32)).astype(BF16)
 
         @pl.when(z == LINE - 1)
         def _():
             self.up_copy(z, h).wait_recv()
-            out_ref[h] = (self.own_part(z, h) + self.from_low[q].astype(F32)).astype(BF16)
+            out_ref[h] = (self.own_part(z, h, side) + self.from_low[q].astype(F32)).astype(BF16)
 
         @pl.when((z > 0) & (z < LINE - 1))
         def _():
             self.up_copy(z, h).wait_recv()
             self.down_copy(z, h).wait_recv()
-            total = self.own_part(z, h) + self.from_low[q].astype(F32)
+            total = self.own_part(z, h, side) + self.from_low[q].astype(F32)
             out_ref[h] = (total + self.from_high[q].astype(F32)).astype(BF16)
+
+    def drain_gather(self):
+        z = self.z
+
+        def one(q, carry):
+            c, h = lax.div(q, HALVES), lax.rem(q, HALVES)
+            pl.when((z < LINE - 1) & (c <= z))(lambda: self.forward_up(c, h).wait_send())
+            pl.when((z > 0) & (c >= z))(lambda: self.forward_down(c, h).wait_send())
+            self.forward_side(c, h).wait_send()
+            return carry
+
+        lax.fori_loop(0, LINE * HALVES, one, 0)
 
     def drain(self):
         z = self.z
@@ -412,7 +434,7 @@
                         down_other, rows_hbm, kept_hbm, scaled_hbm, *refs):
     (later, refs) = (refs[:4], refs[4:]) if beside else ((), refs)
     (db_ref, keep_gu_hbm, keep_down_hbm, send_gu_hbm, send_down_hbm, grad_router_ref), refs = refs[:6], refs[6:]
-    (later_out, refs) = (refs[:3], refs[3:]) if beside else ((), refs)
+    (later_out, refs) = (refs[:4], refs[4:]) if beside else ((), refs)
     (gu_v, down_v, fwd_rows, kept, scaled, dgu, send_gu, grad_gu, send_down, grad_down,
      load_sem, store_sem), refs = refs[:12], refs[12:]
     (later_v, refs) = (refs[:8], refs[8:]) if beside else ((), refs)
@@ -546,18 +568,18 @@
 
 
 class LaterExperts:
-    def __init__(self, plane, keep_gu, keep_down, send_gu, send_down, sum_gu_hbm, sum_down_hbm, land_gu,
+    def __init__(self, plane, keep_gu, keep_down, send_gu, send_down, sum_gu_hbm, sum_down_hbm, land_gu, land_down,
                  gu_a, gu_b, down_a, down_b, load_sem, core_sem, send_sem, recv_sem):
         self.parts = []
         for keep, sent, out, land, a, b, count in (
             (keep_gu, send_gu, sum_gu_hbm, land_gu, gu_a, gu_b, 4),
-            (keep_down, send_down, sum_down_hbm, None, down_a, down_b, 2),
+            (keep_down, send_down, sum_down_hbm, land_down, down_a, down_b, 2),
         ):
             size = a.shape[0] // count
             for n in range(count):
                 at, k = pl.ds(n * size, size), len(self.parts)
                 shard_copy = land_copy = None
-                if land is not None:
+                if k < LATER_CROSS:
                     shard_copy = pltpu.make_async_remote_copy(
                         src_ref=a.at[at], dst_ref=land.at[at], send_sem=send_sem.at[k], recv_sem=recv_sem.at[k],
                         device_id=plane.other_shard(), device_id_type=MESH)
@@ -612,11 +634,11 @@
     down_shape = jax.ShapeDtypeStruct((FF, width), BF16)
     later_out, later_scratch = (), []
     if later:
-        later_out = (gu_shape, down_shape, gu_shape)
+        later_out = (gu_shape, down_shape) * 2
         later_scratch = [
             expert_gu, expert_gu, expert_down, expert_down,
             pltpu.SemaphoreType.DMA((3, 6)), pltpu.SemaphoreType.DMA((2, 6)),
-            pltpu.SemaphoreType.DMA((4,)), pltpu.SemaphoreType.DMA((4,)),
+            pltpu.SemaphoreType.DMA((LATER_CROSS,)), pltpu.SemaphoreType.DMA((LATER_CROSS,)),
         ]
     return pl.pallas_call(
         functools.partial(moe_backward_kernel, layer, experts, rows, width, bool(later)),
@@ -662,41 +684,129 @@
     return jnp.where(z < 2, low, high)
 
 
-def reduce_kernel(sub, cols, g1, g0, t1, t0, gu_hbm, down_hbm, sent_gu_hbm, sent_down_hbm, gu1_hbm, down1_hbm, edge,
+def remote_copy(src, dst, send_sem, recv_sem, device):
+    return pltpu.make_async_remote_copy(
+        src_ref=src, dst_ref=dst, send_sem=send_sem, recv_sem=recv_sem, device_id=device, device_id_type=MESH)
+
+
+class GradientSum:
+    def __init__(self, plane, h, cols, grad, small, core_got, small_own, small_got, load_sem, core_sem, small_sem):
+        self.plane, self.h, self.cols = plane, h, cols
+        self.core_got, self.small_own, self.small_got = core_got, small_own, small_got
+        core, shard = plane.sec, plane.shard
+        places = [(c, side) for c in range(LINE) for side in range(SIDE)]
+        self.loads = [
+            pltpu.make_async_copy(
+                grad.at[n, core], plane.parts.at[plane.block(c, h, side), pl.ds(0, cols)], load_sem.at[n])
+            for n, (c, side) in enumerate(places)
+        ]
+        self.loads.append(pltpu.make_async_copy(small.at[shard, :, core], small_own, load_sem.at[len(places)]))
+        self.copies = [
+            remote_copy(grad.at[:, 1 - core], core_got, core_sem.at[0], core_sem.at[1], plane.other_core())
+        ]
+        for n, (there, half, device) in enumerate((
+            (shard, 1 - core, plane.other_core()),
+            (1 - shard, core, plane.other_shard()),
+            (1 - shard, 1 - core, self.diagonal(plane)),
+        )):
+            self.copies.append(remote_copy(
+                small.at[there, :, half], small_got.at[n], small_sem.at[0, n], small_sem.at[1, n], device))
+
+    @staticmethod
+    def diagonal(plane):
+        return (1 - plane.sec, plane.owner, 1 - plane.shard)
+
+    def start_loads(self):
+        for load in self.loads:
+            load.start()
+
+    def start_copies(self):
+        for copy in self.copies:
+            copy.start()
+
+    def wait_terms(self):
+        for load in self.loads:
+            load.wait()
+        for copy in self.copies:
+            copy.wait_recv()
+
+    def prepare(self, first, last):
+        plane, h, cols = self.plane, self.h, self.cols
+
+        def one(k, carry):
+            c = jnp.where(k < 2 * (LINE - 1), far_order(plane.z, lax.div(k, 2)), plane.z)
+            side = jnp.where(lax.rem(k, 2) == 0, 1 - plane.x, plane.x)
+            n = c * SIDE + side
+            at = plane.block(c, h, side)
+            plane.parts[at, pl.ds(0, cols)] = (
+                plane.parts[at, pl.ds(0, cols)].astype(F32) + self.core_got[n].astype(F32)).astype(BF16)
+            total = self.small_own[n].astype(F32)
+            for other in range(3):
+                total = total + self.small_got[other, n].astype(F32)
+            plane.parts[at, pl.ds(cols, LANES)] = total.astype(BF16)
+            pl.when(side != plane.x)(lambda: plane.side_copy(c, h).start())
+            return carry
+
+        lax.fori_loop(first, last, one, 0)
+
+    def pass_on(self, i):
+        self.plane.pass_chunk(far_order(self.plane.z, i), self.h)
+
+    def hand_over(self, out_ref):
+        plane, h = self.plane, self.h
+        second, third = far_order(plane.z, 1), far_order(plane.z, 2)
+        plane.pass_chunk(second, h, send=False)
+        out_ref[0] = plane.sums[second * HALVES + h]
+        for n, c in ((1, third), (2, plane.z)):
+            plane.side_copy(c, h).wait_recv()
+            out_ref[n] = plane.own_part(c, h).astype(BF16)
+
+    def drain(self, chunks=LINE - 1):
+        plane, h = self.plane, self.h
+        for copy in self.copies:
+            copy.wait_send()
+
+        def one(c, carry):
+            plane.side_copy(c, h).wait_send()
+            return carry
+
+        lax.fori_loop(0, LINE, one, 0)
+        for i in range(chunks):
+            plane.wait_sent_sum(far_order(plane.z, i), h)
+
+
+def sum_scratch(places, sub, cols):
+    plane = plane_scratch(HALVES * sub, cols + LANES, cols + LANES)
+    own = [
+        pltpu.VMEM((places, sub, cols), BF16),
+        pltpu.VMEM((places, sub, LANES), BF16),
+        pltpu.VMEM((3, places, sub, LANES), BF16),
+        pltpu.SemaphoreType.DMA((places + 1,)),
+        pltpu.SemaphoreType.DMA((2,)),
+        pltpu.SemaphoreType.DMA((2, 3)),
+    ]
+    return own, plane
+
+
+def reduce_kernel(sub, cols, g0, t0, shares1, gu_hbm, down_hbm, sent_gu_hbm, sent_down_hbm, gu1_hbm, down1_hbm, tail1_hbm, edge,
                   sum_hbm, own_gu_hbm, own_down_hbm, got_gu_hbm, got_down_hbm, own_down1_hbm, got_gu1_hbm,
                   got_down1_hbm, got_edge,
-                  core_got, small_own, small_got, result, own_gu, core_gu, other_gu, own_down, core_down, other_down,
-                  own_down1, other_down1,
-                  load_sem, expert_load_sem, expert_core_sem, edge_sem, core_sem, small_sem, move_sem, expert_sem, core_expert_sem, store_sem,
-                  *plane_refs):
+                  core_got, small_own, small_got, load_sem, core_sem, small_sem,
+                  result, own_gu, core_gu, other_gu, own_down, core_down, other_down,
+                  share_sem, expert_load_sem, expert_core_sem, edge_sem, move_sem, expert_sem,
+                  core_expert_sem, store_sem, *plane_refs):
     plane = Plane(HALVES * sub, plane_refs)
-    gathered, parts = plane.gathered, plane.parts
-    core, shard, z, x = plane.sec, plane.shard, plane.z, plane.x
-    wide = cols + LANES
-    grads, smalls = (g1, g0), (t1, t0)
-    diagonal = (1 - core, plane.owner, 1 - shard)
-    places = [(c, side) for c in range(LINE) for side in range(SIDE)]
-
-    def remote(src, dst, send_sem, recv_sem, device):
-        return pltpu.make_async_remote_copy(
-            src_ref=src, dst_ref=dst, send_sem=send_sem, recv_sem=recv_sem,
-            device_id=device, device_id_type=MESH)
-
-    loads = []
-    for h in range(2):
-        for n, (c, side) in enumerate(places):
-            loads.append(pltpu.make_async_copy(
-                grads[h].at[n, core], parts.at[plane.block(c, h, side), pl.ds(0, cols)], load_sem.at[h, n]))
-        loads.append(pltpu.make_async_copy(
-            smalls[h].at[shard, :, core], small_own.at[h], load_sem.at[h, len(places)]))
+    gathered = plane.gathered
+    core, z, x = plane.sec, plane.z, plane.x
+    remote = remote_copy
+    sums = GradientSum(plane, 1, cols, g0, t0, core_got, small_own, small_got, load_sem, core_sem, small_sem)
     pieces, expert_loads = [], []
-    for layer, hbm, sent, own, there, other, own_hbm, got_hbm, count in (
-        (1, down1_hbm, None, own_down1, None, other_down1, own_down1_hbm, got_down1_hbm, 2),
-        (0, gu_hbm, sent_gu_hbm, own_gu, core_gu, other_gu, own_gu_hbm, got_gu_hbm, 4),
-        (0, down_hbm, sent_down_hbm, own_down, core_down, other_down, own_down_hbm, got_down_hbm, 2),
+    for layer, hbm, sent, own, there, other, own_hbm, got_hbm, count, first in (
+        (0, gu_hbm, sent_gu_hbm, own_gu, core_gu, other_gu, own_gu_hbm, got_gu_hbm, 4, 0),
+        (0, down_hbm, sent_down_hbm, own_down, core_down, other_down, own_down_hbm, got_down_hbm, 2, 0),
     ):
         size = own.shape[0] // count
-        for n in range(count):
+        for n in range(first, count):
             at, k = pl.ds(n * size, size), len(pieces)
             pieces.append((layer, own, there, other, own_hbm, got_hbm, at))
             expert_loads.append((
@@ -705,32 +815,54 @@
                     sent.at[at], there.at[at], expert_core_sem.at[0, k], expert_core_sem.at[1, k],
                     plane.other_core()),
             ))
-    for load in [load for load, _ in expert_loads[:2]] + loads + [load for load, _ in expert_loads[2:]]:
+    count = LINE * SIDE * HALVES
+    split = tail1_hbm.shape[0]
+    low, high = pl.ds(0, split), pl.ds(split, split)
+    ready_copies = [
+        pltpu.make_async_copy(down1_hbm.at[low], own_down1_hbm.at[low], store_sem.at[count + 6]),
+        pltpu.make_async_copy(tail1_hbm, own_down1_hbm.at[high], store_sem.at[count + 7]),
+    ]
+    second, third = far_order(z, 1), far_order(z, 2)
+    load_shares = [
+        pltpu.make_async_copy(shares1.at[0], plane.sums.at[second * HALVES], share_sem.at[0]),
+        pltpu.make_async_copy(shares1.at[1], plane.parts.at[plane.block(third, 0, x)], share_sem.at[1]),
+        pltpu.make_async_copy(shares1.at[2], plane.parts.at[plane.block(z, 0, x)], share_sem.at[2]),
+    ]
+    for load in load_shares:
         load.start()
-    plane.barrier(plane.other_core(), plane.other_shard(), diagonal)
-    cores = [
-        remote(grads[h].at[:, 1 - core], core_got.at[h], core_sem.at[0, h], core_sem.at[1, h], plane.other_core())
-        for h in range(2)
-    ]
-    small = []
-    for h in range(2):
-        for n, (there, half, device) in enumerate((
-            (shard, 1 - core, plane.other_core()),
-            (1 - shard, core, plane.other_shard()),
-            (1 - shard, 1 - core, diagonal),
-        )):
-            small.append(remote(
-                smalls[h].at[there, :, half], small_got.at[h, n], small_sem.at[0, h, n], small_sem.at[1, h, n],
-                device))
-    for copy in cores[:1] + small + cores[1:]:
-        copy.start()
+    expert_loads[0][0].start()
+    sums.start_loads()
+    for load, _ in expert_loads[1:]:
+        load.start()
+    plane.barrier(plane.other_core(), plane.other_shard(), sums.diagonal(plane))
+    sums.start_copies()
     for _, copy in expert_loads:
         if copy is not None:
             copy.start()
-    edges = remote(edge, got_edge, edge_sem.at[0], edge_sem.at[1], plane.other_core())
-    edges.start()
-    gu1_copy = remote(gu1_hbm, got_gu1_hbm, edge_sem.at[2], edge_sem.at[3], plane.other_core())
-    pl.when(core == 0)(lambda: gu1_copy.start())
+
+    def move(h):
+        return remote(
+            result.at[h], gathered.at[plane.block(z, core, x)], move_sem.at[0], move_sem.at[1], plane.other_core())
+
+    def send_block(h):
+        pl.when(z < LINE - 1)(lambda: plane.forward_up(z, h).start())
+        pl.when(z > 0)(lambda: plane.forward_down(z, h).start())
+        plane.forward_side(z, h).start()
+
+    def begin_gather(h):
+        own_layer = core == 1 - h
+        pl.when(jnp.logical_not(own_layer))(lambda: move(h).start())
+
+        @pl.when(own_layer)
+        def _():
+            gathered[plane.block(z, core, x)] = result[h]
+            send_block(core)
+            arrived = remote(
+                result.at[h], gathered.at[plane.block(z, 1 - core, x)], move_sem.at[0], move_sem.at[1],
+                plane.other_core())
+            arrived.wait_recv()
+            send_block(1 - core)
+
     exchange = []
 
     def send_piece():
@@ -745,60 +877,21 @@
             remote(own.at[at], other.at[at], expert_sem.at[0, n], expert_sem.at[1, n], plane.other_shard()))
         exchange[-1].start()
 
-    def prepare(h):
-        cores[h].wait_recv()
-        for copy in small[3 * h : 3 * h + 3]:
-            copy.wait_recv()
-
-        def one(k, carry):
-            c = jnp.where(k < 2 * (LINE - 1), far_order(z, lax.div(k, 2)), z)
-            side = jnp.where(lax.rem(k, 2) == 0, 1 - x, x)
-            n = c * SIDE + side
-            at = plane.block(c, h, side)
-            parts[at, pl.ds(0, cols)] = (
-                parts[at, pl.ds(0, cols)].astype(F32) + core_got[h, n].astype(F32)).astype(BF16)
-            total = small_own[h, n].astype(F32)
-            for other in range(3):
-                total = total + small_got[h, other, n].astype(F32)
-            parts[at, pl.ds(cols, LANES)] = total.astype(BF16)
-            pl.when(side != x)(lambda: plane.side_copy(c, h).start())
-            return carry
-
-        lax.fori_loop(0, LINE * SIDE, one, 0)
-
     send_piece()
-    send_piece()
-    for load in loads:
+    for load in load_shares:
         load.wait()
-    prepare(0)
-    send_piece()
-
-    def pass_piece(i, h):
-        plane.pass_chunk(far_order(z, i), h)
-
-    def move(h):
-        return remote(
-            result.at[h], gathered.at[plane.block(z, core, x)], move_sem.at[0], move_sem.at[1], plane.other_core())
-
-    def send_block(h):
-        pl.when(z < LINE - 1)(lambda: plane.forward_up(z, h).start())
-        pl.when(z > 0)(lambda: plane.forward_down(z, h).start())
-        plane.forward_side(z, h).start()
-
-    def finish(h):
-        plane.finish_piece(h, result)
-        own_layer = core == 1 - h
-        pl.when(jnp.logical_not(own_layer))(lambda: move(h).start())
-
-        @pl.when(own_layer)
-        def _():
-            gathered[plane.block(z, core, x)] = result[h]
-            send_block(core)
-            arrived = remote(
-                result.at[h], gathered.at[plane.block(z, 1 - core, x)], move_sem.at[0], move_sem.at[1],
-                plane.other_core())
-            arrived.wait_recv()
-            send_block(1 - core)
+    plane.send_sum(second, 0)
+    edges = remote(edge, got_edge, edge_sem.at[0], edge_sem.at[1], plane.other_core())
+    edges.start()
+    later_copies = [
+        remote(gu1_hbm, got_gu1_hbm, edge_sem.at[2], edge_sem.at[3], plane.other_core()),
+        remote(down1_hbm.at[low], got_down1_hbm.at[low], edge_sem.at[4], edge_sem.at[5], plane.other_core()),
+        remote(tail1_hbm, got_down1_hbm.at[high], edge_sem.at[6], edge_sem.at[7], plane.other_core()),
+    ]
+    for copy in later_copies:
+        pl.when(core == 0)(lambda copy=copy: copy.start())
+    for copy in ready_copies:
+        copy.start()
 
     def out_copy(c, h, side):
         at = pl.multiple_of(((c * SIDE + side) * HALVES + h) * sub, sub)
@@ -815,8 +908,6 @@
             out_copy(c, h, x).start()
             out_copy(c, h, 1 - x).start()
 
-    count = LINE * SIDE * HALVES
-
     def to_core(n):
         layer, own, there, other, own_hbm, got_hbm, at = pieces[n]
         return remote(
@@ -833,21 +924,30 @@
         pl.when(core != layer)(lambda: to_core(n).start())
         keep(n).start()
 
-    pass_piece(0, 0)
-    prepare(1)
+    sums.wait_terms()
+    sums.prepare(0, LINE)
+    plane.pass_chunk(third, 0, side=False)
     send_piece()
-    pass_piece(1, 0)
+    sums.prepare(LINE, LINE * SIDE)
+    sums.pass_on(0)
     send_piece()
-    pass_piece(2, 0)
-    finish(0)
+    plane.finish_piece(0, result, side=False)
+    begin_gather(0)
+    for i in range(1, LINE - 1):
+        sums.pass_on(i)
+        send_piece()
+        pl.when(core == 1)(lambda i=i: gather(i))
     while len(exchange) < len(pieces):
         send_piece()
-    for i in range(LINE - 1):
-        pass_piece(i, 1)
-        pl.when(core == 1)(lambda i=i: gather(i + 1))
-        expert_piece(i)
-    finish(1)
-    pl.when(core == 1)(lambda: gather(LINE))
+    plane.finish_piece(1, result)
+    begin_gather(1)
+    for n in range(2):
+        expert_piece(n)
+
+    @pl.when(core == 1)
+    def _():
+        gather(LINE - 1)
+        gather(LINE)
 
     @pl.when(core == 0)
     def _():
@@ -857,11 +957,12 @@
 
         lax.fori_loop(1, LINE + 1, one, 0)
 
-    for n in range(LINE - 1, len(pieces)):
+    for n in range(2, len(pieces)):
         expert_piece(n)
-    plane.drain()
-    for copy in cores + small:
-        copy.wait_send()
+    sums.drain()
+    plane.wait_sent_sum(second, 0)
+    plane.wait_sent_sum(third, 0)
+    plane.drain_gather()
     move(0).wait_send()
 
     def stored(k, carry):
@@ -874,17 +975,21 @@
         pl.when(core != pieces[n][0])(lambda n=n: to_core(n).wait_send())
         pl.when(core == pieces[n][0])(lambda n=n: to_core(n).wait_recv())
     edges.wait()
-    pl.when(core == 0)(lambda: gu1_copy.wait_send())
-    pl.when(core == 1)(lambda: gu1_copy.wait_recv())
-
-
-def reduce_gradients(g1, g0, t1, t0, experts0, gu1, down1, edge, collective_id):
-    places, halves, sub, cols = g1.shape
+    for copy in ready_copies:
+        copy.wait()
+    for copy in later_copies:
+        pl.when(core == 0)(lambda copy=copy: copy.wait_send())
+        pl.when(core == 1)(lambda copy=copy: copy.wait_recv())
+
+
+def reduce_gradients(g0, t0, shares1, experts0, gu1, down1, tail1, edge, collective_id):
+    places, halves, sub, cols = g0.shape
     grad_gu, grad_down = experts0[:2]
     any_spec = pl.BlockSpec(memory_space=pl.ANY)
     wide = cols + LANES
     gu, down = jax.ShapeDtypeStruct(grad_gu.shape, BF16), jax.ShapeDtypeStruct(grad_down.shape, BF16)
     gu_v, down_v = pltpu.VMEM(grad_gu.shape, BF16), pltpu.VMEM(grad_down.shape, BF16)
+    own, plane = sum_scratch(places, sub, cols)
     return pl.pallas_call(
         functools.partial(reduce_kernel, sub, cols),
         name="reduce_gradients",
@@ -894,26 +999,21 @@
         ),
         in_specs=[any_spec] * 11,
         out_specs=(any_spec,) * 9,
-        scratch_shapes=[
-            pltpu.VMEM((2, places, sub, cols), BF16),
-            pltpu.VMEM((2, places, sub, LANES), BF16),
-            pltpu.VMEM((2, 3, places, sub, LANES), BF16),
+        scratch_shapes=own + [
             pltpu.VMEM((2, sub, wide), BF16),
-            gu_v, gu_v, gu_v, down_v, down_v, down_v, down_v, down_v,
-            pltpu.SemaphoreType.DMA((2, places + 1)),
+            gu_v, gu_v, gu_v, down_v, down_v, down_v,
+            pltpu.SemaphoreType.DMA((3,)),
+            pltpu.SemaphoreType.DMA((6,)),
+            pltpu.SemaphoreType.DMA((2, 6)),
             pltpu.SemaphoreType.DMA((8,)),
-            pltpu.SemaphoreType.DMA((2, 8)),
-            pltpu.SemaphoreType.DMA((4,)),
-            pltpu.SemaphoreType.DMA((2, 2)),
-            pltpu.SemaphoreType.DMA((2, 2, 3)),
             pltpu.SemaphoreType.DMA((2,)),
-            pltpu.SemaphoreType.DMA((2, 8)),
-            pltpu.SemaphoreType.DMA((2, 8)),
+            pltpu.SemaphoreType.DMA((2, 6)),
+            pltpu.SemaphoreType.DMA((2, 6)),
             pltpu.SemaphoreType.DMA((places * halves + 8,)),
-        ] + plane_scratch(halves * sub, wide, wide),
+        ] + plane,
         compiler_params=pltpu.CompilerParams(
             collective_id=collective_id, has_side_effects=True, vmem_limit_bytes=VMEM_BYTES),
-    )(g1, g0, t1, t0, *experts0, gu1, down1, edge)
+    )(g0, t0, shares1, *experts0, gu1, down1, tail1, edge)
 
 
 def finish_kernel(qkv_cols, attn, gu_own, gu_got, gu_one, gu_moved, down_own, down_got, down_one, down_moved,
@@ -1088,14 +1188,14 @@
     a = (h * r1 * gains_ref[pl.ds(0, 1), :]).astype(BF16)
     for j in range(2):
         a_parts[j] = a[:, j * half : (j + 1) * half]
+    a_half[span(me)] = a_parts[me]
+    for load in loads[:-1]:
+        load.wait()
+    part_send[span(me)] = nn(a_parts[me], wq_v[peer]).astype(BF16)
     if turn:
         pl.when(pair.sec == 0)(lambda: pl.semaphore_wait(turn[0], 1))
     send_a = pair.send(a_parts.at[peer], a_half.at[span(me)], send_sem.at[0], recv_sem.at[0])
     send_a.start()
-    a_half[span(me)] = a_parts[me]
-    for load in loads[:-1]:
-        load.wait()
-    part_send[span(me)] = nn(a_parts[me], wq_v[peer]).astype(BF16)
     send_own = pair.send(part_send.at[span(me)], got_part.at[span(me)], send_sem.at[1], recv_sem.at[1])
     send_own.start()
     send_a.wait_recv()
@@ -1186,17 +1286,38 @@
     )(h, allowed, gains, router, mask, *weights)
 
 
+ATTENTION_BACKWARD_REFS = 20
+
+
 def attention_backward_kernel(layer, rows, width, experts, router_grad_ref, db_ref, dout_ref, h1_ref, h_ref, gains_ref, a_ref, qkv_ref,
-                              p_ref, o_ref, wq, wq_other, wo, wo_other, dh_ref, columns_ref, grad_hbm,
-                              wq_v, wo_v, d_all, do, dqkv, got_dqkv, da_send, got_da, dh1_v, grad_q, grad_o,
-                              gain_grads_ref, columns_v, load_sem, store_sem, send_sem, recv_sem):
+                              p_ref, o_ref, wq, wq_other, wo, wo_other, *refs):
+    beside = len(refs) > ATTENTION_BACKWARD_REFS
+    (later, refs) = (refs[:3], refs[3:]) if beside else ((), refs)
+    (dh_ref, columns_ref, grad_hbm), refs = refs[:3], refs[3:]
+    (later_out, refs) = (refs[:2], refs[2:]) if beside else ((), refs)
+    (wq_v, wo_v, d_all, do, dqkv, got_dqkv, da_send, got_da, dh1_v, grad_q, grad_o,
+     gain_grads_ref, columns_v, load_sem, store_sem, send_sem, recv_sem), refs = refs[:17], refs[17:]
     pair = Pair()
     me, peer = pair.me, pair.peer
     half = width // 2
     qkv_cols = dqkv.shape[1]
     pair_cols = qkv_cols // PAIRS
     loads = load_attention(layer, pair.sec, wq, wq_other, wo, wo_other, wq_v, wo_v, load_sem)
-    pair.barrier()
+    if beside:
+        sub, cols_all = later[0].shape[2:]
+        plane = Plane(HALVES * sub, (None,) + tuple(refs[10:]))
+        sums = GradientSum(plane, 0, cols_all, *later[:2], *refs[:6])
+        tail_own, tail_got, tail_load, tail_sem = refs[6:10]
+        tail_rows = tail_own.shape[0]
+        load_tail = pltpu.make_async_copy(later[2].at[pl.ds(tail_rows, tail_rows)], tail_own, tail_load)
+        load_tail.start()
+        sums.start_loads()
+        plane.barrier(plane.other_core(), plane.other_shard(), sums.diagonal(plane))
+        sums.start_copies()
+        load_tail.wait()
+        tail_copy = pair.send(tail_own, tail_got, tail_sem.at[0], tail_sem.at[1])
+    else:
+        pair.barrier()
 
     def span(who):
         return pl.ds(pl.multiple_of(who * rows, rows), rows)
@@ -1218,12 +1339,19 @@
     lane = lax.broadcasted_iota(jnp.int32, router_terms.shape, 1)
     router_terms = router_terms + pltpu.roll(router_terms, LANES // 2, 1)
     columns_v[...] = jnp.where(lane < experts, router_terms, 0.0)
+    if beside:
+        sums.wait_terms()
+        sums.prepare(0, LINE)
     for load in loads:
         load.wait()
     do[span(me)] = nt(d_all[span(me)], wo_v[...]).astype(BF16)
     send_d.wait_recv()
     do[span(peer)] = nt(d_all[span(peer)], wo_v[...]).astype(BF16)
     sends = [send_d]
+    if beside:
+        tail_copy.start()
+        pl.when(plane.inner == 0)(lambda: sums.pass_on(0))
+        sums.prepare(LINE, LINE * SIDE)
     for i in range(PAIRS):
         cols = pl.ds(i * pair_cols, pair_cols)
         for n in range(KV_IN_PAIR):
@@ -1245,6 +1373,8 @@
         send = pair.send(dqkv.at[:, cols], got_dqkv.at[:, cols], send_sem.at[1 + i], recv_sem.at[1 + i])
         send.start()
         sends.append(send)
+        if beside and i == 0:
+            pl.when(plane.inner == 1)(lambda: sums.pass_on(0))
     da = nt(dqkv[...], wq_v[me])
     grad_q[me] = tn(a_ref[...], dqkv[...]).astype(BF16)
     grad_o[...] = tn(o_ref[...], d_all[...]).astype(BF16)
@@ -1285,18 +1415,39 @@
     columns_ref[...] = columns.astype(BF16)
     for cols, scaled, normed in halves:
         dh_ref[:, cols] = dh1_v[:, cols] + r1 * (scaled - normed * (total / width))
+    if beside:
+        sums.hand_over(later_out[0])
+        tail_copy.wait()
+        later_out[1][...] = (tail_own[...].astype(F32) + tail_got[...].astype(F32)).astype(BF16)
+        sums.drain(1)
     for send in sends + [send_da]:
         send.wait_send()
     for store in stores:
         store.wait()
 
 
-def attention_backward(layer, experts, router_grad, db, dout, h1, h, gains, a_half, qkv, p, o, weights, collective_id):
+def attention_backward(layer, experts, router_grad, db, dout, h1, h, gains, a_half, qkv, p, o, weights, later,
+                       collective_id):
     rows, width = db.shape
     half, group = width // 2, 2 * rows
     cols = (QUERY_WIDTH + 2 * KV_WIDTH) // 2
     any_spec = pl.BlockSpec(memory_space=pl.ANY)
     vmem = pl.BlockSpec(memory_space=pltpu.VMEM)
+    later_out, later_scratch = (), []
+    if later:
+        places, _, sub, later_cols = later[0].shape
+        own, plane = sum_scratch(places, sub, later_cols)
+        tail_shape = (later[2].shape[0] // 2, later[2].shape[1])
+        later_out = (
+            jax.ShapeDtypeStruct((3, sub, later_cols + LANES), BF16),
+            jax.ShapeDtypeStruct(tail_shape, BF16),
+        )
+        later_scratch = own + [
+            pltpu.VMEM(tail_shape, BF16),
+            pltpu.VMEM(tail_shape, BF16),
+            pltpu.SemaphoreType.DMA,
+            pltpu.SemaphoreType.DMA((2,)),
+        ] + plane[1:]
     return pl.pallas_call(
         functools.partial(attention_backward_kernel, layer, rows, width, experts),
         name="attention_backward",
@@ -1304,9 +1455,9 @@
             jax.ShapeDtypeStruct((rows, width), F32),
             jax.ShapeDtypeStruct((width, LANES), BF16),
             jax.ShapeDtypeStruct((half, QUERY_WIDTH + 2 * KV_WIDTH + width), BF16),
-        ),
-        in_specs=[vmem] * 10 + [any_spec] * 4,
-        out_specs=(vmem, vmem, any_spec),
+        ) + later_out,
+        in_specs=[vmem] * 10 + [any_spec] * (4 + len(later)),
+        out_specs=(vmem, vmem, any_spec) + (vmem,) * len(later_out),
         scratch_shapes=[
             pltpu.VMEM((2, half, cols), BF16),
             pltpu.VMEM((QUERY_WIDTH // 2, width), BF16),
@@ -1325,11 +1476,11 @@
             pltpu.SemaphoreType.DMA((LOADS,)),
             pltpu.SemaphoreType.DMA((2 + PAIRS,)),
             pltpu.SemaphoreType.DMA((2 + PAIRS,)),
-        ],
+        ] + later_scratch,
         cost_estimate=COST,
         compiler_params=pltpu.CompilerParams(
             collective_id=collective_id, has_side_effects=True, vmem_limit_bytes=VMEM_BYTES),
-    )(router_grad, db, dout, h1, h, gains, a_half, qkv, p, o, *weights)
+    )(router_grad, db, dout, h1, h, gains, a_half, qkv, p, o, *weights, *later)
 
 
 def dot(a, b, dims):
@@ -1653,7 +1804,7 @@
         moe, *expert_state = moe_forward(layer, block, expert_weights, experts, 3 + layer)
         return h1 + moe, (h, h1, moe, attn_state, expert_state)
 
-    def backward(layer, dout, state, later):
+    def backward(layer, dout, state, later, later_attn):
         h, h1, moe, attn_state, expert_state = state
         outer = jnp.sum(dout.astype(F32) * moe, axis=1, keepdims=True)
         block = with_lanes(dout, split_terms(outer))
@@ -1665,25 +1816,25 @@
             layer, block, own_router, expert_weights, expert_state, later, experts, 5 + layer
         )
         db, keep_gu, keep_down, send_gu, send_down, grad_router = results[:6]
-        dh, columns, grad_attn = attention_backward(
+        dh, columns, grad_attn, *piece = attention_backward(
             layer, experts, grad_router, db, dout, h1, h, gains[layer], *attn_state, attn_weights,
-            7 + layer,
+            later_attn + tuple(results[7:8]) if later else (), 7 + layer,
         )
         places = LINE * SIDE
         sub = half // (2 * places)
         grad_attn = grad_attn.reshape(places, 2, sub, attn_cols)
         columns = columns.reshape(2, places, 2, sub, LANES)
-        return dh, grad_attn, columns, (keep_gu, keep_down, send_gu, send_down), results[6:8]
+        return dh, grad_attn, columns, (keep_gu, keep_down, send_gu, send_down), results[6:8], piece
 
     out0, state0 = forward(0, x_in)
     final, state1 = forward(1, out0.astype(BF16))
-    dh_one, attn1, columns1, experts1, _ = backward(1, dy, state1, ())
-    dh_zero, attn0, columns0, experts0, sums1 = backward(
-        0, dh_one.astype(BF16), state0, experts1
+    dh_one, attn1, columns1, experts1, *_ = backward(1, dy, state1, (), ())
+    dh_zero, attn0, columns0, experts0, sums1, (shares1, tail1) = backward(
+        0, dh_one.astype(BF16), state0, experts1, (attn1, columns1)
     )
     send = jnp.where(sec == 0, final, dh_zero)
     attn, gu_own, down_own, gu_got, down_got, down_one, gu_moved, down_moved, got = reduce_gradients(
-        attn1, attn0, columns1, columns0, experts0, *sums1, send, 9
+        attn0, columns0, shares1, experts0, *sums1, tail1, send, 9
     )
     grad_qkv, grad_out, grad_gu, grad_down = finish_outputs(
         attn,

time: 657 us -> 651 us (level)
  Pallas kernels: 619 us -> 612 us
    pallas_call x1, Pallas kernels: 155 us -> 120 us  [reduce_gradients(): pl.pallas_call(functools.partial(reduce_kernel, sub, cols), name='reduce_...]
    pallas_call x2, Pallas kernels: 69.3 us -> 93.3 us  [attention_backward(): pl.pallas_call(functools.partial(attention_backward_kernel, layer, rows,...]
where the time goes in v1:
time: 651 us; the launch traced here: 644 us
  Pallas kernels  612 us (94%)
  other arithmetic  20 us (3%)
    pallas_call x2, Pallas kernels, moe_backward(): pl.pallas_call(functools.partial(moe_backward_kernel, layer, experts, row...  163 us
    pallas_call x2, Pallas kernels, moe_forward(): pl.pallas_call(functools.partial(moe_forward_kernel, layer, experts, rows...  138 us
    pallas_call x1, Pallas kernels, reduce_gradients(): pl.pallas_call(functools.partial(reduce_kernel, sub, cols), name='reduce_...  120 us
    pallas_call x2, Pallas kernels, attention_backward(): pl.pallas_call(functools.partial(attention_backward_kernel, layer, rows,...  93.3 us
    pallas_call x2, Pallas kernels, attention_forward(): pl.pallas_call(functools.partial(attention_forward_kernel, layer, rows, w...  81.5 us
    pallas_call x1, Pallas kernels, finish_outputs(): pl.pallas_call(functools.partial(finish_kernel, qkv_cols), name='finish_o...  15.4 us
  transfers between devices with their start and end apart: 9, of which 0 were waited for; matrix products, arithmetic and copies ran while one was open for 2% of the time, Pallas kernels for 8%

profile of v1, /device:TPU:0, one launch (start us, length us, event | category | flops | bytes accessed | tf_op | source)
XLA Modules:
  0.0 644.2 jit_solution(13907832888722448706)
XLA Ops:
  0.7 0.9 pad_maximum_fusion
  1.5 2.5 collective-permute-start.3
  4.0 0.7 collective-permute-start.2
  4.7 0.7 dynamic-slice_bitcast_fusion.1
  6.2 0.8 fusion.11.allowed_ref
  7.0 1.0 dynamic-slice_bitcast_fusion
  8.3 0.7 bitcast_select_fusion.3
  9.6 0.7 and_select_fusion
  11.1 0.9 broadcast_select_fusion.1
  12.0 0.9 broadcast_select_fusion.2
  14.8 0.8 fusion.8.router_ref
  16.2 0.8 fusion.9.router_ref
  17.0 0.9 bitcast_select_fusion.h_ref
  17.9 51.7 %attention_forward.2 = (bf16[128,1664]{1,0:T(8,128)(2,1)}, f32[128,1536]{1,0:T(8,128)}, bf16[256,768]{1,0:T(8,128)(2,1)}, bf16[256,1280]{1,0:T(8,128)(2,1)}, bf1...) custom-call(bf16[128,1536]{1,0:T(8,128)(2,1)} %bitcast_select_fusion.h_ref, f32[256,256]{1,0:T(8,128)} %fusion.11.allowed_ref, ...), custom_call_target="tpu_custom_call" | custom-call | flops 99999997952 | bytes 16777216 | tf_op jit(solution)/shard_map/attention_forward/pallas_call | solution.py:1257
  69.6 71.3 %moe_forward.2 = (f32[128,1536]{1,0:T(8,128)}, bf16[1024,1664]{1,0:T(8,128)(2,1)}, bf16[1024,2048]{1,0:T(8,128)(2,1)}, bf16[1024,1024]{1,0:T(8,128)(2,1)}) custom-call(bf16[128,1664]{1,0:T(8,128)(2,1)} %get-tuple-element.64.block_ref, bf16[2,1536,1024]{2,1,0:T(8,128)(2,1)} %bitcast.57, bf16[2,1536,1024]{2,1,0:T(8,128)(2,1)} %collective-permute-done.7.gu_other, ...), custom_call_target="tpu_custom_call" | custom-call | flops 99999997952 | bytes 16777216 | tf_op jit(solution)/shard_map/moe_forward/pallas_call | solution.py:408
  141.0 2.0 add_convert_fusion.h_ref
  143.0 29.8 %attention_forward.3 = (bf16[128,1664]{1,0:T(8,128)(2,1)}, f32[128,1536]{1,0:T(8,128)}, bf16[256,768]{1,0:T(8,128)(2,1)}, bf16[256,1280]{1,0:T(8,128)(2,1)}, bf1...) custom-call(bf16[128,1536]{1,0:T(8,128)(2,1)} %add_convert_fusion.h_ref, f32[256,256]{1,0:T(8,128)} %fusion.11.allowed_ref, ...), custom_call_target="tpu_custom_call" | custom-call | flops 99999997952 | bytes 16777216 | tf_op jit(solution)/shard_map/attention_forward/pallas_call | solution.py:1257
  172.8 67.1 %moe_forward.3 = (f32[128,1536]{1,0:T(8,128)}, bf16[1024,1664]{1,0:T(8,128)(2,1)}, bf16[1024,2048]{1,0:T(8,128)(2,1)}, bf16[1024,1024]{1,0:T(8,128)(2,1)}) custom-call(bf16[128,1664]{1,0:T(8,128)(2,1)} %get-tuple-element.66.block_ref, bf16[2,1536,1024]{2,1,0:T(8,128)(2,1)} %bitcast.58, bf16[2,1536,1024]{2,1,0:T(8,128)(2,1)} %collective-permute-done.7.gu_other, ...), custom_call_target="tpu_custom_call" | custom-call | flops 99999997952 | bytes 16777216 | tf_op jit(solution)/shard_map/moe_forward/pallas_call | solution.py:408
  239.9 1.4 multiply_reduce_fusion.1
  241.5 0.8 fusion.6.block_ref
  242.3 65.7 %moe_backward.2 = (f32[128,1536]{1,0:T(8,128)}, bf16[1536,1024]{1,0:T(8,128)(2,1)}, bf16[512,1536]{1,0:T(8,128)(2,1)}, bf16[1536,1024]{1,0:T(8,128)(2,1)}, bf16[...) custom-call(bf16[128,1664]{1,0:T(8,128)(2,1)} %fusion.6.block_ref, f32[8,1536]{1,0:T(8,128)} %pad.38.router_ref, ...), custom_call_target="tpu_custom_call" | custom-call | flops 99999997952 | bytes 16777216 | tf_op jit(solution)/shard_map/moe_backward/pallas_call | solution.py:643
  308.0 31.6 %attention_backward.2 = (f32[128,1536]{1,0:T(8,128)}, bf16[1536,128]{1,0:T(8,128)(2,1)}, bf16[768,4096]{1,0:T(8,128)(2,1)}) custom-call(f32[1536,128]{1,0:T(8,128)} %get-tuple-element.71.router_grad_ref, f32[128,1536]{1,0:T(8,128)} %get-tuple-element.72.db_ref, bf16[128,1536]{1,0:T(8,128)(2,1)} %copy-done.9, f32[128,1536]{1,0:T(8,128)} %get-tuple-element.73.h1_ref, ...), custom_call_target="tpu_custom_call" | custom-call | flops 99999997952 | bytes 16777216 | tf_op jit(solution)/shard_map/attention_backward/pallas_call | solution.py:1451
  339.6 1.3 multiply_reduce_fusion
  341.1 0.8 fusion.7.block_ref
  341.9 97.4 %moe_backward.3 = (f32[128,1536]{1,0:T(8,128)}, bf16[1536,1024]{1,0:T(8,128)(2,1)}, bf16[512,1536]{1,0:T(8,128)(2,1)}, bf16[1536,1024]{1,0:T(8,128)(2,1)}, bf16[...) custom-call(bf16[128,1664]{1,0:T(8,128)(2,1)} %fusion.7.block_ref, ...), custom_call_target="tpu_custom_call" | custom-call | flops 99999997952 | bytes 16777216 | tf_op jit(solution)/shard_map/moe_backward/pallas_call | solution.py:643
  439.4 61.7 %attention_backward.3 = (f32[128,1536]{1,0:T(8,128)}, bf16[1536,128]{1,0:T(8,128)(2,1)}, bf16[768,4096]{1,0:T(8,128)(2,1)}, bf16[3,48,4224]{2,1,0:T(8,128)(2,1)}, bf16[256,1536]{1,0:T(8,128)(2,1)}) custom-call(f32[1536,128]{1,0:T(8,128)} %get-tuple-element.86.router_grad_ref, f32[128,1536]{1,0:T(8,128)} %get-tuple-element.87.db_ref, ...), custom_call_target="tpu_custom_call" | custom-call | flops 99999997952 | bytes 16777216 | tf_op jit(solution)/shard_map/attention_backward/pallas_call | solution.py:1451
  501.1 2.2 select_bitcast_fusion
  503.3 120.2 %reduce_gradients.1 = (bf16[768,4224]{1,0:T(8,128)(2,1)}, bf16[1536,1024]{1,0:T(8,128)(2,1)}, bf16[512,1536]{1,0:T(8,128)(2,1)}, bf16[1536,1024]{1,0:T(8,128)(2,...) custom-call(bf16[8,2,48,4096]{3,2,1,0:T(8,128)(2,1)} %bitcast.48, ...), custom_call_target="tpu_custom_call" | custom-call | tf_op jit(solution)/shard_map/reduce_gradients/pallas_call | solution.py:993
  623.6 1.0 slice_convert_fusion
  625.1 0.8 copy.39
  627.1 1.3 maximum_select_fusion
  628.3 15.4 %finish_outputs.1 = (f32[768,2560]{1,0:T(8,128)}, f32[768,1536]{1,0:T(8,128)}, f32[2,1536,1024]{2,1,0:T(8,128)}, f32[2,512,1536]{2,1,0:T(8,128)}) custom-call(bf16[768,4224]{1,0:T(8,128)(2,1)} %get-tuple-element.106.attn, bf16[1536,1024]{1,0:T(8,128)(2,1)} %get-tuple-element.107.gu_own, bf16[1536,1024]{1,0:T(8,128)(2,1)} %get-tuple-element.108.gu_got, ...), custom_call_target="tpu_custom_call" | custom-call | tf_op jit(solution)/shard_map/finish_outputs/pallas_call | solution.py:1081
  (70 shorter events, 7.2 us)
Async XLA Ops:
  0.6 5.3 copy-start
  0.6 16.4 %copy-start.4 = (bf16[1,2,128,1536]{3,2,1,0:T(8,128)(2,1)S(1)}, bf16[1,2,128,1536]{3,2,1,0:T(8,128)(2,1)}, u32[]{:S(2)}) copy-start(bf16[1,2,128,1536]{3,2,1,0:T(8,128)(2,1)} %param.10) | copy-start | bytes 2359300
  1.5 8.8 %collective-permute-start.3 = (bf16[18,768]{1,0:T(8,128)(2,1)S(1)}, bf16[18,768]{1,0:T(8,128)(2,1)S(1)}, u32[]{:S(2)}, u32[]{:S(2)}) collective-permute-start(bf16[18,768]{1,0:T(8,128)(2,1)S(1)} %pad_maximum_fusion), channel_id=1, source_target_pairs={{0,17},{1,16},{16,1},{17,0},{2,19},{3,18},{18,3},{19,2},{4,21},{5,... | collective-permute-start | bytes 82952 | tf_op jit(solution)/shard_map/ppermute | solution.py:1769
  4.0 6.6 %collective-permute-start.2 = (bf16[18,768]{1,0:T(8,128)(2,1)S(1)}, bf16[18,768]{1,0:T(8,128)(2,1)S(1)}, u32[]{:S(2)}, u32[]{:S(2)}) collective-permute-start(bf16[18,768]{1,0:T(8,128)(2,1)S(1)} %pad_maximum_fusion), channel_id=1, source_target_pairs={{0,16},{16,0},{1,17},{17,1},{2,18},{18,2},{3,19},{19,3},{4,20},{20... | collective-permute-start | bytes 82952 | tf_op jit(solution)/shard_map/ppermute | solution.py:1495
  4.7 6.1 collective-permute-start.1
  5.4 2.7 collective-permute-start.4
  5.6 12.3 %collective-permute-start.5 = (bf16[768,2560]{1,0:T(8,128)(2,1)}, bf16[768,2560]{1,0:T(8,128)(2,1)}, u32[]{:S(2)}, u32[]{:S(2)}) collective-permute-start(bf16[768,2560]{1,0:T(8,128)(2,1)} %bitcast.63), channel_id=1, source_target_pairs={{0,16},{16,0},{1,17},{17,1},{2,18},{18,2},{3,19},{19,3},{4,20},{20... | collective-permute-start | bytes 11796488 | tf_op jit(solution)/shard_map/ppermute | solution.py:1495
  8.1 9.8 %collective-permute-start.6 = (bf16[768,1536]{1,0:T(8,128)(2,1)}, bf16[768,1536]{1,0:T(8,128)(2,1)}, u32[]{:S(2)}, u32[]{:S(2)}) collective-permute-start(bf16[768,1536]{1,0:T(8,128)(2,1)} %bitcast.73), channel_id=1, source_target_pairs={{0,16},{16,0},{1,17},{17,1},{2,18},{18,2},{3,19},{19,3},{4,20},{20... | collective-permute-start | bytes 7077896 | tf_op jit(solution)/shard_map/ppermute | solution.py:1495
  10.3 6.7 %collective-permute-start = (bf16[128,1536]{1,0:T(8,128)(2,1)S(1)}, bf16[128,1536]{1,0:T(8,128)(2,1)S(1)}, u32[]{:S(2)}, u32[]{:S(2)}) collective-permute-start(bf16[128,1536]{1,0:T(8,128)(2,1)S(1)} %dynamic-slice_bitcast_fusion), channel_id=1, source_target_pairs={{0,16},{16,0},{1,17},{17,1},{2,18},{18,2},{3,19},{19,3},{4,20},{20... | collective-permute-start | bytes 1179656 | tf_op jit(solution)/shard_map/ppermute | solution.py:1495
  10.6 58.9 %collective-permute-start.8 = (bf16[2,512,1536]{2,1,0:T(8,128)(2,1)}, bf16[2,512,1536]{2,1,0:T(8,128)(2,1)}, u32[]{:S(2)}, u32[]{:S(2)}) collective-permute-start(bf16[2,512,1536]{2,1,0:T(8,128)(2,1)} %bitcast.68), channel_id=1, source_target_pairs={{0,16},{16,0},{1,17},{17,1},{2,18},{18,2},{3,19},{19,3},{4,20},{20... | collective-permute-start | bytes 9437192 | tf_op jit(solution)/shard_map/ppermute | solution.py:1495
  10.8 58.8 %collective-permute-start.7 = (bf16[2,1536,1024]{2,1,0:T(8,128)(2,1)}, bf16[2,1536,1024]{2,1,0:T(8,128)(2,1)}, u32[]{:S(2)}, u32[]{:S(2)}) collective-permute-start(bf16[2,1536,1024]{2,1,0:T(8,128)(2,1)} %bitcast.56), channel_id=1, source_target_pairs={{0,16},{16,0},{1,17},{17,1},{2,18},{18,2},{3,19},{19,3},{4,20},{20... | collective-permute-start | bytes 18874376 | tf_op jit(solution)/shard_map/ppermute | solution.py:1495
  17.0 0.9 copy-start.7
  69.6 71.4 %copy-start.10 = (f32[128,1536]{1,0:T(8,128)S(1)}, f32[128,1536]{1,0:T(8,128)}, u32[]{:S(2)}) copy-start(f32[128,1536]{1,0:T(8,128)} %get-tuple-element.63.h1_ref) | copy-start | bytes 2359300
  172.8 67.1 %copy-start.5 = (bf16[1,2,128,1536]{3,2,1,0:T(8,128)(2,1)S(1)}, bf16[1,2,128,1536]{3,2,1,0:T(8,128)(2,1)}, u32[]{:S(2)}) copy-start(bf16[1,2,128,1536]{3,2,1,0:T(8,128)(2,1)} %param.10) | copy-start | bytes 2359300
  172.8 67.1 %copy-start.8 = (bf16[128,1536]{1,0:T(8,128)(2,1)S(1)}, bf16[128,1536]{1,0:T(8,128)(2,1)}, u32[]{:S(2)}) copy-start(bf16[128,1536]{1,0:T(8,128)(2,1)} %copy-done.7) | copy-start | bytes 1179652
  241.3 66.7 %copy-start.9 = (bf16[128,1536]{1,0:T(8,128)(2,1)}, bf16[128,1536]{1,0:T(8,128)(2,1)S(1)}, u32[]{:S(2)}) copy-start(bf16[128,1536]{1,0:T(8,128)(2,1)S(1)} %get-tuple-element.157.dout_ref) | copy-start | bytes 1179652
  308.0 31.6 %copy-start.2 = (f32[128,1536]{1,0:T(8,128)S(1)}, f32[128,1536]{1,0:T(8,128)}, u32[]{:S(2)}) copy-start(f32[128,1536]{1,0:T(8,128)} %get-tuple-element.65) | copy-start | bytes 2359300
  340.9 98.4 %copy-start.6 = (bf16[128,1536]{1,0:T(8,128)(2,1)}, bf16[128,1536]{1,0:T(8,128)(2,1)S(1)}, u32[]{:S(2)}) copy-start(bf16[128,1536]{1,0:T(8,128)(2,1)S(1)} %get-tuple-element.155.dout_ref) | copy-start | bytes 1179652
  439.3 61.7 %copy-start.3 = (f32[128,1536]{1,0:T(8,128)S(1)}, f32[128,1536]{1,0:T(8,128)}, u32[]{:S(2)}) copy-start(f32[128,1536]{1,0:T(8,128)} %get-tuple-element.67) | copy-start | bytes 2359300
  439.3 61.7 %copy-start.11 = (f32[128,1536]{1,0:T(8,128)S(1)}, f32[128,1536]{1,0:T(8,128)}, u32[]{:S(2)}) copy-start(f32[128,1536]{1,0:T(8,128)} %get-tuple-element.73.h1_ref) | copy-start | bytes 2359300
  623.6 3.5 copy-start.12
  628.3 15.4 %copy-start.1 = (s32[2,1,3]{2,1,0:T(1,128)S(1)}, s32[2,1,3]{2,1,0:T(1,128)}, u32[]{:S(2)}) copy-start(s32[2,1,3]{2,1,0:T(1,128)} %param.11) | copy-start | bytes 76

commit v2 on v1

--- a/solution.py
+++ b/solution.py
@@ -142,13 +142,15 @@
         q = c * HALVES + h
         return pltpu.make_async_remote_copy(
             src_ref=self.sums.at[q], dst_ref=self.from_low.at[q], send_sem=self.sum_send.at[q],
-            recv_sem=self.low_recv.at[q], device_id=self.device(self.z + 1, self.x), device_id_type=MESH)
+            recv_sem=self.low_recv.at[q],
+            device_id=self.device(jnp.minimum(self.z + 1, LINE - 1), self.x), device_id_type=MESH)
 
     def down_copy(self, c, h):
         q = c * HALVES + h
         return pltpu.make_async_remote_copy(
             src_ref=self.sums.at[q], dst_ref=self.from_high.at[q], send_sem=self.sum_send.at[q],
-            recv_sem=self.high_recv.at[q], device_id=self.device(self.z - 1, self.x), device_id_type=MESH)
+            recv_sem=self.high_recv.at[q],
+            device_id=self.device(jnp.maximum(self.z - 1, 0), self.x), device_id_type=MESH)
 
     def own_part(self, c, h, side=True):
         part = self.parts[self.block(c, h, self.x)].astype(F32)
@@ -328,8 +330,8 @@
     return loads
 
 
-def moe_forward_kernel(layer, experts, rows, width, block_ref, gu_hbm, gu_other, down_hbm, down_other,
-                       moe_ref, rows_hbm, kept_hbm, scaled_hbm,
+def moe_forward_kernel(layer, experts, rows, width, block_ref, h1_ref, gu_hbm, gu_other, down_hbm, down_other,
+                       moe_ref, out_ref, rows_hbm, kept_hbm, scaled_hbm,
                        gu_v, down_v, kept, scaled, load_sem, store_sem, *plane_refs):
     plane = Plane(rows, plane_refs)
     gathered, parts = plane.gathered, plane.parts
@@ -389,6 +391,7 @@
         return carry
 
     lax.fori_loop(0, HALVES, finish, 0)
+    out_ref[...] = (h1_ref[...] + moe_ref[...]).astype(out_ref.dtype)
     plane.drain()
 
     def stored(q, carry):
@@ -399,7 +402,7 @@
     lax.fori_loop(0, LINE * HALVES, stored, 0)
 
 
-def moe_forward(layer, block, weights, experts, collective_id):
+def moe_forward(layer, block, h1, weights, experts, out_type, collective_id):
     rows, wide = block.shape
     width = wide - LANES
     total = LINE * SIDE * rows
@@ -410,12 +413,13 @@
         name="moe_forward",
         out_shape=(
             jax.ShapeDtypeStruct((rows, width), F32),
+            jax.ShapeDtypeStruct((rows, width), out_type),
             jax.ShapeDtypeStruct((total, wide), BF16),
             jax.ShapeDtypeStruct((total, EXP_DEV * 2 * FF), BF16),
             jax.ShapeDtypeStruct((total, EXP_DEV * FF), BF16),
         ),
-        in_specs=[vmem] + [any_spec] * 4,
-        out_specs=(vmem, any_spec, any_spec, any_spec),
+        in_specs=[vmem] * 2 + [any_spec] * 4,
+        out_specs=(vmem, vmem, any_spec, any_spec, any_spec),
         scratch_shapes=[
             pltpu.VMEM((EXP_DEV, width, 2 * FF), BF16),
             pltpu.VMEM((EXP_DEV * FF, width), BF16),
@@ -427,36 +431,46 @@
         cost_estimate=COST,
         compiler_params=pltpu.CompilerParams(
             collective_id=collective_id, has_side_effects=True, vmem_limit_bytes=VMEM_BYTES),
-    )(block, *weights)
-
-
-def moe_backward_kernel(layer, experts, rows, width, beside, block_ref, router_ref, gu_hbm, gu_other, down_hbm,
+    )(block, h1, *weights)
+
+
+def moe_backward_kernel(layer, experts, rows, width, beside, dout_ref, moe_ref, small_ref, gu_hbm, gu_other, down_hbm,
                         down_other, rows_hbm, kept_hbm, scaled_hbm, *refs):
     (later, refs) = (refs[:4], refs[4:]) if beside else ((), refs)
     (db_ref, keep_gu_hbm, keep_down_hbm, send_gu_hbm, send_down_hbm, grad_router_ref), refs = refs[:6], refs[6:]
     (later_out, refs) = (refs[:4], refs[4:]) if beside else ((), refs)
-    (gu_v, down_v, fwd_rows, kept, scaled, dgu, send_gu, grad_gu, send_down, grad_down,
-     load_sem, store_sem), refs = refs[:12], refs[12:]
+    (gu_v, down_v, fwd_rows, kept, scaled, dgu, send_gu, grad_gu, send_down, grad_down, router,
+     load_sem, store_sem), refs = refs[:13], refs[13:]
     (later_v, refs) = (refs[:8], refs[8:]) if beside else ((), refs)
     plane_refs = refs
     plane = Plane(rows, plane_refs)
     gathered, parts = plane.gathered, plane.parts
+    if beside:
+        other_layer = LaterExperts(plane, *later, *later_out, *later_v)
+        other_layer.start_loads()
     loads = load_experts(layer, plane.sec, gu_hbm, gu_other, down_hbm, down_other, gu_v, down_v, load_sem)
     loads.append(pltpu.make_async_copy(rows_hbm, fwd_rows, load_sem.at[3]))
     loads.append(pltpu.make_async_copy(kept_hbm, kept, load_sem.at[4]))
     loads.append(pltpu.make_async_copy(scaled_hbm, scaled, load_sem.at[5]))
     for load in loads[3:]:
         load.start()
-    plane.place(block_ref)
+    dout = dout_ref[...]
+    outer = jnp.sum(dout.astype(F32) * moe_ref[...], axis=1, keepdims=True)
+    top = outer.astype(BF16).astype(F32)
+    lane = lax.broadcasted_iota(jnp.int32, (rows, LANES), 1)
+    terms = (jnp.where(lane == 0, top, 0.0) + jnp.where(lane == 1, outer - top, 0.0)).astype(BF16)
+    for h in range(HALVES):
+        at, part = plane.block(plane.z, h, plane.x), slice(h * plane.sub, (h + 1) * plane.sub)
+        gathered[at, pl.ds(0, width)] = dout[part]
+        gathered[at, pl.ds(width, LANES)] = terms[part]
+    router[...] = small_ref[pl.ds(0, experts)].astype(F32)
     plane.barrier(*([plane.other_core(), plane.other_shard()] if beside else []))
     plane.start_gather()
     if beside:
-        other_layer = LaterExperts(plane, *later, *later_out, *later_v)
-        other_layer.start_loads()
+        other_layer.start_copies()
+        other_layer.send()
     for load in loads:
         load.wait()
-    if beside:
-        other_layer.send()
     total = plane.both
     up_at = EXP_DEV * 2 * FF
 
@@ -501,7 +515,7 @@
             for j in range(1, EXP_DEV):
                 acc = acc + nt(dgu[at, pl.ds(j * 2 * FF, 2 * FF)], gu_v[j, cols, :])
             for j in range(EXP_DEV):
-                acc = acc + dcs[j] * router_ref[pl.ds(j, 1), cols]
+                acc = acc + dcs[j] * router[pl.ds(plane.owner * EXP_DEV + j, 1), cols]
             parts[at, cols] = acc.astype(BF16)
         plane.side_copy(c, h).start()
 
@@ -595,8 +609,11 @@
                 ))
 
     def start_loads(self):
-        for _, _, load, core_copy, *_ in self.parts:
+        for _, _, load, *_ in self.parts:
             load.start()
+
+    def start_copies(self):
+        for _, _, _, core_copy, *_ in self.parts:
             core_copy.start()
 
     def send(self):
@@ -623,9 +640,9 @@
             store.wait()
 
 
-def moe_backward(layer, block, router, weights, kept, later, experts, collective_id):
-    rows, wide = block.shape
-    width = wide - LANES
+def moe_backward(layer, dout, moe, small, weights, kept, later, experts, collective_id):
+    rows, width = dout.shape
+    wide = width + LANES
     total = LINE * SIDE * rows
     any_spec = pl.BlockSpec(memory_space=pl.ANY)
     vmem = pl.BlockSpec(memory_space=pltpu.VMEM)
@@ -648,7 +665,7 @@
             gu_shape, down_shape, gu_shape, down_shape,
             jax.ShapeDtypeStruct((width, LANES), F32),
         ) + later_out,
-        in_specs=[vmem, vmem] + [any_spec] * (7 + len(later)),
+        in_specs=[vmem] * 3 + [any_spec] * (7 + len(later)),
         out_specs=(vmem,) + (any_spec,) * 4 + (vmem,) + (any_spec,) * len(later_out),
         scratch_shapes=[
             pltpu.VMEM((EXP_DEV, width, 2 * FF), BF16),
@@ -658,13 +675,14 @@
             pltpu.VMEM((total, EXP_DEV * FF), BF16),
             pltpu.VMEM((total, EXP_DEV * 2 * FF + LANES), BF16),
             expert_gu, expert_gu, expert_down, expert_down,
+            pltpu.VMEM((experts, width), F32),
             pltpu.SemaphoreType.DMA((6,)),
             pltpu.SemaphoreType.DMA((4, width // TILE)),
         ] + later_scratch + plane_scratch(rows, width, wide),
         cost_estimate=COST,
         compiler_params=pltpu.CompilerParams(
             collective_id=collective_id, has_side_effects=True, vmem_limit_bytes=VMEM_BYTES),
-    )(block, router, *weights, *kept, *later)
+    )(dout, moe, small, *weights, *kept, *later)
 
 
 def split_terms(values):
@@ -835,10 +853,10 @@
     for load, _ in expert_loads[1:]:
         load.start()
     plane.barrier(plane.other_core(), plane.other_shard(), sums.diagonal(plane))
+    expert_loads[0][1].start()
     sums.start_copies()
-    for _, copy in expert_loads:
-        if copy is not None:
-            copy.start()
+    for _, copy in expert_loads[1:]:
+        copy.start()
 
     def move(h):
         return remote(
@@ -1170,9 +1188,9 @@
 LOADS = 2 * PAIRS * 3 + 1
 
 
-def attention_forward_kernel(layer, rows, width, h_ref, allowed_ref, gains_ref, router_ref, mask_ref, wq, wq_other,
+def attention_forward_kernel(layer, experts, rows, width, lens_ref, h_ref, small_ref, routes_ref, wq, wq_other,
                              wo, wo_other, block_ref, h1_ref, a_ref, qkv_ref, p_ref, o_ref,
-                             wq_v, wo_v, a_parts, a_half, part_send, got_part, out_send, got_out,
+                             router_v, wq_v, wo_v, a_parts, a_half, part_send, got_part, out_send, got_out,
                              load_sem, send_sem, recv_sem, *turn):
     pair = Pair()
     me, peer = pair.me, pair.peer
@@ -1185,7 +1203,8 @@
 
     h = h_ref[...].astype(F32)
     r1 = lax.rsqrt(jnp.mean(h * h, axis=1, keepdims=True) + EPS)
-    a = (h * r1 * gains_ref[pl.ds(0, 1), :]).astype(BF16)
+    gains = small_ref[pl.ds(experts, 2)].astype(F32)
+    a = (h * r1 * gains[0:1]).astype(BF16)
     for j in range(2):
         a_parts[j] = a[:, j * half : (j + 1) * half]
     a_half[span(me)] = a_parts[me]
@@ -1208,7 +1227,13 @@
     send_own.wait_recv()
     send_other.wait_recv()
     qkv_ref[...] = (mine + got_part[...].astype(F32)).astype(BF16)
-    allowed = allowed_ref[...] > 0
+    query = lax.broadcasted_iota(jnp.int32, (2 * rows, 2 * rows), 0)
+    key = lax.broadcasted_iota(jnp.int32, (2 * rows, 2 * rows), 1)
+    allowed = key <= query
+    end = 0
+    for n in range(lens_ref.shape[0]):
+        end = end + lens_ref[n]
+        allowed = allowed & ((query >= end) == (key >= end))
     for i in range(PAIRS):
         for n in range(KV_IN_PAIR):
             for g in range(GROUP):
@@ -1235,19 +1260,28 @@
     h1 = h + own + got_out[...].astype(F32)
     h1_ref[...] = h1
     r2 = lax.rsqrt(jnp.mean(h1 * h1, axis=1, keepdims=True) + EPS)
-    b = (h1 * r2 * gains_ref[pl.ds(1, 1), :]).astype(BF16)
+    b = (h1 * r2 * gains[1:2]).astype(BF16)
     block_ref[:, pl.ds(0, width)] = b
-    mask = mask_ref[...] > 0
-    logits = jnp.where(mask, nt(b, router_ref[...]), MASKED_SCORE)
+    router_v[...] = jnp.zeros_like(router_v)
+    for copy in range(2):
+        router_v[pl.ds(copy * experts, experts)] = small_ref[pl.ds(0, experts)]
+    lane = lax.broadcasted_iota(jnp.int32, (rows, LANES), 1)
+    column = jnp.where(lane < experts, lane, lane - experts)
+    routes = routes_ref[...]
+    mask = routes[:, 0:1] == column
+    for n in range(1, TOP):
+        mask = mask | (routes[:, n : n + 1] == column)
+    mask = mask & (lane < 2 * experts)
+    logits = jnp.where(mask, nt(b, router_v[...]), MASKED_SCORE)
     ex = jnp.where(mask, jnp.exp(logits - jnp.max(logits, axis=1, keepdims=True)), 0.0)
     gates = ex / (0.5 * jnp.sum(ex, axis=1, keepdims=True))
     high = gates.astype(BF16).astype(F32)
-    block_ref[:, pl.ds(width, LANES)] = jnp.where(mask_ref[...] > 1, gates - high, high).astype(BF16)
+    block_ref[:, pl.ds(width, LANES)] = jnp.where(lane >= experts, gates - high, high).astype(BF16)
     for send in (send_a, send_own, send_other, send_out):
         send.wait_send()
 
 
-def attention_forward(layer, h, allowed, gains, router, mask, weights, collective_id):
+def attention_forward(layer, experts, lens, h, small, routes, weights, collective_id):
     rows, width = h.shape
     half, group = width // 2, 2 * rows
     qkv = (QUERY_WIDTH + 2 * KV_WIDTH) // 2
@@ -1255,7 +1289,7 @@
     any_spec = pl.BlockSpec(memory_space=pl.ANY)
     vmem = pl.BlockSpec(memory_space=pltpu.VMEM)
     return pl.pallas_call(
-        functools.partial(attention_forward_kernel, layer, rows, width),
+        functools.partial(attention_forward_kernel, layer, experts, rows, width),
         name="attention_forward",
         out_shape=(
             jax.ShapeDtypeStruct((rows, width + LANES), BF16),
@@ -1265,9 +1299,10 @@
             jax.ShapeDtypeStruct((heads, group, group), BF16),
             jax.ShapeDtypeStruct((group, QUERY_WIDTH // 2), BF16),
         ),
-        in_specs=[vmem] * 5 + [any_spec] * 4,
+        in_specs=[pl.BlockSpec(memory_space=pltpu.SMEM)] + [vmem] * 3 + [any_spec] * 4,
         out_specs=(vmem,) * 6,
         scratch_shapes=[
+            pltpu.VMEM((LANES, width), BF16),
             pltpu.VMEM((2, half, qkv), BF16),
             pltpu.VMEM((QUERY_WIDTH // 2, width), BF16),
             pltpu.VMEM((2, rows, half), BF16),
@@ -1283,13 +1318,13 @@
         cost_estimate=COST,
         compiler_params=pltpu.CompilerParams(
             collective_id=collective_id, has_side_effects=True, vmem_limit_bytes=VMEM_BYTES),
-    )(h, allowed, gains, router, mask, *weights)
+    )(lens, h, small, routes, *weights)
 
 
 ATTENTION_BACKWARD_REFS = 20
 
 
-def attention_backward_kernel(layer, rows, width, experts, router_grad_ref, db_ref, dout_ref, h1_ref, h_ref, gains_ref, a_ref, qkv_ref,
+def attention_backward_kernel(layer, rows, width, experts, router_grad_ref, db_ref, dout_ref, h1_ref, h_ref, small_ref, a_ref, qkv_ref,
                               p_ref, o_ref, wq, wq_other, wo, wo_other, *refs):
     beside = len(refs) > ATTENTION_BACKWARD_REFS
     (later, refs) = (refs[:3], refs[3:]) if beside else ((), refs)
@@ -1315,7 +1350,11 @@
         plane.barrier(plane.other_core(), plane.other_shard(), sums.diagonal(plane))
         sums.start_copies()
         load_tail.wait()
-        tail_copy = pair.send(tail_own, tail_got, tail_sem.at[0], tail_sem.at[1])
+        tail_copies = []
+        for n in range(2):
+            at = pl.ds(n * (tail_rows // 2), tail_rows // 2)
+            tail_copies.append(pair.send(tail_own.at[at], tail_got.at[at], tail_sem.at[0, n], tail_sem.at[1, n]))
+        tail_copies[0].start()
     else:
         pair.barrier()
 
@@ -1326,7 +1365,8 @@
     r2 = lax.rsqrt(jnp.mean(h1 * h1, axis=1, keepdims=True) + EPS)
     normed = h1 * r2
     db = db_ref[...]
-    scaled = db * gains_ref[pl.ds(1, 1), :]
+    gains = small_ref[pl.ds(experts, 2)].astype(F32)
+    scaled = db * gains[1:2]
     gain_grads_ref[...] = jnp.zeros_like(gain_grads_ref)
     gain_grads_ref[pl.ds(experts + 1, 1), :] = jnp.sum(db * normed, axis=0, keepdims=True)
     dh1 = dout_ref[...].astype(F32) + r2 * (
@@ -1349,7 +1389,7 @@
     do[span(peer)] = nt(d_all[span(peer)], wo_v[...]).astype(BF16)
     sends = [send_d]
     if beside:
-        tail_copy.start()
+        tail_copies[1].start()
         pl.when(plane.inner == 0)(lambda: sums.pass_on(0))
         sums.prepare(LINE, LINE * SIDE)
     for i in range(PAIRS):
@@ -1408,16 +1448,17 @@
         da_j = jnp.where(me == j, own_da, other_da)
         normed = h[:, j * half : (j + 1) * half] * r1
         gain_grads_ref[pl.ds(experts, 1), cols] = jnp.sum(da_j * normed, axis=0, keepdims=True)
-        scaled = da_j * gains_ref[pl.ds(0, 1), cols]
+        scaled = da_j * gains[0:1, j * half : (j + 1) * half]
         total = total + jnp.sum(scaled * normed, axis=1, keepdims=True)
         halves.append((cols, scaled, normed))
     columns = columns_v[...] + jnp.transpose(gain_grads_ref[...])
     columns_ref[...] = columns.astype(BF16)
     for cols, scaled, normed in halves:
-        dh_ref[:, cols] = dh1_v[:, cols] + r1 * (scaled - normed * (total / width))
+        dh_ref[:, cols] = (dh1_v[:, cols] + r1 * (scaled - normed * (total / width))).astype(dh_ref.dtype)
     if beside:
         sums.hand_over(later_out[0])
-        tail_copy.wait()
+        for copy in tail_copies:
+            copy.wait()
         later_out[1][...] = (tail_own[...].astype(F32) + tail_got[...].astype(F32)).astype(BF16)
         sums.drain(1)
     for send in sends + [send_da]:
@@ -1426,7 +1467,7 @@
         store.wait()
 
 
-def attention_backward(layer, experts, router_grad, db, dout, h1, h, gains, a_half, qkv, p, o, weights, later,
+def attention_backward(layer, experts, router_grad, db, dout, h1, h, small, a_half, qkv, p, o, weights, later,
                        collective_id):
     rows, width = db.shape
     half, group = width // 2, 2 * rows
@@ -1446,13 +1487,13 @@
             pltpu.VMEM(tail_shape, BF16),
             pltpu.VMEM(tail_shape, BF16),
             pltpu.SemaphoreType.DMA,
-            pltpu.SemaphoreType.DMA((2,)),
+            pltpu.SemaphoreType.DMA((2, 2)),
         ] + plane[1:]
     return pl.pallas_call(
         functools.partial(attention_backward_kernel, layer, rows, width, experts),
         name="attention_backward",
         out_shape=(
-            jax.ShapeDtypeStruct((rows, width), F32),
+            jax.ShapeDtypeStruct((rows, width), F32 if layer == 0 else BF16),
             jax.ShapeDtypeStruct((width, LANES), BF16),
             jax.ShapeDtypeStruct((half, QUERY_WIDTH + 2 * KV_WIDTH + width), BF16),
         ) + later_out,
@@ -1480,7 +1521,7 @@
         cost_estimate=COST,
         compiler_params=pltpu.CompilerParams(
             collective_id=collective_id, has_side_effects=True, vmem_limit_bytes=VMEM_BYTES),
-    )(router_grad, db, dout, h1, h, gains, a_half, qkv, p, o, *weights, *later)
+    )(router_grad, db, dout, h1, h, small, a_half, qkv, p, o, *weights, *later)
 
 
 def dot(a, b, dims):
@@ -1778,46 +1819,29 @@
     layer_small = by_core(joined(small, swap_shards(small)), joined(swap_cores(small), across))
     x_in, dy = by_core(pick(edge_inputs[0], sec), swap_cores(pick(edge_inputs[0], 1 - sec)))
     layer_routes = by_core(pick(routes[0], sec), swap_cores(pick(routes[0], 1 - sec)))
-    allowed = document_mask(pick(seq_lengths, sec)[0], 2 * rows).astype(F32)
+    lens = pick(seq_lengths, sec)[0]
     attn_weights = (w_qkv[0], swap_cores(w_qkv[0]), w_out[0], swap_cores(w_out[0]))
     expert_weights = (
         w_gate_up[0], swap_cores(w_gate_up[0]), w_down[0], swap_cores(w_down[0])
     )
-    gains, routers, masks = [], [], []
-    for layer in range(2):
-        gains.append(
-            jnp.pad(layer_small[layer][experts:].astype(F32), ((0, 8 - 2), (0, 0)))
-        )
-        router = layer_small[layer][:experts]
-        router = jnp.concatenate([router, router], axis=0)
-        routers.append(jnp.pad(router, ((0, LANES - 2 * experts), (0, 0))))
-        lane = jnp.arange(LANES, dtype=jnp.int32)[None, :]
-        hot = jnp.any(layer_routes[layer][:, :, None] == lane[None] % experts, axis=1)
-        masks.append(
-            jnp.where(hot & (lane < 2 * experts), 1.0 + (lane >= experts), 0.0).astype(F32)
-        )
-
     def forward(layer, h):
         block, h1, *attn_state = attention_forward(
-            layer, h, allowed, gains[layer], routers[layer], masks[layer], attn_weights, 1 + layer
+            layer, experts, lens, h, layer_small[layer], layer_routes[layer], attn_weights, 1 + layer
         )
-        moe, *expert_state = moe_forward(layer, block, expert_weights, experts, 3 + layer)
-        return h1 + moe, (h, h1, moe, attn_state, expert_state)
+        moe, out, *expert_state = moe_forward(
+            layer, block, h1, expert_weights, experts, F32 if layer else BF16, 3 + layer
+        )
+        return out, (h, h1, moe, attn_state, expert_state)
 
     def backward(layer, dout, state, later, later_attn):
         h, h1, moe, attn_state, expert_state = state
-        outer = jnp.sum(dout.astype(F32) * moe, axis=1, keepdims=True)
-        block = with_lanes(dout, split_terms(outer))
-        own_router = lax.dynamic_slice_in_dim(
-            layer_small[layer].astype(F32), owner * EXP_DEV, EXP_DEV, 0
-        )
-        own_router = jnp.pad(own_router, ((0, 8 - EXP_DEV), (0, 0)))
         results = moe_backward(
-            layer, block, own_router, expert_weights, expert_state, later, experts, 5 + layer
+            layer, dout, moe, layer_small[layer], expert_weights, expert_state, later, experts,
+            5 + layer,
         )
         db, keep_gu, keep_down, send_gu, send_down, grad_router = results[:6]
         dh, columns, grad_attn, *piece = attention_backward(
-            layer, experts, grad_router, db, dout, h1, h, gains[layer], *attn_state, attn_weights,
+            layer, experts, grad_router, db, dout, h1, h, layer_small[layer], *attn_state, attn_weights,
             later_attn + tuple(results[7:8]) if later else (), 7 + layer,
         )
         places = LINE * SIDE
@@ -1827,10 +1851,10 @@
         return dh, grad_attn, columns, (keep_gu, keep_down, send_gu, send_down), results[6:8], piece
 
     out0, state0 = forward(0, x_in)
-    final, state1 = forward(1, out0.astype(BF16))
+    final, state1 = forward(1, out0)
     dh_one, attn1, columns1, experts1, *_ = backward(1, dy, state1, (), ())
     dh_zero, attn0, columns0, experts0, sums1, (shares1, tail1) = backward(
-        0, dh_one.astype(BF16), state0, experts1, (attn1, columns1)
+        0, dh_one, state0, experts1, (attn1, columns1)
     )
     send = jnp.where(sec == 0, final, dh_zero)
     attn, gu_own, down_own, gu_got, down_got, down_one, gu_moved, down_moved, got = reduce_gradients(

time: 651 us -> 650 us (level)
  other arithmetic: 20 us -> 10.9 us
  transfers between devices with their start and end apart: 9 -> 9, of which waited for: 0 -> 2; matrix products, arithmetic and copies ran while one was open for 2% -> 1% of each run, Pallas kernels for 8% -> 8%
where the time goes in v2:
time: 650 us; the launch traced here: 644 us
  Pallas kernels  615 us (95%)
  other arithmetic  10.9 us (2%)
  starting transfers between devices  7.26 us (1%)
    pallas_call x2, Pallas kernels, moe_backward(): pl.pallas_call(functools.partial(moe_backward_kernel, layer, experts, row...  163 us
    pallas_call x2, Pallas kernels, moe_forward(): pl.pallas_call(functools.partial(moe_forward_kernel, layer, experts, rows...  142 us
    pallas_call x1, Pallas kernels, reduce_gradients(): pl.pallas_call(functools.partial(reduce_kernel, sub, cols), name='reduce_...  120 us
    pallas_call x2, Pallas kernels, attention_backward(): pl.pallas_call(functools.partial(attention_backward_kernel, layer, rows,...  93.2 us
    pallas_call x2, Pallas kernels, attention_forward(): pl.pallas_call(functools.partial(attention_forward_kernel, layer, experts...  81.7 us
    pallas_call x1, Pallas kernels, finish_outputs(): pl.pallas_call(functools.partial(finish_kernel, qkv_cols), name='finish_o...  15.4 us
  transfers between devices with their start and end apart: 9, of which 2 were waited for; matrix products, arithmetic and copies ran while one was open for 1% of the time, Pallas kernels for 8%

profile of v2, /device:TPU:0, one launch (start us, length us, event | category | flops | bytes accessed | tf_op | source)
XLA Modules:
  0.0 643.6 jit_solution(5968598757693675803)
XLA Ops:
  0.6 0.5 collective-permute-start.5
  1.2 0.8 pad_maximum_fusion
  2.0 2.7 collective-permute-start.3
  5.2 0.7 constant_dynamic-slice_fusion.1
  6.1 1.0 dynamic-slice_bitcast_fusion
  7.1 0.5 fusion.lens_ref
  7.8 2.1 collective-permute-done.4
  9.8 2.9 collective-permute-start.1
  12.7 0.7 bitcast_select_fusion.2
  13.4 0.5 collective-permute-start.8
  13.9 0.7 collective-permute-done.1
  14.6 1.5 broadcast_select_fusion.1.small_ref
  16.2 1.5 broadcast_select_fusion.2.small_ref
  17.7 1.9 bitcast_select_fusion
  19.6 1.4 copy-done.4
  21.0 52.0 %attention_forward.2 = (bf16[128,1664]{1,0:T(8,128)(2,1)}, f32[128,1536]{1,0:T(8,128)}, bf16[256,768]{1,0:T(8,128)(2,1)}, bf16[256,1280]{1,0:T(8,128)(2,1)}, bf1...) custom-call(s32[3]{0:T(128)} %fusion.lens_ref, bf16[128,1536]{1,0:T(8,128)(2,1)} %get-tuple-element.142.h_ref, ...), custom_call_target="tpu_custom_call" | custom-call | flops 99999997952 | bytes 16777216 | tf_op jit(solution)/shard_map/attention_forward/pallas_call | solution.py:1291
  73.0 71.7 %moe_forward.2 = (f32[128,1536]{1,0:T(8,128)}, bf16[128,1536]{1,0:T(8,128)(2,1)}, bf16[1024,1664]{1,0:T(8,128)(2,1)}, bf16[1024,2048]{1,0:T(8,128)(2,1)}, bf16[1024,1024]{1,0:T(8,128)(2,1)}) custom-call(bf16[128,1664]{1,0:T(8,128)(2,1)} %get-tuple-element.65.block_ref, f32[128,1536]{1,0:T(8,128)} %get-tuple-element.66.h1_ref, ...), custom_call_target="tpu_custom_call" | custom-call | flops 99999997952 | bytes 16777216 | tf_op jit(solution)/shard_map/moe_forward/pallas_call | solution.py:411
  144.8 29.7 %attention_forward.3 = (bf16[128,1664]{1,0:T(8,128)(2,1)}, f32[128,1536]{1,0:T(8,128)}, bf16[256,768]{1,0:T(8,128)(2,1)}, bf16[256,1280]{1,0:T(8,128)(2,1)}, bf1...) custom-call(s32[3]{0:T(128)} %fusion.lens_ref, bf16[128,1536]{1,0:T(8,128)(2,1)} %get-tuple-element.67.h_ref, ...), custom_call_target="tpu_custom_call" | custom-call | flops 99999997952 | bytes 16777216 | tf_op jit(solution)/shard_map/attention_forward/pallas_call | solution.py:1291
  174.5 70.0 %moe_forward.3 = (f32[128,1536]{1,0:T(8,128)}, f32[128,1536]{1,0:T(8,128)}, bf16[1024,1664]{1,0:T(8,128)(2,1)}, bf16[1024,2048]{1,0:T(8,128)(2,1)}, bf16[1024,1024]{1,0:T(8,128)(2,1)}) custom-call(bf16[128,1664]{1,0:T(8,128)(2,1)} %get-tuple-element.68.block_ref, f32[128,1536]{1,0:T(8,128)} %get-tuple-element.69.h1_ref, bf16[2,1536,1024]{2,1,0:T(8,128)(2,1)} %bitcast.42, ...), custom_call_target="tpu_custom_call" | custom-call | flops 99999997952 | bytes 16777216 | tf_op jit(solution)/shard_map/moe_forward/pallas_call | solution.py:411
  244.5 65.4 %moe_backward.2 = (f32[128,1536]{1,0:T(8,128)}, bf16[1536,1024]{1,0:T(8,128)(2,1)}, bf16[512,1536]{1,0:T(8,128)(2,1)}, bf16[1536,1024]{1,0:T(8,128)(2,1)}, bf16[...) custom-call(bf16[128,1536]{1,0:T(8,128)(2,1)} %get-tuple-element.143.dout_ref, f32[128,1536]{1,0:T(8,128)} %get-tuple-element.70.moe_ref, ...), custom_call_target="tpu_custom_call" | custom-call | flops 99999997952 | bytes 16777216 | tf_op jit(solution)/shard_map/moe_backward/pallas_call | solution.py:660
  309.9 31.4 %attention_backward.2 = (bf16[128,1536]{1,0:T(8,128)(2,1)}, bf16[1536,128]{1,0:T(8,128)(2,1)}, bf16[768,4096]{1,0:T(8,128)(2,1)}) custom-call(f32[1536,128]{1,0:T(8,128)} %get-tuple-element.74.router_grad_ref, f32[128,1536]{1,0:T(8,128)} %get-tuple-element.75.db_ref, bf16[128,1536]{1,0:T(8,128)(2,1)} %get-tuple-element.143.dout_ref, ...), custom_call_target="tpu_custom_call" | custom-call | flops 99999997952 | bytes 16777216 | tf_op jit(solution)/shard_map/attention_backward/pallas_call | solution.py:1492
  341.3 98.1 %moe_backward.3 = (f32[128,1536]{1,0:T(8,128)}, bf16[1536,1024]{1,0:T(8,128)(2,1)}, bf16[512,1536]{1,0:T(8,128)(2,1)}, bf16[1536,1024]{1,0:T(8,128)(2,1)}, bf16[...) custom-call(bf16[128,1536]{1,0:T(8,128)(2,1)} %get-tuple-element.80., ...), custom_call_target="tpu_custom_call" | custom-call | flops 99999997952 | bytes 16777216 | tf_op jit(solution)/shard_map/moe_backward/pallas_call | solution.py:660
  439.4 61.9 %attention_backward.3 = (f32[128,1536]{1,0:T(8,128)}, bf16[1536,128]{1,0:T(8,128)(2,1)}, bf16[768,4096]{1,0:T(8,128)(2,1)}, bf16[3,48,4224]{2,1,0:T(8,128)(2,1)}, bf16[256,1536]{1,0:T(8,128)(2,1)}) custom-call(f32[1536,128]{1,0:T(8,128)} %get-tuple-element.89.router_grad_ref, f32[128,1536]{1,0:T(8,128)} %get-tuple-element.90.db_ref, ...), custom_call_target="tpu_custom_call" | custom-call | flops 99999997952 | bytes 16777216 | tf_op jit(solution)/shard_map/attention_backward/pallas_call | solution.py:1492
  501.3 2.2 select_bitcast_fusion
  503.5 119.6 %reduce_gradients.1 = (bf16[768,4224]{1,0:T(8,128)(2,1)}, bf16[1536,1024]{1,0:T(8,128)(2,1)}, bf16[512,1536]{1,0:T(8,128)(2,1)}, bf16[1536,1024]{1,0:T(8,128)(2,...) custom-call(bf16[8,2,48,4096]{3,2,1,0:T(8,128)(2,1)} %bitcast.31, ...), custom_call_target="tpu_custom_call" | custom-call | tf_op jit(solution)/shard_map/reduce_gradients/pallas_call | solution.py:1011
  623.1 1.0 slice_convert_fusion
  624.1 0.5 slice_reduce_fusion
  624.7 0.8 copy.23
  625.4 0.6 broadcast_in_dim_squeeze.7
  626.0 0.6 broadcast_in_dim_squeeze.6
  626.6 1.3 maximum_select_fusion
  627.8 15.4 %finish_outputs.1 = (f32[768,2560]{1,0:T(8,128)}, f32[768,1536]{1,0:T(8,128)}, f32[2,1536,1024]{2,1,0:T(8,128)}, f32[2,512,1536]{2,1,0:T(8,128)}) custom-call(bf16[768,4224]{1,0:T(8,128)(2,1)} %get-tuple-element.110.attn, bf16[1536,1024]{1,0:T(8,128)(2,1)} %get-tuple-element.111.gu_own, bf16[1536,1024]{1,0:T(8,128)(2,1)} %get-tuple-element.112.gu_got, ...), custom_call_target="tpu_custom_call" | custom-call | tf_op jit(solution)/shard_map/finish_outputs/pallas_call | solution.py:1099
  (24 shorter events, 0.9 us)
Async XLA Ops:
  0.6 6.5 %copy-start = (s32[2,1,3]{2,1,0:T(1,128)S(1)}, s32[2,1,3]{2,1,0:T(1,128)}, u32[]{:S(2)}) copy-start(s32[2,1,3]{2,1,0:T(1,128)} %param.11) | copy-start | bytes 76
  0.6 19.0 %collective-permute-start.5 = (bf16[768,2560]{1,0:T(8,128)(2,1)}, bf16[768,2560]{1,0:T(8,128)(2,1)}, u32[]{:S(2)}, u32[]{:S(2)}) collective-permute-start(bf16[768,2560]{1,0:T(8,128)(2,1)} %bitcast.47), channel_id=1, source_target_pairs={{0,16},{16,0},{1,17},{17,1},{2,18},{18,2},{3,19},{19,3},{4,20},{20... | collective-permute-start | bytes 11796488 | tf_op jit(solution)/shard_map/ppermute | solution.py:1536
  1.2 18.4 %collective-permute-start.6 = (bf16[768,1536]{1,0:T(8,128)(2,1)}, bf16[768,1536]{1,0:T(8,128)(2,1)S(1)}, u32[]{:S(2)}, u32[]{:S(2)}) collective-permute-start(bf16[768,1536]{1,0:T(8,128)(2,1)} %bitcast.57), channel_id=1, source_target_pairs={{0,16},{16,0},{1,17},{17,1},{2,18},{18,2},{3,19},{19,3},{4,20},{20... | collective-permute-start | bytes 7077896 | tf_op jit(solution)/shard_map/ppermute | solution.py:1536
  2.0 11.4 %collective-permute-start.3 = (bf16[18,768]{1,0:T(8,128)(2,1)S(1)}, bf16[18,768]{1,0:T(8,128)(2,1)S(1)}, u32[]{:S(2)}, u32[]{:S(2)}) collective-permute-start(bf16[18,768]{1,0:T(8,128)(2,1)S(1)} %pad_maximum_fusion), channel_id=1, source_target_pairs={{0,17},{1,16},{16,1},{17,0},{2,19},{3,18},{18,3},{19,2},{4,21},{5,... | collective-permute-start | bytes 82952 | tf_op jit(solution)/shard_map/ppermute | solution.py:1810
  4.7 8.7 %collective-permute-start.2 = (bf16[18,768]{1,0:T(8,128)(2,1)S(1)}, bf16[18,768]{1,0:T(8,128)(2,1)S(1)}, u32[]{:S(2)}, u32[]{:S(2)}) collective-permute-start(bf16[18,768]{1,0:T(8,128)(2,1)S(1)} %pad_maximum_fusion), channel_id=1, source_target_pairs={{0,16},{16,0},{1,17},{17,1},{2,18},{18,2},{3,19},{19,3},{4,20},{20... | collective-permute-start | bytes 82952 | tf_op jit(solution)/shard_map/ppermute | solution.py:1536
  6.0 3.9 collective-permute-start.4
  9.8 4.8 collective-permute-start.1
  13.4 4.3 collective-permute-start
  13.4 59.6 %collective-permute-start.8 = (bf16[2,512,1536]{2,1,0:T(8,128)(2,1)}, bf16[2,512,1536]{2,1,0:T(8,128)(2,1)}, u32[]{:S(2)}, u32[]{:S(2)}) collective-permute-start(bf16[2,512,1536]{2,1,0:T(8,128)(2,1)} %bitcast.52), channel_id=1, source_target_pairs={{0,16},{16,0},{1,17},{17,1},{2,18},{18,2},{3,19},{19,3},{4,20},{20... | collective-permute-start | bytes 9437192 | tf_op jit(solution)/shard_map/ppermute | solution.py:1536
  14.6 58.4 %collective-permute-start.7 = (bf16[2,1536,1024]{2,1,0:T(8,128)(2,1)}, bf16[2,1536,1024]{2,1,0:T(8,128)(2,1)}, u32[]{:S(2)}, u32[]{:S(2)}) collective-permute-start(bf16[2,1536,1024]{2,1,0:T(8,128)(2,1)} %bitcast.40), channel_id=1, source_target_pairs={{0,16},{16,0},{1,17},{17,1},{2,18},{18,2},{3,19},{19,3},{4,20},{20... | collective-permute-start | bytes 18874376 | tf_op jit(solution)/shard_map/ppermute | solution.py:1536
  19.6 1.4 copy-start.4
  439.4 61.9 %copy-start.2 = (f32[128,1536]{1,0:T(8,128)S(1)}, f32[128,1536]{1,0:T(8,128)}, u32[]{:S(2)}) copy-start(f32[128,1536]{1,0:T(8,128)} %get-tuple-element.99) | copy-start | bytes 2359300
  623.1 3.5 copy-start.3
  627.8 15.4 %copy-start.1 = (s32[2,1,3]{2,1,0:T(1,128)S(1)}, s32[2,1,3]{2,1,0:T(1,128)}, u32[]{:S(2)}) copy-start(s32[2,1,3]{2,1,0:T(1,128)} %param.11) | copy-start | bytes 76

commit v3 on v2

--- a/solution.py
+++ b/solution.py
@@ -434,7 +434,7 @@
     )(block, h1, *weights)
 
 
-def moe_backward_kernel(layer, experts, rows, width, beside, dout_ref, moe_ref, small_ref, gu_hbm, gu_other, down_hbm,
+def moe_backward_kernel(layer, experts, rows, width, beside, dout_ref, moe_ref, s0, s1, s2, s3, gu_hbm, gu_other, down_hbm,
                         down_other, rows_hbm, kept_hbm, scaled_hbm, *refs):
     (later, refs) = (refs[:4], refs[4:]) if beside else ((), refs)
     (db_ref, keep_gu_hbm, keep_down_hbm, send_gu_hbm, send_down_hbm, grad_router_ref), refs = refs[:6], refs[6:]
@@ -463,7 +463,8 @@
         at, part = plane.block(plane.z, h, plane.x), slice(h * plane.sub, (h + 1) * plane.sub)
         gathered[at, pl.ds(0, width)] = dout[part]
         gathered[at, pl.ds(width, LANES)] = terms[part]
-    router[...] = small_ref[pl.ds(0, experts)].astype(F32)
+    for j, part in enumerate(layer_rows(layer, plane.sec, plane.shard, (s0, s1, s2, s3))):
+        router[:, pl.ds(j * (width // 2), width // 2)] = part[:experts]
     plane.barrier(*([plane.other_core(), plane.other_shard()] if beside else []))
     plane.start_gather()
     if beside:
@@ -581,6 +582,13 @@
             store.wait()
 
 
+def layer_rows(layer, sec, shard, refs):
+    own, sideways, across, diagonal = (ref[...].astype(F32) for ref in refs)
+    mine = jnp.where(sec == layer, own, across)
+    others = jnp.where(sec == layer, sideways, diagonal)
+    return jnp.where(shard == 0, mine, others), jnp.where(shard == 0, others, mine)
+
+
 class LaterExperts:
     def __init__(self, plane, keep_gu, keep_down, send_gu, send_down, sum_gu_hbm, sum_down_hbm, land_gu, land_down,
                  gu_a, gu_b, down_a, down_b, load_sem, core_sem, send_sem, recv_sem):
@@ -665,7 +673,7 @@
             gu_shape, down_shape, gu_shape, down_shape,
             jax.ShapeDtypeStruct((width, LANES), F32),
         ) + later_out,
-        in_specs=[vmem] * 3 + [any_spec] * (7 + len(later)),
+        in_specs=[vmem] * 6 + [any_spec] * (7 + len(later)),
         out_specs=(vmem,) + (any_spec,) * 4 + (vmem,) + (any_spec,) * len(later_out),
         scratch_shapes=[
             pltpu.VMEM((EXP_DEV, width, 2 * FF), BF16),
@@ -682,7 +690,7 @@
         cost_estimate=COST,
         compiler_params=pltpu.CompilerParams(
             collective_id=collective_id, has_side_effects=True, vmem_limit_bytes=VMEM_BYTES),
-    )(dout, moe, small, *weights, *kept, *later)
+    )(dout, moe, *small, *weights, *kept, *later)
 
 
 def split_terms(values):
@@ -806,7 +814,7 @@
     return own, plane
 
 
-def reduce_kernel(sub, cols, g0, t0, shares1, gu_hbm, down_hbm, sent_gu_hbm, sent_down_hbm, gu1_hbm, down1_hbm, tail1_hbm, edge,
+def reduce_kernel(sub, cols, g0, t0, shares1, gu_hbm, down_hbm, sent_gu_hbm, sent_down_hbm, gu1_hbm, down1_hbm, tail1_hbm, dh, final,
                   sum_hbm, own_gu_hbm, own_down_hbm, got_gu_hbm, got_down_hbm, own_down1_hbm, got_gu1_hbm,
                   got_down1_hbm, got_edge,
                   core_got, small_own, small_got, load_sem, core_sem, small_sem,
@@ -899,8 +907,10 @@
     for load in load_shares:
         load.wait()
     plane.send_sum(second, 0)
-    edges = remote(edge, got_edge, edge_sem.at[0], edge_sem.at[1], plane.other_core())
-    edges.start()
+    edges = remote(final, got_edge, edge_sem.at[0], edge_sem.at[1], plane.other_core())
+    edge_back = remote(dh, got_edge, edge_sem.at[0], edge_sem.at[1], plane.other_core())
+    pl.when(core == 0)(lambda: edges.start())
+    pl.when(core == 1)(lambda: edge_back.start())
     later_copies = [
         remote(gu1_hbm, got_gu1_hbm, edge_sem.at[2], edge_sem.at[3], plane.other_core()),
         remote(down1_hbm.at[low], got_down1_hbm.at[low], edge_sem.at[4], edge_sem.at[5], plane.other_core()),
@@ -1000,7 +1010,7 @@
         pl.when(core == 1)(lambda copy=copy: copy.wait_recv())
 
 
-def reduce_gradients(g0, t0, shares1, experts0, gu1, down1, tail1, edge, collective_id):
+def reduce_gradients(g0, t0, shares1, experts0, gu1, down1, tail1, dh, final, collective_id):
     places, halves, sub, cols = g0.shape
     grad_gu, grad_down = experts0[:2]
     any_spec = pl.BlockSpec(memory_space=pl.ANY)
@@ -1013,9 +1023,9 @@
         name="reduce_gradients",
         out_shape=(
             jax.ShapeDtypeStruct((places * halves * sub, wide), BF16), gu, down, gu, down, down, gu, down,
-            jax.ShapeDtypeStruct(edge.shape, edge.dtype),
+            jax.ShapeDtypeStruct(dh.shape, dh.dtype),
         ),
-        in_specs=[any_spec] * 11,
+        in_specs=[any_spec] * 12,
         out_specs=(any_spec,) * 9,
         scratch_shapes=own + [
             pltpu.VMEM((2, sub, wide), BF16),
@@ -1031,7 +1041,7 @@
         ] + plane,
         compiler_params=pltpu.CompilerParams(
             collective_id=collective_id, has_side_effects=True, vmem_limit_bytes=VMEM_BYTES),
-    )(g0, t0, shares1, *experts0, gu1, down1, tail1, edge)
+    )(g0, t0, shares1, *experts0, gu1, down1, tail1, dh, final)
 
 
 def finish_kernel(qkv_cols, attn, gu_own, gu_got, gu_one, gu_moved, down_own, down_got, down_one, down_moved,
@@ -1188,9 +1198,10 @@
 LOADS = 2 * PAIRS * 3 + 1
 
 
-def attention_forward_kernel(layer, experts, rows, width, lens_ref, h_ref, small_ref, routes_ref, wq, wq_other,
+def attention_forward_kernel(layer, experts, rows, width, lens_ref, h_ref, s0, s1, s2, s3, routes_own, routes_other, wq,
+                             wq_other,
                              wo, wo_other, block_ref, h1_ref, a_ref, qkv_ref, p_ref, o_ref,
-                             router_v, wq_v, wo_v, a_parts, a_half, part_send, got_part, out_send, got_out,
+                             small_v, router_v, wq_v, wo_v, a_parts, a_half, part_send, got_part, out_send, got_out,
                              load_sem, send_sem, recv_sem, *turn):
     pair = Pair()
     me, peer = pair.me, pair.peer
@@ -1203,7 +1214,9 @@
 
     h = h_ref[...].astype(F32)
     r1 = lax.rsqrt(jnp.mean(h * h, axis=1, keepdims=True) + EPS)
-    gains = small_ref[pl.ds(experts, 2)].astype(F32)
+    for j, part in enumerate(layer_rows(layer, pair.sec, me, (s0, s1, s2, s3))):
+        small_v[:, pl.ds(j * half, half)] = part
+    gains = small_v[pl.ds(experts, 2)]
     a = (h * r1 * gains[0:1]).astype(BF16)
     for j in range(2):
         a_parts[j] = a[:, j * half : (j + 1) * half]
@@ -1264,10 +1277,10 @@
     block_ref[:, pl.ds(0, width)] = b
     router_v[...] = jnp.zeros_like(router_v)
     for copy in range(2):
-        router_v[pl.ds(copy * experts, experts)] = small_ref[pl.ds(0, experts)]
+        router_v[pl.ds(copy * experts, experts)] = small_v[pl.ds(0, experts)].astype(BF16)
     lane = lax.broadcasted_iota(jnp.int32, (rows, LANES), 1)
     column = jnp.where(lane < experts, lane, lane - experts)
-    routes = routes_ref[...]
+    routes = jnp.where(pair.sec == layer, routes_own[...], routes_other[...])
     mask = routes[:, 0:1] == column
     for n in range(1, TOP):
         mask = mask | (routes[:, n : n + 1] == column)
@@ -1299,9 +1312,10 @@
             jax.ShapeDtypeStruct((heads, group, group), BF16),
             jax.ShapeDtypeStruct((group, QUERY_WIDTH // 2), BF16),
         ),
-        in_specs=[pl.BlockSpec(memory_space=pltpu.SMEM)] + [vmem] * 3 + [any_spec] * 4,
+        in_specs=[pl.BlockSpec(memory_space=pltpu.SMEM)] + [vmem] * 7 + [any_spec] * 4,
         out_specs=(vmem,) * 6,
         scratch_shapes=[
+            pltpu.VMEM((experts + 2, width), F32),
             pltpu.VMEM((LANES, width), BF16),
             pltpu.VMEM((2, half, qkv), BF16),
             pltpu.VMEM((QUERY_WIDTH // 2, width), BF16),
@@ -1318,13 +1332,13 @@
         cost_estimate=COST,
         compiler_params=pltpu.CompilerParams(
             collective_id=collective_id, has_side_effects=True, vmem_limit_bytes=VMEM_BYTES),
-    )(lens, h, small, routes, *weights)
+    )(lens, h, *small, *routes, *weights)
 
 
 ATTENTION_BACKWARD_REFS = 20
 
 
-def attention_backward_kernel(layer, rows, width, experts, router_grad_ref, db_ref, dout_ref, h1_ref, h_ref, small_ref, a_ref, qkv_ref,
+def attention_backward_kernel(layer, rows, width, experts, router_grad_ref, db_ref, dout_ref, h1_ref, h_ref, s0, s1, s2, s3, a_ref, qkv_ref,
                               p_ref, o_ref, wq, wq_other, wo, wo_other, *refs):
     beside = len(refs) > ATTENTION_BACKWARD_REFS
     (later, refs) = (refs[:3], refs[3:]) if beside else ((), refs)
@@ -1365,7 +1379,8 @@
     r2 = lax.rsqrt(jnp.mean(h1 * h1, axis=1, keepdims=True) + EPS)
     normed = h1 * r2
     db = db_ref[...]
-    gains = small_ref[pl.ds(experts, 2)].astype(F32)
+    halves = layer_rows(layer, pair.sec, me, (s0, s1, s2, s3))
+    gains = jnp.concatenate([part[experts : experts + 2] for part in halves], axis=1)
     scaled = db * gains[1:2]
     gain_grads_ref[...] = jnp.zeros_like(gain_grads_ref)
     gain_grads_ref[pl.ds(experts + 1, 1), :] = jnp.sum(db * normed, axis=0, keepdims=True)
@@ -1497,7 +1512,7 @@
             jax.ShapeDtypeStruct((width, LANES), BF16),
             jax.ShapeDtypeStruct((half, QUERY_WIDTH + 2 * KV_WIDTH + width), BF16),
         ) + later_out,
-        in_specs=[vmem] * 10 + [any_spec] * (4 + len(later)),
+        in_specs=[vmem] * 13 + [any_spec] * (4 + len(later)),
         out_specs=(vmem, vmem, any_spec) + (vmem,) * len(later_out),
         scratch_shapes=[
             pltpu.VMEM((2, half, cols), BF16),
@@ -1521,7 +1536,7 @@
         cost_estimate=COST,
         compiler_params=pltpu.CompilerParams(
             collective_id=collective_id, has_side_effects=True, vmem_limit_bytes=VMEM_BYTES),
-    )(router_grad, db, dout, h1, h, small, a_half, qkv, p, o, *weights, *later)
+    )(router_grad, db, dout, h1, h, *small, a_half, qkv, p, o, *weights, *later)
 
 
 def dot(a, b, dims):
@@ -1809,16 +1824,9 @@
     small = jnp.concatenate([w_router[0].T, gain_attn, gain_moe], axis=0)
     across = lax.ppermute(small, ("section", "shard"), [(0, 3), (1, 2), (2, 1), (3, 0)])
 
-    def joined(mine, other):
-        return jnp.where(
-            shard_pos == 0,
-            jnp.concatenate([mine, other], axis=1),
-            jnp.concatenate([other, mine], axis=1),
-        )
-
-    layer_small = by_core(joined(small, swap_shards(small)), joined(swap_cores(small), across))
+    smalls = (small, swap_shards(small), swap_cores(small), across)
     x_in, dy = by_core(pick(edge_inputs[0], sec), swap_cores(pick(edge_inputs[0], 1 - sec)))
-    layer_routes = by_core(pick(routes[0], sec), swap_cores(pick(routes[0], 1 - sec)))
+    core_routes = (pick(routes[0], sec), swap_cores(pick(routes[0], 1 - sec)))
     lens = pick(seq_lengths, sec)[0]
     attn_weights = (w_qkv[0], swap_cores(w_qkv[0]), w_out[0], swap_cores(w_out[0]))
     expert_weights = (
@@ -1826,7 +1834,7 @@
     )
     def forward(layer, h):
         block, h1, *attn_state = attention_forward(
-            layer, experts, lens, h, layer_small[layer], layer_routes[layer], attn_weights, 1 + layer
+            layer, experts, lens, h, smalls, core_routes, attn_weights, 1 + layer
         )
         moe, out, *expert_state = moe_forward(
             layer, block, h1, expert_weights, experts, F32 if layer else BF16, 3 + layer
@@ -1836,12 +1844,12 @@
     def backward(layer, dout, state, later, later_attn):
         h, h1, moe, attn_state, expert_state = state
         results = moe_backward(
-            layer, dout, moe, layer_small[layer], expert_weights, expert_state, later, experts,
+            layer, dout, moe, smalls, expert_weights, expert_state, later, experts,
             5 + layer,
         )
         db, keep_gu, keep_down, send_gu, send_down, grad_router = results[:6]
         dh, columns, grad_attn, *piece = attention_backward(
-            layer, experts, grad_router, db, dout, h1, h, layer_small[layer], *attn_state, attn_weights,
+            layer, experts, grad_router, db, dout, h1, h, smalls, *attn_state, attn_weights,
             later_attn + tuple(results[7:8]) if later else (), 7 + layer,
         )
         places = LINE * SIDE
@@ -1856,9 +1864,8 @@
     dh_zero, attn0, columns0, experts0, sums1, (shares1, tail1) = backward(
         0, dh_one, state0, experts1, (attn1, columns1)
     )
-    send = jnp.where(sec == 0, final, dh_zero)
     attn, gu_own, down_own, gu_got, down_got, down_one, gu_moved, down_moved, got = reduce_gradients(
-        attn0, columns0, shares1, experts0, *sums1, tail1, send, 9
+        attn0, columns0, shares1, experts0, *sums1, tail1, dh_zero, final, 9
     )
     grad_qkv, grad_out, grad_gu, grad_down = finish_outputs(
         attn,

time: 650 us -> 643 us (0.989)
  transfers between devices with their start and end apart: 9 -> 9, of which waited for: 2 -> 1; matrix products, arithmetic and copies ran while one was open for 1% -> 1% of each run, Pallas kernels for 8% -> 8%
where the time goes in v3:
time: 643 us; the launch traced here: 637 us
  Pallas kernels  614 us (95%)
  local copies, waits for them, and re-layouts  7.77 us (1%)
  starting transfers between devices  7.48 us (1%)
    pallas_call x2, Pallas kernels, moe_backward(): pl.pallas_call(functools.partial(moe_backward_kernel, layer, experts, row...  163 us
    pallas_call x2, Pallas kernels, moe_forward(): pl.pallas_call(functools.partial(moe_forward_kernel, layer, experts, rows...  142 us
    pallas_call x1, Pallas kernels, reduce_gradients(): pl.pallas_call(functools.partial(reduce_kernel, sub, cols), name='reduce_...  118 us
    pallas_call x2, Pallas kernels, attention_backward(): pl.pallas_call(functools.partial(attention_backward_kernel, layer, rows,...  94.4 us
    pallas_call x2, Pallas kernels, attention_forward(): pl.pallas_call(functools.partial(attention_forward_kernel, layer, experts...  80.9 us
    pallas_call x1, Pallas kernels, finish_outputs(): pl.pallas_call(functools.partial(finish_kernel, qkv_cols), name='finish_o...  15.4 us
  transfers between devices with their start and end apart: 9, of which 1 were waited for; matrix products, arithmetic and copies ran while one was open for 1% of the time, Pallas kernels for 8%

profile of v3, /device:TPU:0, one launch (start us, length us, event | category | flops | bytes accessed | tf_op | source)
XLA Modules:
  0.0 636.8 jit_solution(16601390827093232390)
XLA Ops:
  0.6 0.5 collective-permute-start.5
  1.2 1.0 dynamic-slice_bitcast_fusion
  2.3 0.5 collective-permute-start
  2.8 0.8 pad_maximum_fusion.s0
  3.6 2.7 collective-permute-start.3
  6.3 0.7 constant_dynamic-slice_fusion
  7.2 0.5 fusion.lens_ref
  7.7 0.7 copy.21
  8.5 0.4 collective-permute-done.4.routes_other
  8.9 0.4 collective-permute-start.2
  9.3 2.7 collective-permute-start.1
  11.9 2.0 bitcast_select_fusion
  14.0 0.4 collective-permute-start.7
  14.6 0.4 copy-done.9
  15.0 51.1 %attention_forward.2 = (bf16[128,1664]{1,0:T(8,128)(2,1)}, f32[128,1536]{1,0:T(8,128)}, bf16[256,768]{1,0:T(8,128)(2,1)}, bf16[256,1280]{1,0:T(8,128)(2,1)}, bf1...) custom-call(s32[3]{0:T(128)} %fusion.lens_ref, bf16[128,1536]{1,0:T(8,128)(2,1)} %get-tuple-element.140.h_ref, ...), custom_call_target="tpu_custom_call" | custom-call | flops 99999997952 | bytes 16777216 | tf_op jit(solution)/shard_map/attention_forward/pallas_call | solution.py:1304
  66.2 1.6 copy-done.5
  67.8 71.8 %moe_forward.2 = (f32[128,1536]{1,0:T(8,128)}, bf16[128,1536]{1,0:T(8,128)(2,1)}, bf16[1024,1664]{1,0:T(8,128)(2,1)}, bf16[1024,2048]{1,0:T(8,128)(2,1)}, bf16[1024,1024]{1,0:T(8,128)(2,1)}) custom-call(bf16[128,1664]{1,0:T(8,128)(2,1)} %get-tuple-element.65.block_ref, f32[128,1536]{1,0:T(8,128)} %get-tuple-element.66.h1_ref, ...), custom_call_target="tpu_custom_call" | custom-call | flops 99999997952 | bytes 16777216 | tf_op jit(solution)/shard_map/moe_forward/pallas_call | solution.py:411
  139.6 29.8 %attention_forward.3 = (bf16[128,1664]{1,0:T(8,128)(2,1)}, f32[128,1536]{1,0:T(8,128)}, bf16[256,768]{1,0:T(8,128)(2,1)}, bf16[256,1280]{1,0:T(8,128)(2,1)}, bf1...) custom-call(s32[3]{0:T(128)} %fusion.lens_ref, bf16[128,1536]{1,0:T(8,128)(2,1)} %get-tuple-element.67.h_ref, ...), custom_call_target="tpu_custom_call" | custom-call | flops 99999997952 | bytes 16777216 | tf_op jit(solution)/shard_map/attention_forward/pallas_call | solution.py:1304
  169.4 69.7 %moe_forward.3 = (f32[128,1536]{1,0:T(8,128)}, f32[128,1536]{1,0:T(8,128)}, bf16[1024,1664]{1,0:T(8,128)(2,1)}, bf16[1024,2048]{1,0:T(8,128)(2,1)}, bf16[1024,1024]{1,0:T(8,128)(2,1)}) custom-call(bf16[128,1664]{1,0:T(8,128)(2,1)} %get-tuple-element.68.block_ref, f32[128,1536]{1,0:T(8,128)} %get-tuple-element.69.h1_ref, bf16[2,1536,1024]{2,1,0:T(8,128)(2,1)} %bitcast.40, ...), custom_call_target="tpu_custom_call" | custom-call | flops 99999997952 | bytes 16777216 | tf_op jit(solution)/shard_map/moe_forward/pallas_call | solution.py:411
  239.1 65.6 %moe_backward.2 = (f32[128,1536]{1,0:T(8,128)}, bf16[1536,1024]{1,0:T(8,128)(2,1)}, bf16[512,1536]{1,0:T(8,128)(2,1)}, bf16[1536,1024]{1,0:T(8,128)(2,1)}, bf16[...) custom-call(bf16[128,1536]{1,0:T(8,128)(2,1)} %get-tuple-element.141.dout_ref, f32[128,1536]{1,0:T(8,128)} %get-tuple-element.70.moe_ref, ...), custom_call_target="tpu_custom_call" | custom-call | flops 99999997952 | bytes 16777216 | tf_op jit(solution)/shard_map/moe_backward/pallas_call | solution.py:668
  304.7 31.4 %attention_backward.2 = (bf16[128,1536]{1,0:T(8,128)(2,1)}, bf16[1536,128]{1,0:T(8,128)(2,1)}, bf16[768,4096]{1,0:T(8,128)(2,1)}) custom-call(f32[1536,128]{1,0:T(8,128)} %get-tuple-element.74.router_grad_ref, f32[128,1536]{1,0:T(8,128)} %get-tuple-element.75.db_ref, bf16[128,1536]{1,0:T(8,128)(2,1)} %get-tuple-element.141.dout_ref, ...), custom_call_target="tpu_custom_call" | custom-call | flops 99999997952 | bytes 16777216 | tf_op jit(solution)/shard_map/attention_backward/pallas_call | solution.py:1507
  336.1 97.7 %moe_backward.3 = (f32[128,1536]{1,0:T(8,128)}, bf16[1536,1024]{1,0:T(8,128)(2,1)}, bf16[512,1536]{1,0:T(8,128)(2,1)}, bf16[1536,1024]{1,0:T(8,128)(2,1)}, bf16[...) custom-call(bf16[128,1536]{1,0:T(8,128)(2,1)} %get-tuple-element.80., ...), custom_call_target="tpu_custom_call" | custom-call | flops 99999997952 | bytes 16777216 | tf_op jit(solution)/shard_map/moe_backward/pallas_call | solution.py:668
  433.8 63.0 %attention_backward.3 = (f32[128,1536]{1,0:T(8,128)}, bf16[1536,128]{1,0:T(8,128)(2,1)}, bf16[768,4096]{1,0:T(8,128)(2,1)}, bf16[3,48,4224]{2,1,0:T(8,128)(2,1)}, bf16[256,1536]{1,0:T(8,128)(2,1)}) custom-call(f32[1536,128]{1,0:T(8,128)} %get-tuple-element.89.router_grad_ref, f32[128,1536]{1,0:T(8,128)} %get-tuple-element.90.db_ref, ...), custom_call_target="tpu_custom_call" | custom-call | flops 99999997952 | bytes 16777216 | tf_op jit(solution)/shard_map/attention_backward/pallas_call | solution.py:1507
  496.8 1.3 select_bitcast_fusion
  498.1 118.3 %reduce_gradients.1 = (bf16[768,4224]{1,0:T(8,128)(2,1)}, bf16[1536,1024]{1,0:T(8,128)(2,1)}, bf16[512,1536]{1,0:T(8,128)(2,1)}, bf16[1536,1024]{1,0:T(8,128)(2,...) custom-call(bf16[8,2,48,4096]{3,2,1,0:T(8,128)(2,1)} %bitcast.29, ...), custom_call_target="tpu_custom_call" | custom-call | tf_op jit(solution)/shard_map/reduce_gradients/pallas_call | solution.py:1021
  616.4 1.0 slice_convert_fusion
  617.4 0.5 slice_reduce_fusion
  617.9 0.8 copy.23
  618.7 0.6 broadcast_in_dim_squeeze.7
  619.3 0.6 broadcast_in_dim_squeeze.6
  619.9 1.3 maximum_select_fusion
  621.1 15.4 %finish_outputs.1 = (f32[768,2560]{1,0:T(8,128)}, f32[768,1536]{1,0:T(8,128)}, f32[2,1536,1024]{2,1,0:T(8,128)}, f32[2,512,1536]{2,1,0:T(8,128)}) custom-call(bf16[768,4224]{1,0:T(8,128)(2,1)} %get-tuple-element.110.attn, bf16[1536,1024]{1,0:T(8,128)(2,1)} %get-tuple-element.111.gu_own, bf16[1536,1024]{1,0:T(8,128)(2,1)} %get-tuple-element.112.gu_got, ...), custom_call_target="tpu_custom_call" | custom-call | tf_op jit(solution)/shard_map/finish_outputs/pallas_call | solution.py:1109
  (31 shorter events, 0.6 us)
Async XLA Ops:
  0.6 6.6 %copy-start = (s32[2,1,3]{2,1,0:T(1,128)S(1)}, s32[2,1,3]{2,1,0:T(1,128)}, u32[]{:S(2)}) copy-start(s32[2,1,3]{2,1,0:T(1,128)} %param.11) | copy-start | bytes 76
  0.6 13.8 %collective-permute-start.5 = (bf16[768,2560]{1,0:T(8,128)(2,1)}, bf16[768,2560]{1,0:T(8,128)(2,1)}, u32[]{:S(2)}, u32[]{:S(2)}) collective-permute-start(bf16[768,2560]{1,0:T(8,128)(2,1)} %bitcast.45), channel_id=1, source_target_pairs={{0,16},{16,0},{1,17},{17,1},{2,18},{18,2},{3,19},{19,3},{4,20},{20... | collective-permute-start | bytes 11796488 | tf_op jit(solution)/shard_map/ppermute | solution.py:1551
  1.2 13.3 %collective-permute-start.6 = (bf16[768,1536]{1,0:T(8,128)(2,1)}, bf16[768,1536]{1,0:T(8,128)(2,1)}, u32[]{:S(2)}, u32[]{:S(2)}) collective-permute-start(bf16[768,1536]{1,0:T(8,128)(2,1)} %bitcast.55), channel_id=1, source_target_pairs={{0,16},{16,0},{1,17},{17,1},{2,18},{18,2},{3,19},{19,3},{4,20},{20... | collective-permute-start | bytes 7077896 | tf_op jit(solution)/shard_map/ppermute | solution.py:1551
  2.3 7.0 %collective-permute-start = (bf16[128,1536]{1,0:T(8,128)(2,1)S(1)}, bf16[128,1536]{1,0:T(8,128)(2,1)S(1)}, u32[]{:S(2)}, u32[]{:S(2)}) collective-permute-start(bf16[128,1536]{1,0:T(8,128)(2,1)S(1)} %dynamic-slice_bitcast_fusion), channel_id=1, source_target_pairs={{0,16},{16,0},{1,17},{17,1},{2,18},{18,2},{3,19},{19,3},{4,20},{20... | collective-permute-start | bytes 1179656 | tf_op jit(solution)/shard_map/ppermute | solution.py:1551
  3.6 10.9 %copy-start.4 = (bf16[18,768]{1,0:T(8,128)(2,1)}, bf16[18,768]{1,0:T(8,128)(2,1)S(1)}, u32[]{:S(2)}) copy-start(bf16[18,768]{1,0:T(8,128)(2,1)S(1)} %pad_maximum_fusion.s0) | copy-start | bytes 82948
  3.6 10.3 %collective-permute-start.3 = (bf16[18,768]{1,0:T(8,128)(2,1)S(1)}, bf16[18,768]{1,0:T(8,128)(2,1)S(1)}, u32[]{:S(2)}, u32[]{:S(2)}) collective-permute-start(bf16[18,768]{1,0:T(8,128)(2,1)S(1)} %pad_maximum_fusion.s0), channel_id=1, source_target_pairs={{0,17},{1,16},{16,1},{17,0},{2,19},{3,18},{18,3},{19,2},{4,21},{5,... | collective-permute-start | bytes 82952 | tf_op jit(solution)/shard_map/ppermute | solution.py:1825
  7.1 1.8 collective-permute-start.4
  8.9 5.6 copy-start.6
  8.9 5.1 collective-permute-start.2
  9.3 5.2 collective-permute-start.1
  13.9 0.6 copy-start.7
  13.9 52.2 %collective-permute-start.8 = (bf16[2,512,1536]{2,1,0:T(8,128)(2,1)}, bf16[2,512,1536]{2,1,0:T(8,128)(2,1)S(1)}, u32[]{:S(2)}, u32[]{:S(2)}) collective-permute-start(bf16[2,512,1536]{2,1,0:T(8,128)(2,1)} %bitcast.50), channel_id=1, source_target_pairs={{0,16},{16,0},{1,17},{17,1},{2,18},{18,2},{3,19},{19,3},{4,20},{20... | collective-permute-start | bytes 9437192 | tf_op jit(solution)/shard_map/ppermute | solution.py:1551
  14.0 0.6 copy-start.8
  14.0 52.2 %collective-permute-start.7 = (bf16[2,1536,1024]{2,1,0:T(8,128)(2,1)}, bf16[2,1536,1024]{2,1,0:T(8,128)(2,1)}, u32[]{:S(2)}, u32[]{:S(2)}) collective-permute-start(bf16[2,1536,1024]{2,1,0:T(8,128)(2,1)} %bitcast.38), channel_id=1, source_target_pairs={{0,16},{16,0},{1,17},{17,1},{2,18},{18,2},{3,19},{19,3},{4,20},{20... | collective-permute-start | bytes 18874376 | tf_op jit(solution)/shard_map/ppermute | solution.py:1551
  14.4 0.6 copy-start.9
  66.2 1.7 copy-start.5
  433.8 63.0 %copy-start.2 = (f32[128,1536]{1,0:T(8,128)S(1)}, f32[128,1536]{1,0:T(8,128)}, u32[]{:S(2)}) copy-start(f32[128,1536]{1,0:T(8,128)} %get-tuple-element.99.final) | copy-start | bytes 2359300
  616.4 3.5 copy-start.3
  621.1 15.4 %copy-start.1 = (s32[2,1,3]{2,1,0:T(1,128)S(1)}, s32[2,1,3]{2,1,0:T(1,128)}, u32[]{:S(2)}) copy-start(s32[2,1,3]{2,1,0:T(1,128)} %param.11) | copy-start | bytes 76
